TPU v7x, 32 devices: a whole 2x2x4 slice. The times are simulated.
32 devices in a mesh: irrep: 4 (over z), row: 8 (over y, x, core).
Axes of the slice: x: 2, y: 2, z: 4, core: 2. Of those that a mesh axis runs over, the one named last changes fastest.
Arguments:
- densities: float32 [4, 2048, 512], P('irrep', 'row'), may hold values from -6 to 6
- reduced_kernel: float32 [4, 12288, 2048], P('irrep', 'row'), may hold values from -0.125 to 0.125
Outputs:
- potentials: float32 [4, 12288, 512], P('irrep', 'row')
All inputs are finite; a program needn't handle non-finite values.
Results may differ from a plain program's by a relative error of at most 0.000086.
Values sent between devices are 32-bit elements; how exact they have to be, the bound alone decides.
No kernel may reach another device: no remote copies, remote signals or barrier semaphores. Data moves between devices by JAX's collectives and lax.ppermute only.
A program may use at most 128 MiB of HBM per device.

v0:
```python
import functools
import math

import jax
import jax.numpy as jnp
from jax import lax
from jax.experimental import pallas as pl
from jax.experimental.pallas import tpu as pltpu
from jax.sharding import PartitionSpec as P

HALF = jnp.bfloat16
AXES = ("irrep", "row")
TILES = 3
WEIGHT = 6


def exchange(value, masks):
    devices = lax.axis_size("irrep") * lax.axis_size("row")
    pairs = [(at, at ^ masks[at & 1]) for at in range(devices)]
    return lax.ppermute(value, AXES, pairs)


def turns(step, count):
    return [(step + core) % count for core in range(2)]


def across(held, step, bits):
    return exchange(held, [2 << bit for bit in turns(step, bits)])


def swapped(held, parts):
    size = held.shape[0] // parts
    return [exchange(held[at : at + size], [1, 1]) for at in range(0, held.shape[0], size)]


def gather_chips(held, steps, bits, others=None):
    for step in steps:
        held = jnp.concatenate([held, after(across(held, step, bits), others)])
    return held


def numbers(levels, bits):
    me = lax.axis_index("row").astype(jnp.int32)
    octant = lax.axis_index("irrep").astype(jnp.int32)
    core = me & 1
    half = 1 << (bits - 1)
    table = []
    for group in range(2):
        for other in range(2):
            for at in range(group * half, (group + 1) * half):
                rel = [other, other]
                for step in range(bits):
                    if at >> step & 1:
                        for side, bit in enumerate(turns(step, bits)):
                            rel[side] ^= 2 << bit
                table.append(me ^ jnp.where(core ^ other == 1, rel[1], rel[0]))
    signs = []
    for step in range(levels):
        bit = turns(step, levels)
        upper = octant >> jnp.where(core == 1, bit[1], bit[0]) & 1
        signs.append((1 - 2 * upper).astype(jnp.float32))
    return lax.optimization_barrier((jnp.stack(table).astype(jnp.int32), signs))


VMEM = pl.BlockSpec(memory_space=pltpu.VMEM)
SMEM = pl.BlockSpec(memory_space=pltpu.SMEM)
ANY = pl.BlockSpec(memory_space=pl.ANY)


def fold(holding, partner, sign, step, levels):
    total = partner + sign * holding
    if step == levels - 1:
        total = total * (1.0 / math.sqrt(lax.axis_size("irrep")))
    return lax.optimization_barrier(total)


def partner_of(holding, step, levels):
    owners = lax.axis_size("row")
    return exchange(holding, [owners << bit for bit in turns(step, levels)])


def in_two(value):
    high = value.astype(HALF)
    return high, (value - high.astype(jnp.float32)).astype(HALF)


def split_kernel(owners, chunks, table_ref, k_ref, high_ref, low_ref, buffers, sems):
    count, tile, sources = buffers.shape
    depth = sources // owners // chunks
    steps = k_ref.shape[0] // tile

    def fetch(step):
        here = pl.ds(pl.multiple_of(step * tile, tile), tile)
        slot = lax.rem(step, count)
        return pltpu.make_async_copy(k_ref.at[here, :], buffers.at[slot], sems.at[slot])

    for step in range(count - 1):
        fetch(step).start()

    @pl.loop(0, steps)
    def _(step):
        fetch(step).wait()

        @pl.when(step + count - 1 < steps)
        def _():
            fetch(step + count - 1).start()

        slot = lax.rem(step, count)
        here = pl.ds(pl.multiple_of(step * tile, tile), tile)
        for chunk in range(chunks):
            for piece in range(owners):
                start = (table_ref[piece] * chunks + chunk) * depth
                columns = pl.ds(pl.multiple_of(start, depth), depth)
                high, low = in_two(buffers[slot, :, columns])
                at = (chunk * owners + piece) * depth
                high_ref[here, at : at + depth] = high
                low_ref[here, at : at + depth] = low


def split(table, k, chunks):
    rows, sources = k.shape
    count, tile = 3, rows // 6
    return pl.pallas_call(
        functools.partial(split_kernel, lax.axis_size("row"), chunks),
        in_specs=[SMEM, ANY],
        out_specs=[VMEM, VMEM],
        out_shape=[pltpu.VMEM((rows, sources), HALF)] * 2,
        scratch_shapes=[
            pltpu.VMEM((count, tile, sources), jnp.float32),
            pltpu.SemaphoreType.DMA((count,)),
        ],
        cost_estimate=pl.CostEstimate(
            flops=4 * rows * sources, bytes_accessed=4 * rows * sources, transcendentals=0
        ),
        compiler_params=pltpu.CompilerParams(vmem_limit_bytes=18 * 2**20),
        name="split_reduced_kernel",
    )(table, pltpu.with_memory_space_constraint(k, pltpu.HBM))


def multiply_kernel(start, arrays, accumulate, last, high_ref, low_ref, *refs):
    refs = list(refs)
    f_refs = [refs.pop(0) for _ in range(arrays)]
    before = refs.pop(0) if accumulate else None
    out_ref, f_high, f_low = refs[:3]
    depth = f_refs[0].shape[1]
    at = 0
    for ref in f_refs:
        for piece in range(ref.shape[0]):
            high, low = in_two(ref[piece])
            f_high[at : at + depth, :] = high
            f_low[at : at + depth, :] = low
            at += depth
    sources = slice(start * depth, start * depth + at)
    tile = high_ref.shape[0] // TILES

    def product(step):
        here = pl.ds(pl.multiple_of(step * tile, tile), tile)
        high, low = high_ref[here, sources], low_ref[here, sources]
        left = jnp.concatenate([low, high, high], axis=1)
        right = jnp.concatenate([f_high[...], f_low[...], f_high[...]], axis=0)
        total = jnp.dot(left, right, preferred_element_type=jnp.float32)
        return here, total + before[here, :] if accumulate else total

    if not last:

        @pl.loop(0, TILES)
        def _(step):
            here, total = product(step)
            out_ref[here, :] = total

    else:
        result, sems = refs[3:]

        def copy(here, step):
            return pltpu.make_async_copy(
                result.at[here, :], out_ref.at[0, here, :], sems.at[step]
            )

        @pl.loop(0, TILES)
        def _(step):
            here, total = product(step)
            result[here, :] = total
            copy(here, step).start()

        for step in range(TILES):
            copy(slice(step * tile, (step + 1) * tile), step).wait()


def multiply(k_high, k_low, pieces, start, before, last=False):
    rows = k_high.shape[0]
    count, (depth, width) = sum(a.shape[0] for a in pieces), pieces[0].shape[1:]
    accumulate = before is not None
    operands = [k_high, k_low, *pieces] + ([before] if accumulate else [])
    operands = [pltpu.with_memory_space_constraint(a, pltpu.VMEM) for a in operands]
    scratch = [pltpu.VMEM((count * depth, width), HALF)] * 2
    alias = {}
    if last:
        scratch += [pltpu.VMEM((rows, width), jnp.float32), pltpu.SemaphoreType.DMA((TILES,))]
        shape = jax.ShapeDtypeStruct((1, rows, width), jnp.float32)
    else:
        shape = pltpu.VMEM((rows, width), jnp.float32)
        alias = {len(operands) - 1: 0} if accumulate else {}
    return pl.pallas_call(
        functools.partial(multiply_kernel, start, len(pieces), accumulate, last),
        in_specs=[VMEM] * len(operands),
        out_specs=ANY if last else VMEM,
        out_shape=shape,
        input_output_aliases=alias,
        scratch_shapes=scratch,
        cost_estimate=pl.CostEstimate(
            flops=int(WEIGHT * rows * count * depth * width), bytes_accessed=0, transcendentals=0
        ),
        compiler_params=pltpu.CompilerParams(vmem_limit_bytes=14 * 2**20),
        name="multiply_sources",
    )(*operands)


def after(value, others):
    return value if others is None else lax.optimization_barrier((value, others))[0]


def body(densities, reduced_kernel):
    levels = lax.axis_size("irrep").bit_length() - 1
    bits = lax.axis_size("row").bit_length() - 2
    mine = densities[0]
    half = mine.shape[0] // 2
    table, signs = numbers(levels, bits)
    ks = split(table, reduced_kernel[0], 2)
    parts = [lax.optimization_barrier(mine[at * half : (at + 1) * half]) for at in range(2)]
    for step in range(levels):
        partners = [partner_of(part, step, levels) for part in parts]
        partners[0] = after(partners[0], tuple(ks) if step == 0 else parts[1])
        parts = [fold(*pair, signs[step], step, levels) for pair in zip(parts, partners)]
    last = bits - 1
    group = lax.axis_size("row") // 2
    early = gather_chips(parts[0][None], range(last), bits)
    early = after(early, parts[1])
    arrived = across(early, last, bits)
    out = multiply(*ks, [early, exchange(early, [1, 1])], 0, None)
    late = gather_chips(parts[1][None], range(last), bits, out)
    out = multiply(*ks, [late, exchange(late, [1, 1])], 2 * group, out)
    out = multiply(*ks, [arrived, *swapped(arrived, 2)], group, out)
    arrived = after(across(late, last, bits), out)
    out = multiply(*ks, [arrived], 3 * group, out)
    return multiply(*ks, [exchange(arrived, [1, 1])], 3 * group + group // 2, out, True)


def solution(mesh):
    placed = (P("irrep", "row", None), P("irrep", "row", None))
    return jax.shard_map(
        body, mesh=mesh, in_specs=placed, out_specs=P("irrep", "row", None), check_vma=False
    )
```

profile of v0, /device:TPU:0, one launch (start us, length us, event | category | flops | bytes accessed | tf_op | source)
XLA Modules:
  0.0 55.0 jit_solution(971574905891841170)
XLA Ops:
  0.0 1.1 %slice_bitcast_fusion = (f32[128,512]{1,0:T(8,128)S(1)}, f32[128,512]{1,0:T(8,128)S(1)}) fusion(f32[1,256,512]{2,1,0:T(8,128)} %param.2), kind=kLoop, calls=%fused_computation.4 | loop fusion | bytes 1048576 | tf_op jit(solution)/shard_map/slice | solution.py:229
  1.1 3.1 %collective-permute-start.3 = (f32[128,512]{1,0:T(8,128)S(1)}, f32[128,512]{1,0:T(8,128)S(1)}, u32[]{:S(2)}, u32[]{:S(2)}) collective-permute-start(f32[128,512]{1,0:T(8,128)S(1)} %get-tuple-element.27), channel_id=1, source_target_pairs={{0,8},{1,17},{2,10},{3,19},{4,12},{5,21},{6,14},{7,23},{8,0},{9,25... | collective-permute-start | bytes 786440 | tf_op jit(solution)/shard_map/ppermute | solution.py:20
  4.2 0.1 collective-permute-start
  4.2 0.1 stack.35.table_ref
  4.3 6.8 %split_reduced_kernel.1 = (bf16[1536,2048]{1,0:T(8,128)(2,1)S(1)}, bf16[1536,2048]{1,0:T(8,128)(2,1)S(1)}) custom-call(s32[8]{0:T(128)S(1)} %stack.35.table_ref, f32[1536,2048]{1,0:T(8,128)} %bitcast.15), custom_call_target="tpu_custom_call" | custom-call | flops 12582912 | bytes 12582912 | tf_op jit(solution)/shard_map/split_reduced_kernel/pallas_call | solution.py:123
  11.2 0.0 collective-permute-done.3
  11.2 3.3 %collective-permute-start.4 = (f32[128,512]{1,0:T(8,128)S(1)}, f32[128,512]{1,0:T(8,128)S(1)}, u32[]{:S(2)}, u32[]{:S(2)}) collective-permute-start(f32[128,512]{1,0:T(8,128)S(1)} %multiply_add_fusion), channel_id=1, source_target_pairs={{0,16},{1,9},{2,18},{3,11},{4,20},{5,13},{6,22},{7,15},{8,24},{9,1... | collective-permute-start | bytes 786440 | tf_op jit(solution)/shard_map/ppermute | solution.py:20
  14.5 6.3 %collective-permute-done = f32[128,512]{1,0:T(8,128)S(1)} collective-permute-done((f32[128,512]{1,0:T(8,128)S(1)}, f32[128,512]{1,0:T(8,128)S(1)}, u32[]{:S(2)}, u32[]{:S(2)}) %collective-permute-start) | collective-permute-done | bytes 262176 | tf_op jit(solution)/shard_map/ppermute | solution.py:20
  20.8 1.0 %collective-permute-start.1 = (f32[128,512]{1,0:T(8,128)S(1)}, f32[128,512]{1,0:T(8,128)S(1)}, u32[]{:S(2)}, u32[]{:S(2)}) collective-permute-start(f32[128,512]{1,0:T(8,128)S(1)} %multiply_add_fusion.1), channel_id=1, source_target_pairs={{0,16},{1,9},{2,18},{3,11},{4,20},{5,13},{6,22},{7,15},{8,24},{9,1... | collective-permute-start | bytes 786440 | tf_op jit(solution)/shard_map/ppermute | solution.py:20
  21.8 0.3 collective-permute-done.4
  22.1 1.6 %collective-permute-start.5 = (f32[1,128,512]{2,1,0:T(8,128)S(1)}, f32[1,128,512]{2,1,0:T(8,128)S(1)}, u32[]{:S(2)}, u32[]{:S(2)}) collective-permute-start(f32[1,128,512]{2,1,0:T(8,128)S(1)} %bitcast.18), channel_id=1, source_target_pairs={{0,2},{1,5},{2,0},{3,7},{4,6},{5,1},{6,4},{7,3},{8,10},{9,13},{10,... | collective-permute-start | bytes 786440 | tf_op jit(solution)/shard_map/ppermute | solution.py:20
  23.7 7.2 %collective-permute-done.1 = f32[128,512]{1,0:T(8,128)S(1)} collective-permute-done((f32[128,512]{1,0:T(8,128)S(1)}, f32[128,512]{1,0:T(8,128)S(1)}, u32[]{:S(2)}, u32[]{:S(2)}) %collective-permute-start.1) | collective-permute-done | bytes 262176 | tf_op jit(solution)/shard_map/ppermute | solution.py:20
  31.0 0.0 collective-permute-done.5
  31.0 0.1 collective-permute-start.6
  31.1 2.0 %collective-permute-start.2 = (f32[1,128,512]{2,1,0:T(8,128)S(1)}, f32[1,128,512]{2,1,0:T(8,128)S(1)}, u32[]{:S(2)}, u32[]{:S(2)}) collective-permute-start(f32[1,128,512]{2,1,0:T(8,128)S(1)} %bitcast.16), channel_id=1, source_target_pairs={{0,2},{1,5},{2,0},{3,7},{4,6},{5,1},{6,4},{7,3},{8,10},{9,13},{10,... | collective-permute-start | bytes 786440 | tf_op jit(solution)/shard_map/ppermute | solution.py:20
  33.1 1.5 %collective-permute-start.8 = (f32[2,128,512]{2,1,0:T(8,128)S(1)}, f32[2,128,512]{2,1,0:T(8,128)S(1)}, u32[]{:S(2)}, u32[]{:S(2)}) collective-permute-start(f32[2,128,512]{2,1,0:T(8,128)S(1)} %pad_maximum_fusion.refs_0_), channel_id=1, source_target_pairs={{0,4},{1,3},{2,6},{3,1},{4,0},{5,7},{6,2},{7,5},{8,12},{9,11},{10,... | collective-permute-start | bytes 1572872 | tf_op jit(solution)/shard_map/ppermute | solution.py:20
  34.6 0.0 collective-permute-done.6.refs_1_
  34.6 3.1 %multiply_sources.5.refs_2_ = f32[1536,512]{1,0:T(8,128)S(1)} custom-call(bf16[1536,2048]{1,0:T(8,128)(2,1)S(1)} %get-tuple-element.16.high_ref, bf16[1536,2048]{1,0:T(8,128)(2,1)S(1)} %get-tuple-element.17.low_ref, f32[2,128,512]{2,1,0:T(8,128)S(1)} %pad_maximum_fusion.refs_0_, f32[2,128,512]{2,1,0:T(8,128)S(1)} %collective-permute-done.6.refs_1_), custom_call_target="tpu_custom_call" | custom-call | flops 2415919104 | tf_op jit(solution)/shard_map/multiply_sources/pallas_call | solution.py:203
  37.7 1.5 %collective-permute-done.2 = f32[1,128,512]{2,1,0:T(8,128)S(1)} collective-permute-done((f32[1,128,512]{2,1,0:T(8,128)S(1)}, f32[1,128,512]{2,1,0:T(8,128)S(1)}, u32[]{:S(2)}, u32[]{:S(2)}) %collective-permute-start.2) | collective-permute-done | bytes 262176 | tf_op jit(solution)/shard_map/ppermute | solution.py:20
  39.3 0.1 collective-permute-start.11
  39.3 3.1 %collective-permute-start.7 = (f32[2,128,512]{2,1,0:T(8,128)S(1)}, f32[2,128,512]{2,1,0:T(8,128)S(1)}, u32[]{:S(2)}, u32[]{:S(2)}) collective-permute-start(f32[2,128,512]{2,1,0:T(8,128)S(1)} %pad_maximum_fusion.1.refs_0_), channel_id=1, source_target_pairs={{0,4},{1,3},{2,6},{3,1},{4,0},{5,7},{6,2},{7,5},{8,12},{9,11},{10,... | collective-permute-start | bytes 1572872 | tf_op jit(solution)/shard_map/ppermute | solution.py:20
  42.4 0.4 collective-permute-done.8.refs_0_
  42.8 0.2 collective-permute-start.10
  43.1 0.3 collective-permute-start.9
  43.4 0.0 collective-permute-done.11.refs_1_
  43.4 3.3 %multiply_sources.6.refs_3_ = f32[1536,512]{1,0:T(8,128)S(1)} custom-call(bf16[1536,2048]{1,0:T(8,128)(2,1)S(1)} %get-tuple-element.16.high_ref, bf16[1536,2048]{1,0:T(8,128)(2,1)S(1)} %get-tuple-element.17.low_ref, f32[2,128,512]{2,1,0:T(8,128)S(1)} %pad_maximum_fusion.1.refs_0_, ...), custom_call_target="tpu_custom_call", output_to_operand_aliasing={{}: (4, {})} | custom-call | flops 2415919104 | tf_op jit(solution)/shard_map/multiply_sources/pallas_call | solution.py:203
  46.7 0.0 collective-permute-done.10.refs_2_
  46.7 0.0 collective-permute-done.9.refs_1_
  46.7 3.3 %multiply_sources.7.refs_1_ = f32[1536,512]{1,0:T(8,128)S(1)} custom-call(bf16[1536,2048]{1,0:T(8,128)(2,1)S(1)} %get-tuple-element.16.high_ref, bf16[1536,2048]{1,0:T(8,128)(2,1)S(1)} %get-tuple-element.17.low_ref, f32[2,128,512]{2,1,0:T(8,128)S(1)} %collective-permute-done.8.refs_0_, ...), custom_call_target="tpu_custom_call", output_to_operand_aliasing={{}: (5, {})} | custom-call | flops 2415919104 | tf_op jit(solution)/shard_map/multiply_sources/pallas_call | solution.py:203
  50.0 0.0 collective-permute-done.7.refs_0_
  50.0 0.2 collective-permute-start.12
  50.3 1.9 %multiply_sources.8.refs_1_ = f32[1536,512]{1,0:T(8,128)S(1)} custom-call(bf16[1536,2048]{1,0:T(8,128)(2,1)S(1)} %get-tuple-element.16.high_ref, bf16[1536,2048]{1,0:T(8,128)(2,1)S(1)} %get-tuple-element.17.low_ref, f32[2,128,512]{2,1,0:T(8,128)S(1)} %collective-permute-done.7.refs_0_, ...), custom_call_target="tpu_custom_call", output_to_operand_aliasing={{}: (3, {})} | custom-call | flops 1207959552 | tf_op jit(solution)/shard_map/multiply_sources/pallas_call | solution.py:203
  52.1 0.0 collective-permute-done.12.refs_0_
  52.1 2.8 %multiply_sources.9 = f32[1,1536,512]{2,1,0:T(8,128)} custom-call(bf16[1536,2048]{1,0:T(8,128)(2,1)S(1)} %get-tuple-element.16.high_ref, bf16[1536,2048]{1,0:T(8,128)(2,1)S(1)} %get-tuple-element.17.low_ref, f32[2,128,512]{2,1,0:T(8,128)S(1)} %collective-permute-done.12.refs_0_, f32[1536,512]{1,0:T(8,128)S(1)} %multiply_sources.8.refs_1_), custom_call_target="tpu_custom_call" | custom-call | flops 1207959552 | tf_op jit(solution)/shard_map/multiply_sources/pallas_call | solution.py:203
  (7 shorter events, 0.3 us)
Async XLA Ops:
  1.1 10.1 %collective-permute-start.3 = (f32[128,512]{1,0:T(8,128)S(1)}, f32[128,512]{1,0:T(8,128)S(1)}, u32[]{:S(2)}, u32[]{:S(2)}) collective-permute-start(f32[128,512]{1,0:T(8,128)S(1)} %get-tuple-element.27), channel_id=1, source_target_pairs={{0,8},{1,17},{2,10},{3,19},{4,12},{5,21},{6,14},{7,23},{8,0},{9,25... | collective-permute-start | bytes 786440 | tf_op jit(solution)/shard_map/ppermute | solution.py:20
  4.2 16.6 %collective-permute-start = (f32[128,512]{1,0:T(8,128)S(1)}, f32[128,512]{1,0:T(8,128)S(1)}, u32[]{:S(2)}, u32[]{:S(2)}) collective-permute-start(f32[128,512]{1,0:T(8,128)S(1)} %get-tuple-element.28), channel_id=1, source_target_pairs={{0,8},{1,17},{2,10},{3,19},{4,12},{5,21},{6,14},{7,23},{8,0},{9,25... | collective-permute-start | bytes 786440 | tf_op jit(solution)/shard_map/ppermute | solution.py:20
  11.2 10.9 %collective-permute-start.4 = (f32[128,512]{1,0:T(8,128)S(1)}, f32[128,512]{1,0:T(8,128)S(1)}, u32[]{:S(2)}, u32[]{:S(2)}) collective-permute-start(f32[128,512]{1,0:T(8,128)S(1)} %multiply_add_fusion), channel_id=1, source_target_pairs={{0,16},{1,9},{2,18},{3,11},{4,20},{5,13},{6,22},{7,15},{8,24},{9,1... | collective-permute-start | bytes 786440 | tf_op jit(solution)/shard_map/ppermute | solution.py:20
  20.8 10.1 %collective-permute-start.1 = (f32[128,512]{1,0:T(8,128)S(1)}, f32[128,512]{1,0:T(8,128)S(1)}, u32[]{:S(2)}, u32[]{:S(2)}) collective-permute-start(f32[128,512]{1,0:T(8,128)S(1)} %multiply_add_fusion.1), channel_id=1, source_target_pairs={{0,16},{1,9},{2,18},{3,11},{4,20},{5,13},{6,22},{7,15},{8,24},{9,1... | collective-permute-start | bytes 786440 | tf_op jit(solution)/shard_map/ppermute | solution.py:20
  22.1 8.8 %collective-permute-start.5 = (f32[1,128,512]{2,1,0:T(8,128)S(1)}, f32[1,128,512]{2,1,0:T(8,128)S(1)}, u32[]{:S(2)}, u32[]{:S(2)}) collective-permute-start(f32[1,128,512]{2,1,0:T(8,128)S(1)} %bitcast.18), channel_id=1, source_target_pairs={{0,2},{1,5},{2,0},{3,7},{4,6},{5,1},{6,4},{7,3},{8,10},{9,13},{10,... | collective-permute-start | bytes 786440 | tf_op jit(solution)/shard_map/ppermute | solution.py:20
  31.0 3.6 %collective-permute-start.6 = (f32[2,128,512]{2,1,0:T(8,128)S(1)}, f32[2,128,512]{2,1,0:T(8,128)S(1)}, u32[]{:S(2)}, u32[]{:S(2)}) collective-permute-start(f32[2,128,512]{2,1,0:T(8,128)S(1)} %pad_maximum_fusion.refs_0_), channel_id=1, source_target_pairs={{0,1},{1,0},{2,3},{3,2},{4,5},{5,4},{6,7},{7,6},{8,9},{9,8},{10,11... | collective-permute-start | bytes 1572872 | tf_op jit(solution)/shard_map/ppermute | solution.py:20
  31.1 8.1 %collective-permute-start.2 = (f32[1,128,512]{2,1,0:T(8,128)S(1)}, f32[1,128,512]{2,1,0:T(8,128)S(1)}, u32[]{:S(2)}, u32[]{:S(2)}) collective-permute-start(f32[1,128,512]{2,1,0:T(8,128)S(1)} %bitcast.16), channel_id=1, source_target_pairs={{0,2},{1,5},{2,0},{3,7},{4,6},{5,1},{6,4},{7,3},{8,10},{9,13},{10,... | collective-permute-start | bytes 786440 | tf_op jit(solution)/shard_map/ppermute | solution.py:20
  33.1 9.7 %collective-permute-start.8 = (f32[2,128,512]{2,1,0:T(8,128)S(1)}, f32[2,128,512]{2,1,0:T(8,128)S(1)}, u32[]{:S(2)}, u32[]{:S(2)}) collective-permute-start(f32[2,128,512]{2,1,0:T(8,128)S(1)} %pad_maximum_fusion.refs_0_), channel_id=1, source_target_pairs={{0,4},{1,3},{2,6},{3,1},{4,0},{5,7},{6,2},{7,5},{8,12},{9,11},{10,... | collective-permute-start | bytes 1572872 | tf_op jit(solution)/shard_map/ppermute | solution.py:20
  39.3 4.2 %collective-permute-start.11 = (f32[2,128,512]{2,1,0:T(8,128)S(1)}, f32[2,128,512]{2,1,0:T(8,128)S(1)}, u32[]{:S(2)}, u32[]{:S(2)}) collective-permute-start(f32[2,128,512]{2,1,0:T(8,128)S(1)} %pad_maximum_fusion.1.refs_0_), channel_id=1, source_target_pairs={{0,1},{1,0},{2,3},{3,2},{4,5},{5,4},{6,7},{7,6},{8,9},{9,8},{10,11... | collective-permute-start | bytes 1572872 | tf_op jit(solution)/shard_map/ppermute | solution.py:20
  39.3 10.7 %collective-permute-start.7 = (f32[2,128,512]{2,1,0:T(8,128)S(1)}, f32[2,128,512]{2,1,0:T(8,128)S(1)}, u32[]{:S(2)}, u32[]{:S(2)}) collective-permute-start(f32[2,128,512]{2,1,0:T(8,128)S(1)} %pad_maximum_fusion.1.refs_0_), channel_id=1, source_target_pairs={{0,4},{1,3},{2,6},{3,1},{4,0},{5,7},{6,2},{7,5},{8,12},{9,11},{10,... | collective-permute-start | bytes 1572872 | tf_op jit(solution)/shard_map/ppermute | solution.py:20
  42.8 3.9 %collective-permute-start.10 = (f32[1,128,512]{2,1,0:T(8,128)S(1)}, f32[1,128,512]{2,1,0:T(8,128)S(1)}, u32[]{:S(2)}, u32[]{:S(2)}) collective-permute-start(f32[1,128,512]{2,1,0:T(8,128)S(1)} %get-tuple-element.25), channel_id=1, source_target_pairs={{0,1},{1,0},{2,3},{3,2},{4,5},{5,4},{6,7},{7,6},{8,9},{9,8},{10,11... | collective-permute-start | bytes 786440 | tf_op jit(solution)/shard_map/ppermute | solution.py:20
  43.1 3.6 %collective-permute-start.9 = (f32[1,128,512]{2,1,0:T(8,128)S(1)}, f32[1,128,512]{2,1,0:T(8,128)S(1)}, u32[]{:S(2)}, u32[]{:S(2)}) collective-permute-start(f32[1,128,512]{2,1,0:T(8,128)S(1)} %get-tuple-element.26), channel_id=1, source_target_pairs={{0,1},{1,0},{2,3},{3,2},{4,5},{5,4},{6,7},{7,6},{8,9},{9,8},{10,11... | collective-permute-start | bytes 786440 | tf_op jit(solution)/shard_map/ppermute | solution.py:20
  50.0 2.1 %collective-permute-start.12 = (f32[2,128,512]{2,1,0:T(8,128)S(1)}, f32[2,128,512]{2,1,0:T(8,128)S(1)}, u32[]{:S(2)}, u32[]{:S(2)}) collective-permute-start(f32[2,128,512]{2,1,0:T(8,128)S(1)} %collective-permute-done.7.refs_0_), channel_id=1, source_target_pairs={{0,1},{1,0},{2,3},{3,2},{4,5},{5,4},{6,7},{7,6},{8,9},{9,8},{10,11... | collective-permute-start | bytes 1572872 | tf_op jit(solution)/shard_map/ppermute | solution.py:20
where the time goes:
time: 55.1 us; the launch traced here: 55 us
  Pallas kernels  21.2 us (38%)
  starting transfers between devices  16.5 us (30%)
  waiting for transfers between devices  15.7 us (28%)
  local copies, waits for them, and re-layouts  1.18 us (2%)
    ppermute x13, starting transfers between devices, exchange(): return lax.ppermute(value, AXES, pairs)  16.5 us
    ppermute x13, waiting for transfers between devices, exchange(): return lax.ppermute(value, AXES, pairs)  15.7 us
    pallas_call x5, Pallas kernels, multiply(): pl.pallas_call(functools.partial(multiply_kernel, start, len(pieces), acc...  14.4 us
    pallas_call x1, Pallas kernels, split(): pl.pallas_call(functools.partial(split_kernel, lax.axis_size('row'), chun...  6.83 us
  transfers between devices with their start and end apart: 13, of which 5 were waited for; matrix products, arithmetic and copies ran while one was open for 1% of the time, Pallas kernels for 33%

commit v1 on v0

--- a/solution.py
+++ b/solution.py
@@ -10,7 +10,7 @@
 
 HALF = jnp.bfloat16
 AXES = ("irrep", "row")
-TILES = 3
+TILES = 2
 WEIGHT = 6
 
 
@@ -84,51 +84,30 @@
     return high, (value - high.astype(jnp.float32)).astype(HALF)
 
 
-def split_kernel(owners, chunks, table_ref, k_ref, high_ref, low_ref, buffers, sems):
-    count, tile, sources = buffers.shape
-    depth = sources // owners // chunks
-    steps = k_ref.shape[0] // tile
-
-    def fetch(step):
-        here = pl.ds(pl.multiple_of(step * tile, tile), tile)
-        slot = lax.rem(step, count)
-        return pltpu.make_async_copy(k_ref.at[here, :], buffers.at[slot], sems.at[slot])
-
-    for step in range(count - 1):
-        fetch(step).start()
-
-    @pl.loop(0, steps)
-    def _(step):
-        fetch(step).wait()
-
-        @pl.when(step + count - 1 < steps)
-        def _():
-            fetch(step + count - 1).start()
-
-        slot = lax.rem(step, count)
-        here = pl.ds(pl.multiple_of(step * tile, tile), tile)
-        for chunk in range(chunks):
-            for piece in range(owners):
-                start = (table_ref[piece] * chunks + chunk) * depth
-                columns = pl.ds(pl.multiple_of(start, depth), depth)
-                high, low = in_two(buffers[slot, :, columns])
-                at = (chunk * owners + piece) * depth
-                high_ref[here, at : at + depth] = high
-                low_ref[here, at : at + depth] = low
+def split_kernel(owners, chunks, table_ref, k_ref, high_ref, low_ref):
+    depth = k_ref.shape[1] // owners // chunks
+    for chunk in range(chunks):
+        for piece in range(owners):
+            start = (table_ref[piece] * chunks + chunk) * depth
+            high, low = in_two(k_ref[:, pl.ds(pl.multiple_of(start, depth), depth)])
+            at = (chunk * owners + piece) * depth
+            high_ref[:, at : at + depth] = high
+            low_ref[:, at : at + depth] = low
 
 
 def split(table, k, chunks):
     rows, sources = k.shape
-    count, tile = 3, rows // 6
+    tile = rows // 6
+    block = pl.BlockSpec((tile, sources), lambda m, table: (m, 0))
     return pl.pallas_call(
         functools.partial(split_kernel, lax.axis_size("row"), chunks),
-        in_specs=[SMEM, ANY],
-        out_specs=[VMEM, VMEM],
+        grid_spec=pltpu.PrefetchScalarGridSpec(
+            num_scalar_prefetch=1,
+            grid=(rows // tile,),
+            in_specs=[block],
+            out_specs=[block, block],
+        ),
         out_shape=[pltpu.VMEM((rows, sources), HALF)] * 2,
-        scratch_shapes=[
-            pltpu.VMEM((count, tile, sources), jnp.float32),
-            pltpu.SemaphoreType.DMA((count,)),
-        ],
         cost_estimate=pl.CostEstimate(
             flops=4 * rows * sources, bytes_accessed=4 * rows * sources, transcendentals=0
         ),

time: 55.1 us -> 53.2 us (0.966)
  waiting for transfers between devices: 15.7 us -> 13.8 us
    ppermute x13, waiting for transfers between devices: 15.7 us -> 13.8 us  [exchange(): return lax.ppermute(value, AXES, pairs)]
    pallas_call x1, Pallas kernels: 6.83 us -> 8.05 us  [split(): pl.pallas_call(functools.partial(split_kernel, lax.axis_size('row'), chun...]
    pallas_call x5, Pallas kernels: 14.4 us -> 13.6 us  [multiply(): pl.pallas_call(functools.partial(multiply_kernel, start, len(pieces), acc...]
  transfers between devices with their start and end apart: 13 -> 13, of which waited for: 5 -> 5; matrix products, arithmetic and copies ran while one was open for 1% -> 1% of each run, Pallas kernels for 33% -> 36%
where the time goes in v1:
time: 53.2 us; the launch traced here: 53 us
  Pallas kernels  21.7 us (41%)
  starting transfers between devices  16 us (30%)
  waiting for transfers between devices  13.8 us (26%)
  local copies, waits for them, and re-layouts  1.18 us (2%)
    ppermute x13, starting transfers between devices, exchange(): return lax.ppermute(value, AXES, pairs)  16 us
    ppermute x13, waiting for transfers between devices, exchange(): return lax.ppermute(value, AXES, pairs)  13.8 us
    pallas_call x5, Pallas kernels, multiply(): pl.pallas_call(functools.partial(multiply_kernel, start, len(pieces), acc...  13.6 us
    pallas_call x1, Pallas kernels, split(): pl.pallas_call(functools.partial(split_kernel, lax.axis_size('row'), chun...  8.05 us
  transfers between devices with their start and end apart: 13, of which 5 were waited for; matrix products, arithmetic and copies ran while one was open for 1% of the time, Pallas kernels for 36%

profile of v1, /device:TPU:0, one launch (start us, length us, event | category | flops | bytes accessed | tf_op | source)
XLA Modules:
  0.0 53.0 jit_solution(551780375101242997)
XLA Ops:
  0.0 1.1 %slice_bitcast_fusion = (f32[128,512]{1,0:T(8,128)S(1)}, f32[128,512]{1,0:T(8,128)S(1)}) fusion(f32[1,256,512]{2,1,0:T(8,128)} %param.2), kind=kLoop, calls=%fused_computation.4 | loop fusion | bytes 1048576 | tf_op jit(solution)/shard_map/slice | solution.py:208
  1.1 3.1 %collective-permute-start.3 = (f32[128,512]{1,0:T(8,128)S(1)}, f32[128,512]{1,0:T(8,128)S(1)}, u32[]{:S(2)}, u32[]{:S(2)}) collective-permute-start(f32[128,512]{1,0:T(8,128)S(1)} %get-tuple-element.27), channel_id=1, source_target_pairs={{0,8},{1,17},{2,10},{3,19},{4,12},{5,21},{6,14},{7,23},{8,0},{9,25... | collective-permute-start | bytes 786440 | tf_op jit(solution)/shard_map/ppermute | solution.py:20
  4.2 0.1 collective-permute-start
  4.2 0.1 stack.35.table_ref
  4.3 8.0 %split_reduced_kernel.1 = (bf16[1536,2048]{1,0:T(8,128)(2,1)S(1)}, bf16[1536,2048]{1,0:T(8,128)(2,1)S(1)}) custom-call(s32[8]{0:T(128)S(1)} %stack.35.table_ref, f32[1536,2048]{1,0:T(8,128)} %bitcast.15), custom_call_target="tpu_custom_call" | custom-call | flops 12582912 | bytes 12582912 | tf_op jit(solution)/shard_map/split_reduced_kernel/pallas_call | solution.py:102
  12.4 0.0 collective-permute-done.3
  12.4 3.0 %collective-permute-start.4 = (f32[128,512]{1,0:T(8,128)S(1)}, f32[128,512]{1,0:T(8,128)S(1)}, u32[]{:S(2)}, u32[]{:S(2)}) collective-permute-start(f32[128,512]{1,0:T(8,128)S(1)} %multiply_add_fusion), channel_id=1, source_target_pairs={{0,16},{1,9},{2,18},{3,11},{4,20},{5,13},{6,22},{7,15},{8,24},{9,1... | collective-permute-start | bytes 786440 | tf_op jit(solution)/shard_map/ppermute | solution.py:20
  15.5 3.5 %collective-permute-done = f32[128,512]{1,0:T(8,128)S(1)} collective-permute-done((f32[128,512]{1,0:T(8,128)S(1)}, f32[128,512]{1,0:T(8,128)S(1)}, u32[]{:S(2)}, u32[]{:S(2)}) %collective-permute-start) | collective-permute-done | bytes 262176 | tf_op jit(solution)/shard_map/ppermute | solution.py:20
  19.0 1.1 %collective-permute-start.1 = (f32[128,512]{1,0:T(8,128)S(1)}, f32[128,512]{1,0:T(8,128)S(1)}, u32[]{:S(2)}, u32[]{:S(2)}) collective-permute-start(f32[128,512]{1,0:T(8,128)S(1)} %multiply_add_fusion.1), channel_id=1, source_target_pairs={{0,16},{1,9},{2,18},{3,11},{4,20},{5,13},{6,22},{7,15},{8,24},{9,1... | collective-permute-start | bytes 786440 | tf_op jit(solution)/shard_map/ppermute | solution.py:20
  20.1 2.1 %collective-permute-done.4 = f32[128,512]{1,0:T(8,128)S(1)} collective-permute-done((f32[128,512]{1,0:T(8,128)S(1)}, f32[128,512]{1,0:T(8,128)S(1)}, u32[]{:S(2)}, u32[]{:S(2)}) %collective-permute-start.4) | collective-permute-done | bytes 262176 | tf_op jit(solution)/shard_map/ppermute | solution.py:20
  22.3 1.4 %collective-permute-start.5 = (f32[1,128,512]{2,1,0:T(8,128)S(1)}, f32[1,128,512]{2,1,0:T(8,128)S(1)}, u32[]{:S(2)}, u32[]{:S(2)}) collective-permute-start(f32[1,128,512]{2,1,0:T(8,128)S(1)} %bitcast.18), channel_id=1, source_target_pairs={{0,2},{1,5},{2,0},{3,7},{4,6},{5,1},{6,4},{7,3},{8,10},{9,13},{10,... | collective-permute-start | bytes 786440 | tf_op jit(solution)/shard_map/ppermute | solution.py:20
  23.7 5.9 %collective-permute-done.1 = f32[128,512]{1,0:T(8,128)S(1)} collective-permute-done((f32[128,512]{1,0:T(8,128)S(1)}, f32[128,512]{1,0:T(8,128)S(1)}, u32[]{:S(2)}, u32[]{:S(2)}) %collective-permute-start.1) | collective-permute-done | bytes 262176 | tf_op jit(solution)/shard_map/ppermute | solution.py:20
  29.6 0.0 collective-permute-done.5
  29.7 0.1 collective-permute-start.6
  29.7 2.0 %collective-permute-start.2 = (f32[1,128,512]{2,1,0:T(8,128)S(1)}, f32[1,128,512]{2,1,0:T(8,128)S(1)}, u32[]{:S(2)}, u32[]{:S(2)}) collective-permute-start(f32[1,128,512]{2,1,0:T(8,128)S(1)} %bitcast.16), channel_id=1, source_target_pairs={{0,2},{1,5},{2,0},{3,7},{4,6},{5,1},{6,4},{7,3},{8,10},{9,13},{10,... | collective-permute-start | bytes 786440 | tf_op jit(solution)/shard_map/ppermute | solution.py:20
  31.7 1.5 %collective-permute-start.8 = (f32[2,128,512]{2,1,0:T(8,128)S(1)}, f32[2,128,512]{2,1,0:T(8,128)S(1)}, u32[]{:S(2)}, u32[]{:S(2)}) collective-permute-start(f32[2,128,512]{2,1,0:T(8,128)S(1)} %pad_maximum_fusion.refs_0_), channel_id=1, source_target_pairs={{0,4},{1,3},{2,6},{3,1},{4,0},{5,7},{6,2},{7,5},{8,12},{9,11},{10,... | collective-permute-start | bytes 1572872 | tf_op jit(solution)/shard_map/ppermute | solution.py:20
  33.2 0.0 collective-permute-done.6.refs_1_
  33.2 2.9 %multiply_sources.5.refs_2_ = f32[1536,512]{1,0:T(8,128)S(1)} custom-call(bf16[1536,2048]{1,0:T(8,128)(2,1)S(1)} %get-tuple-element.16.high_ref, bf16[1536,2048]{1,0:T(8,128)(2,1)S(1)} %get-tuple-element.17.low_ref, f32[2,128,512]{2,1,0:T(8,128)S(1)} %pad_maximum_fusion.refs_0_, f32[2,128,512]{2,1,0:T(8,128)S(1)} %collective-permute-done.6.refs_1_), custom_call_target="tpu_custom_call" | custom-call | flops 2415919104 | tf_op jit(solution)/shard_map/multiply_sources/pallas_call | solution.py:182
  36.2 1.9 %collective-permute-done.2 = f32[1,128,512]{2,1,0:T(8,128)S(1)} collective-permute-done((f32[1,128,512]{2,1,0:T(8,128)S(1)}, f32[1,128,512]{2,1,0:T(8,128)S(1)}, u32[]{:S(2)}, u32[]{:S(2)}) %collective-permute-start.2) | collective-permute-done | bytes 262176 | tf_op jit(solution)/shard_map/ppermute | solution.py:20
  38.1 0.1 collective-permute-start.11
  38.1 2.7 %collective-permute-start.7 = (f32[2,128,512]{2,1,0:T(8,128)S(1)}, f32[2,128,512]{2,1,0:T(8,128)S(1)}, u32[]{:S(2)}, u32[]{:S(2)}) collective-permute-start(f32[2,128,512]{2,1,0:T(8,128)S(1)} %pad_maximum_fusion.1.refs_0_), channel_id=1, source_target_pairs={{0,4},{1,3},{2,6},{3,1},{4,0},{5,7},{6,2},{7,5},{8,12},{9,11},{10,... | collective-permute-start | bytes 1572872 | tf_op jit(solution)/shard_map/ppermute | solution.py:20
  40.9 0.4 collective-permute-done.8.refs_0_
  41.3 0.4 collective-permute-start.10
  41.7 0.2 collective-permute-start.9
  41.9 0.0 collective-permute-done.11.refs_1_
  41.9 3.1 %multiply_sources.6.refs_3_ = f32[1536,512]{1,0:T(8,128)S(1)} custom-call(bf16[1536,2048]{1,0:T(8,128)(2,1)S(1)} %get-tuple-element.16.high_ref, bf16[1536,2048]{1,0:T(8,128)(2,1)S(1)} %get-tuple-element.17.low_ref, f32[2,128,512]{2,1,0:T(8,128)S(1)} %pad_maximum_fusion.1.refs_0_, ...), custom_call_target="tpu_custom_call", output_to_operand_aliasing={{}: (4, {})} | custom-call | flops 2415919104 | tf_op jit(solution)/shard_map/multiply_sources/pallas_call | solution.py:182
  45.0 0.0 collective-permute-done.10.refs_2_
  45.0 0.0 collective-permute-done.9.refs_1_
  45.0 3.1 %multiply_sources.7.refs_1_ = f32[1536,512]{1,0:T(8,128)S(1)} custom-call(bf16[1536,2048]{1,0:T(8,128)(2,1)S(1)} %get-tuple-element.16.high_ref, bf16[1536,2048]{1,0:T(8,128)(2,1)S(1)} %get-tuple-element.17.low_ref, f32[2,128,512]{2,1,0:T(8,128)S(1)} %collective-permute-done.8.refs_0_, ...), custom_call_target="tpu_custom_call", output_to_operand_aliasing={{}: (5, {})} | custom-call | flops 2415919104 | tf_op jit(solution)/shard_map/multiply_sources/pallas_call | solution.py:182
  48.1 0.0 collective-permute-done.7.refs_0_
  48.1 0.4 collective-permute-start.12
  48.5 1.7 %multiply_sources.8.refs_1_ = f32[1536,512]{1,0:T(8,128)S(1)} custom-call(bf16[1536,2048]{1,0:T(8,128)(2,1)S(1)} %get-tuple-element.16.high_ref, bf16[1536,2048]{1,0:T(8,128)(2,1)S(1)} %get-tuple-element.17.low_ref, f32[2,128,512]{2,1,0:T(8,128)S(1)} %collective-permute-done.7.refs_0_, ...), custom_call_target="tpu_custom_call", output_to_operand_aliasing={{}: (3, {})} | custom-call | flops 1207959552 | tf_op jit(solution)/shard_map/multiply_sources/pallas_call | solution.py:182
  50.2 0.0 collective-permute-done.12.refs_0_
  50.2 2.8 %multiply_sources.9 = f32[1,1536,512]{2,1,0:T(8,128)} custom-call(bf16[1536,2048]{1,0:T(8,128)(2,1)S(1)} %get-tuple-element.16.high_ref, bf16[1536,2048]{1,0:T(8,128)(2,1)S(1)} %get-tuple-element.17.low_ref, f32[2,128,512]{2,1,0:T(8,128)S(1)} %collective-permute-done.12.refs_0_, f32[1536,512]{1,0:T(8,128)S(1)} %multiply_sources.8.refs_1_), custom_call_target="tpu_custom_call" | custom-call | flops 1207959552 | tf_op jit(solution)/shard_map/multiply_sources/pallas_call | solution.py:182
  (7 shorter events, 0.3 us)
Async XLA Ops:
  1.1 11.3 %collective-permute-start.3 = (f32[128,512]{1,0:T(8,128)S(1)}, f32[128,512]{1,0:T(8,128)S(1)}, u32[]{:S(2)}, u32[]{:S(2)}) collective-permute-start(f32[128,512]{1,0:T(8,128)S(1)} %get-tuple-element.27), channel_id=1, source_target_pairs={{0,8},{1,17},{2,10},{3,19},{4,12},{5,21},{6,14},{7,23},{8,0},{9,25... | collective-permute-start | bytes 786440 | tf_op jit(solution)/shard_map/ppermute | solution.py:20
  4.2 14.8 %collective-permute-start = (f32[128,512]{1,0:T(8,128)S(1)}, f32[128,512]{1,0:T(8,128)S(1)}, u32[]{:S(2)}, u32[]{:S(2)}) collective-permute-start(f32[128,512]{1,0:T(8,128)S(1)} %get-tuple-element.28), channel_id=1, source_target_pairs={{0,8},{1,17},{2,10},{3,19},{4,12},{5,21},{6,14},{7,23},{8,0},{9,25... | collective-permute-start | bytes 786440 | tf_op jit(solution)/shard_map/ppermute | solution.py:20
  12.4 9.8 %collective-permute-start.4 = (f32[128,512]{1,0:T(8,128)S(1)}, f32[128,512]{1,0:T(8,128)S(1)}, u32[]{:S(2)}, u32[]{:S(2)}) collective-permute-start(f32[128,512]{1,0:T(8,128)S(1)} %multiply_add_fusion), channel_id=1, source_target_pairs={{0,16},{1,9},{2,18},{3,11},{4,20},{5,13},{6,22},{7,15},{8,24},{9,1... | collective-permute-start | bytes 786440 | tf_op jit(solution)/shard_map/ppermute | solution.py:20
  19.0 10.5 %collective-permute-start.1 = (f32[128,512]{1,0:T(8,128)S(1)}, f32[128,512]{1,0:T(8,128)S(1)}, u32[]{:S(2)}, u32[]{:S(2)}) collective-permute-start(f32[128,512]{1,0:T(8,128)S(1)} %multiply_add_fusion.1), channel_id=1, source_target_pairs={{0,16},{1,9},{2,18},{3,11},{4,20},{5,13},{6,22},{7,15},{8,24},{9,1... | collective-permute-start | bytes 786440 | tf_op jit(solution)/shard_map/ppermute | solution.py:20
  22.3 7.3 %collective-permute-start.5 = (f32[1,128,512]{2,1,0:T(8,128)S(1)}, f32[1,128,512]{2,1,0:T(8,128)S(1)}, u32[]{:S(2)}, u32[]{:S(2)}) collective-permute-start(f32[1,128,512]{2,1,0:T(8,128)S(1)} %bitcast.18), channel_id=1, source_target_pairs={{0,2},{1,5},{2,0},{3,7},{4,6},{5,1},{6,4},{7,3},{8,10},{9,13},{10,... | collective-permute-start | bytes 786440 | tf_op jit(solution)/shard_map/ppermute | solution.py:20
  29.7 3.6 %collective-permute-start.6 = (f32[2,128,512]{2,1,0:T(8,128)S(1)}, f32[2,128,512]{2,1,0:T(8,128)S(1)}, u32[]{:S(2)}, u32[]{:S(2)}) collective-permute-start(f32[2,128,512]{2,1,0:T(8,128)S(1)} %pad_maximum_fusion.refs_0_), channel_id=1, source_target_pairs={{0,1},{1,0},{2,3},{3,2},{4,5},{5,4},{6,7},{7,6},{8,9},{9,8},{10,11... | collective-permute-start | bytes 1572872 | tf_op jit(solution)/shard_map/ppermute | solution.py:20
  29.7 8.3 %collective-permute-start.2 = (f32[1,128,512]{2,1,0:T(8,128)S(1)}, f32[1,128,512]{2,1,0:T(8,128)S(1)}, u32[]{:S(2)}, u32[]{:S(2)}) collective-permute-start(f32[1,128,512]{2,1,0:T(8,128)S(1)} %bitcast.16), channel_id=1, source_target_pairs={{0,2},{1,5},{2,0},{3,7},{4,6},{5,1},{6,4},{7,3},{8,10},{9,13},{10,... | collective-permute-start | bytes 786440 | tf_op jit(solution)/shard_map/ppermute | solution.py:20
  31.7 9.6 %collective-permute-start.8 = (f32[2,128,512]{2,1,0:T(8,128)S(1)}, f32[2,128,512]{2,1,0:T(8,128)S(1)}, u32[]{:S(2)}, u32[]{:S(2)}) collective-permute-start(f32[2,128,512]{2,1,0:T(8,128)S(1)} %pad_maximum_fusion.refs_0_), channel_id=1, source_target_pairs={{0,4},{1,3},{2,6},{3,1},{4,0},{5,7},{6,2},{7,5},{8,12},{9,11},{10,... | collective-permute-start | bytes 1572872 | tf_op jit(solution)/shard_map/ppermute | solution.py:20
  38.1 3.8 %collective-permute-start.11 = (f32[2,128,512]{2,1,0:T(8,128)S(1)}, f32[2,128,512]{2,1,0:T(8,128)S(1)}, u32[]{:S(2)}, u32[]{:S(2)}) collective-permute-start(f32[2,128,512]{2,1,0:T(8,128)S(1)} %pad_maximum_fusion.1.refs_0_), channel_id=1, source_target_pairs={{0,1},{1,0},{2,3},{3,2},{4,5},{5,4},{6,7},{7,6},{8,9},{9,8},{10,11... | collective-permute-start | bytes 1572872 | tf_op jit(solution)/shard_map/ppermute | solution.py:20
  38.1 9.9 %collective-permute-start.7 = (f32[2,128,512]{2,1,0:T(8,128)S(1)}, f32[2,128,512]{2,1,0:T(8,128)S(1)}, u32[]{:S(2)}, u32[]{:S(2)}) collective-permute-start(f32[2,128,512]{2,1,0:T(8,128)S(1)} %pad_maximum_fusion.1.refs_0_), channel_id=1, source_target_pairs={{0,4},{1,3},{2,6},{3,1},{4,0},{5,7},{6,2},{7,5},{8,12},{9,11},{10,... | collective-permute-start | bytes 1572872 | tf_op jit(solution)/shard_map/ppermute | solution.py:20
  41.3 3.7 %collective-permute-start.10 = (f32[1,128,512]{2,1,0:T(8,128)S(1)}, f32[1,128,512]{2,1,0:T(8,128)S(1)}, u32[]{:S(2)}, u32[]{:S(2)}) collective-permute-start(f32[1,128,512]{2,1,0:T(8,128)S(1)} %get-tuple-element.25), channel_id=1, source_target_pairs={{0,1},{1,0},{2,3},{3,2},{4,5},{5,4},{6,7},{7,6},{8,9},{9,8},{10,11... | collective-permute-start | bytes 786440 | tf_op jit(solution)/shard_map/ppermute | solution.py:20
  41.7 3.3 %collective-permute-start.9 = (f32[1,128,512]{2,1,0:T(8,128)S(1)}, f32[1,128,512]{2,1,0:T(8,128)S(1)}, u32[]{:S(2)}, u32[]{:S(2)}) collective-permute-start(f32[1,128,512]{2,1,0:T(8,128)S(1)} %get-tuple-element.26), channel_id=1, source_target_pairs={{0,1},{1,0},{2,3},{3,2},{4,5},{5,4},{6,7},{7,6},{8,9},{9,8},{10,11... | collective-permute-start | bytes 786440 | tf_op jit(solution)/shard_map/ppermute | solution.py:20
  48.1 2.1 %collective-permute-start.12 = (f32[2,128,512]{2,1,0:T(8,128)S(1)}, f32[2,128,512]{2,1,0:T(8,128)S(1)}, u32[]{:S(2)}, u32[]{:S(2)}) collective-permute-start(f32[2,128,512]{2,1,0:T(8,128)S(1)} %collective-permute-done.7.refs_0_), channel_id=1, source_target_pairs={{0,1},{1,0},{2,3},{3,2},{4,5},{5,4},{6,7},{7,6},{8,9},{9,8},{10,11... | collective-permute-start | bytes 1572872 | tf_op jit(solution)/shard_map/ppermute | solution.py:20

commit v2 on v1

--- a/solution.py
+++ b/solution.py
@@ -1,4 +1,5 @@
 import functools
+import itertools
 import math
 
 import jax
@@ -10,7 +11,7 @@
 
 HALF = jnp.bfloat16
 AXES = ("irrep", "row")
-TILES = 2
+TILES = (2, 4)
 WEIGHT = 6
 
 
@@ -24,8 +25,8 @@
     return [(step + core) % count for core in range(2)]
 
 
-def across(held, step, bits):
-    return exchange(held, [2 << bit for bit in turns(step, bits)])
+def across(held, step, bits, chunk):
+    return exchange(held, [2 << bit for bit in turns(step + chunk, bits)])
 
 
 def swapped(held, parts):
@@ -33,9 +34,9 @@
     return [exchange(held[at : at + size], [1, 1]) for at in range(0, held.shape[0], size)]
 
 
-def gather_chips(held, steps, bits, others=None):
+def gather_chips(held, steps, bits, chunk, others=None):
     for step in steps:
-        held = jnp.concatenate([held, after(across(held, step, bits), others)])
+        held = jnp.concatenate([held, after(across(held, step, bits, chunk), others)])
     return held
 
 
@@ -45,15 +46,14 @@
     core = me & 1
     half = 1 << (bits - 1)
     table = []
-    for group in range(2):
-        for other in range(2):
-            for at in range(group * half, (group + 1) * half):
-                rel = [other, other]
-                for step in range(bits):
-                    if at >> step & 1:
-                        for side, bit in enumerate(turns(step, bits)):
-                            rel[side] ^= 2 << bit
-                table.append(me ^ jnp.where(core ^ other == 1, rel[1], rel[0]))
+    for chunk, group, other in itertools.product(range(2), repeat=3):
+        for at in range(group * half, (group + 1) * half):
+            rel = [other, other]
+            for step in range(bits):
+                if at >> step & 1:
+                    for side, bit in enumerate(turns(step + chunk, bits)):
+                        rel[side] ^= 2 << bit
+            table.append(me ^ jnp.where(core ^ other == 1, rel[1], rel[0]))
     signs = []
     for step in range(levels):
         bit = turns(step, levels)
@@ -88,7 +88,7 @@
     depth = k_ref.shape[1] // owners // chunks
     for chunk in range(chunks):
         for piece in range(owners):
-            start = (table_ref[piece] * chunks + chunk) * depth
+            start = (table_ref[chunk * owners + piece] * chunks + chunk) * depth
             high, low = in_two(k_ref[:, pl.ds(pl.multiple_of(start, depth), depth)])
             at = (chunk * owners + piece) * depth
             high_ref[:, at : at + depth] = high
@@ -97,7 +97,7 @@
 
 def split(table, k, chunks):
     rows, sources = k.shape
-    tile = rows // 6
+    tile = rows // 8
     block = pl.BlockSpec((tile, sources), lambda m, table: (m, 0))
     return pl.pallas_call(
         functools.partial(split_kernel, lax.axis_size("row"), chunks),
@@ -130,7 +130,8 @@
             f_low[at : at + depth, :] = low
             at += depth
     sources = slice(start * depth, start * depth + at)
-    tile = high_ref.shape[0] // TILES
+    tiles = TILES[last]
+    tile = high_ref.shape[0] // tiles
 
     def product(step):
         here = pl.ds(pl.multiple_of(step * tile, tile), tile)
@@ -142,7 +143,7 @@
 
     if not last:
 
-        @pl.loop(0, TILES)
+        @pl.loop(0, tiles)
         def _(step):
             here, total = product(step)
             out_ref[here, :] = total
@@ -155,13 +156,13 @@
                 result.at[here, :], out_ref.at[0, here, :], sems.at[step]
             )
 
-        @pl.loop(0, TILES)
+        @pl.loop(0, tiles)
         def _(step):
             here, total = product(step)
             result[here, :] = total
             copy(here, step).start()
 
-        for step in range(TILES):
+        for step in range(tiles):
             copy(slice(step * tile, (step + 1) * tile), step).wait()
 
 
@@ -174,7 +175,7 @@
     scratch = [pltpu.VMEM((count * depth, width), HALF)] * 2
     alias = {}
     if last:
-        scratch += [pltpu.VMEM((rows, width), jnp.float32), pltpu.SemaphoreType.DMA((TILES,))]
+        scratch += [pltpu.VMEM((rows, width), jnp.float32), pltpu.SemaphoreType.DMA((TILES[1],))]
         shape = jax.ShapeDtypeStruct((1, rows, width), jnp.float32)
     else:
         shape = pltpu.VMEM((rows, width), jnp.float32)
@@ -212,14 +213,14 @@
         parts = [fold(*pair, signs[step], step, levels) for pair in zip(parts, partners)]
     last = bits - 1
     group = lax.axis_size("row") // 2
-    early = gather_chips(parts[0][None], range(last), bits)
+    early = gather_chips(parts[0][None], range(last), bits, 0)
     early = after(early, parts[1])
-    arrived = across(early, last, bits)
+    arrived = across(early, last, bits, 0)
     out = multiply(*ks, [early, exchange(early, [1, 1])], 0, None)
-    late = gather_chips(parts[1][None], range(last), bits, out)
+    late = gather_chips(parts[1][None], range(last), bits, 1, out)
     out = multiply(*ks, [late, exchange(late, [1, 1])], 2 * group, out)
     out = multiply(*ks, [arrived, *swapped(arrived, 2)], group, out)
-    arrived = after(across(late, last, bits), out)
+    arrived = after(across(late, last, bits, 1), out)
     out = multiply(*ks, [arrived], 3 * group, out)
     return multiply(*ks, [exchange(arrived, [1, 1])], 3 * group + group // 2, out, True)
 

time: 53.2 us -> 55.6 us (1.045)
  waiting for transfers between devices: 13.8 us -> 16.6 us
  starting transfers between devices: 16 us -> 15 us
  Pallas kernels: 21.7 us -> 22.3 us
    ppermute x13, waiting for transfers between devices: 13.8 us -> 16.6 us  [exchange(): return lax.ppermute(value, AXES, pairs)]
    ppermute x13, starting transfers between devices: 16 us -> 15 us  [exchange(): return lax.ppermute(value, AXES, pairs)]
  transfers between devices with their start and end apart: 13 -> 13, of which waited for: 5 -> 7; matrix products, arithmetic and copies ran while one was open for 1% -> 1% of each run, Pallas kernels for 36% -> 35%
where the time goes in v2:
time: 55.6 us; the launch traced here: 55.4 us
  Pallas kernels  22.3 us (40%)
  waiting for transfers between devices  16.6 us (30%)
  starting transfers between devices  15 us (27%)
  local copies, waits for them, and re-layouts  1.19 us (2%)
    ppermute x13, waiting for transfers between devices, exchange(): return lax.ppermute(value, AXES, pairs)  16.6 us
    ppermute x13, starting transfers between devices, exchange(): return lax.ppermute(value, AXES, pairs)  15 us
    pallas_call x5, Pallas kernels, multiply(): pl.pallas_call(functools.partial(multiply_kernel, start, len(pieces), acc...  13.7 us
    pallas_call x1, Pallas kernels, split(): pl.pallas_call(functools.partial(split_kernel, lax.axis_size('row'), chun...  8.56 us
  transfers between devices with their start and end apart: 13, of which 7 were waited for; matrix products, arithmetic and copies ran while one was open for 1% of the time, Pallas kernels for 35%

profile of v2, /device:TPU:0, one launch (start us, length us, event | category | flops | bytes accessed | tf_op | source)
XLA Modules:
  0.0 55.4 jit_solution(12691439817281068431)
XLA Ops:
  0.0 1.1 %slice_bitcast_fusion = (f32[128,512]{1,0:T(8,128)S(1)}, f32[128,512]{1,0:T(8,128)S(1)}) fusion(f32[1,256,512]{2,1,0:T(8,128)} %param.2), kind=kLoop, calls=%fused_computation.4 | loop fusion | bytes 1048576 | tf_op jit(solution)/shard_map/slice | solution.py:209
  1.1 3.1 %collective-permute-start.3 = (f32[128,512]{1,0:T(8,128)S(1)}, f32[128,512]{1,0:T(8,128)S(1)}, u32[]{:S(2)}, u32[]{:S(2)}) collective-permute-start(f32[128,512]{1,0:T(8,128)S(1)} %get-tuple-element.27), channel_id=1, source_target_pairs={{0,8},{1,17},{2,10},{3,19},{4,12},{5,21},{6,14},{7,23},{8,0},{9,25... | collective-permute-start | bytes 786440 | tf_op jit(solution)/shard_map/ppermute | solution.py:21
  4.2 0.1 collective-permute-start
  4.2 0.1 stack.43.table_ref
  4.3 8.6 %split_reduced_kernel.1 = (bf16[1536,2048]{1,0:T(8,128)(2,1)S(1)}, bf16[1536,2048]{1,0:T(8,128)(2,1)S(1)}) custom-call(s32[16]{0:T(128)S(1)} %stack.43.table_ref, f32[1536,2048]{1,0:T(8,128)} %bitcast.15), custom_call_target="tpu_custom_call" | custom-call | flops 12582912 | bytes 12582912 | tf_op jit(solution)/shard_map/split_reduced_kernel/pallas_call | solution.py:102
  12.9 0.0 collective-permute-done.3
  13.0 3.0 %collective-permute-start.4 = (f32[128,512]{1,0:T(8,128)S(1)}, f32[128,512]{1,0:T(8,128)S(1)}, u32[]{:S(2)}, u32[]{:S(2)}) collective-permute-start(f32[128,512]{1,0:T(8,128)S(1)} %multiply_add_fusion), channel_id=1, source_target_pairs={{0,16},{1,9},{2,18},{3,11},{4,20},{5,13},{6,22},{7,15},{8,24},{9,1... | collective-permute-start | bytes 786440 | tf_op jit(solution)/shard_map/ppermute | solution.py:21
  16.0 0.8 %collective-permute-done = f32[128,512]{1,0:T(8,128)S(1)} collective-permute-done((f32[128,512]{1,0:T(8,128)S(1)}, f32[128,512]{1,0:T(8,128)S(1)}, u32[]{:S(2)}, u32[]{:S(2)}) %collective-permute-start) | collective-permute-done | bytes 262176 | tf_op jit(solution)/shard_map/ppermute | solution.py:21
  16.8 2.6 %collective-permute-start.1 = (f32[128,512]{1,0:T(8,128)S(1)}, f32[128,512]{1,0:T(8,128)S(1)}, u32[]{:S(2)}, u32[]{:S(2)}) collective-permute-start(f32[128,512]{1,0:T(8,128)S(1)} %multiply_add_fusion.1), channel_id=1, source_target_pairs={{0,16},{1,9},{2,18},{3,11},{4,20},{5,13},{6,22},{7,15},{8,24},{9,1... | collective-permute-start | bytes 786440 | tf_op jit(solution)/shard_map/ppermute | solution.py:21
  19.4 3.3 %collective-permute-done.4 = f32[128,512]{1,0:T(8,128)S(1)} collective-permute-done((f32[128,512]{1,0:T(8,128)S(1)}, f32[128,512]{1,0:T(8,128)S(1)}, u32[]{:S(2)}, u32[]{:S(2)}) %collective-permute-start.4) | collective-permute-done | bytes 262176 | tf_op jit(solution)/shard_map/ppermute | solution.py:21
  22.8 1.6 %collective-permute-start.5 = (f32[1,128,512]{2,1,0:T(8,128)S(1)}, f32[1,128,512]{2,1,0:T(8,128)S(1)}, u32[]{:S(2)}, u32[]{:S(2)}) collective-permute-start(f32[1,128,512]{2,1,0:T(8,128)S(1)} %bitcast.18), channel_id=1, source_target_pairs={{0,2},{1,5},{2,0},{3,7},{4,6},{5,1},{6,4},{7,3},{8,10},{9,13},{10,... | collective-permute-start | bytes 786440 | tf_op jit(solution)/shard_map/ppermute | solution.py:21
  24.4 3.2 %collective-permute-done.1 = f32[128,512]{1,0:T(8,128)S(1)} collective-permute-done((f32[128,512]{1,0:T(8,128)S(1)}, f32[128,512]{1,0:T(8,128)S(1)}, u32[]{:S(2)}, u32[]{:S(2)}) %collective-permute-start.1) | collective-permute-done | bytes 262176 | tf_op jit(solution)/shard_map/ppermute | solution.py:21
  27.6 1.6 %collective-permute-done.5 = f32[1,128,512]{2,1,0:T(8,128)S(1)} collective-permute-done((f32[1,128,512]{2,1,0:T(8,128)S(1)}, f32[1,128,512]{2,1,0:T(8,128)S(1)}, u32[]{:S(2)}, u32[]{:S(2)}) %collective-permute-start.5) | collective-permute-done | bytes 262176 | tf_op jit(solution)/shard_map/ppermute | solution.py:21
  29.3 0.1 collective-permute-start.6
  29.4 1.6 %collective-permute-start.2 = (f32[1,128,512]{2,1,0:T(8,128)S(1)}, f32[1,128,512]{2,1,0:T(8,128)S(1)}, u32[]{:S(2)}, u32[]{:S(2)}) collective-permute-start(f32[1,128,512]{2,1,0:T(8,128)S(1)} %bitcast.16), channel_id=1, source_target_pairs={{0,4},{1,3},{2,6},{3,1},{4,0},{5,7},{6,2},{7,5},{8,12},{9,11},{10,... | collective-permute-start | bytes 786440 | tf_op jit(solution)/shard_map/ppermute | solution.py:21
  30.9 0.5 collective-permute-start.8
  31.4 0.0 collective-permute-done.6.refs_1_
  31.4 2.9 %multiply_sources.5.refs_2_ = f32[1536,512]{1,0:T(8,128)S(1)} custom-call(bf16[1536,2048]{1,0:T(8,128)(2,1)S(1)} %get-tuple-element.16.high_ref, bf16[1536,2048]{1,0:T(8,128)(2,1)S(1)} %get-tuple-element.17.low_ref, f32[2,128,512]{2,1,0:T(8,128)S(1)} %pad_maximum_fusion.refs_0_, f32[2,128,512]{2,1,0:T(8,128)S(1)} %collective-permute-done.6.refs_1_), custom_call_target="tpu_custom_call" | custom-call | flops 2415919104 | tf_op jit(solution)/shard_map/multiply_sources/pallas_call | solution.py:183
  34.4 1.4 %collective-permute-done.2 = f32[1,128,512]{2,1,0:T(8,128)S(1)} collective-permute-done((f32[1,128,512]{2,1,0:T(8,128)S(1)}, f32[1,128,512]{2,1,0:T(8,128)S(1)}, u32[]{:S(2)}, u32[]{:S(2)}) %collective-permute-start.2) | collective-permute-done | bytes 262176 | tf_op jit(solution)/shard_map/ppermute | solution.py:21
  35.8 0.1 collective-permute-start.11
  35.9 1.6 %collective-permute-start.7 = (f32[2,128,512]{2,1,0:T(8,128)S(1)}, f32[2,128,512]{2,1,0:T(8,128)S(1)}, u32[]{:S(2)}, u32[]{:S(2)}) collective-permute-start(f32[2,128,512]{2,1,0:T(8,128)S(1)} %pad_maximum_fusion.1.refs_0_), channel_id=1, source_target_pairs={{0,2},{1,5},{2,0},{3,7},{4,6},{5,1},{6,4},{7,3},{8,10},{9,13},{10,... | collective-permute-start | bytes 1572872 | tf_op jit(solution)/shard_map/ppermute | solution.py:21
  37.5 6.2 %collective-permute-done.8.refs_0_ = f32[2,128,512]{2,1,0:T(8,128)S(1)} collective-permute-done((f32[2,128,512]{2,1,0:T(8,128)S(1)}, f32[2,128,512]{2,1,0:T(8,128)S(1)}, u32[]{:S(2)}, u32[]{:S(2)}) %collective-permute-start.8) | collective-permute-done | bytes 524320 | tf_op jit(solution)/shard_map/ppermute | solution.py:21
  43.8 0.1 collective-permute-start.10
  43.9 0.5 collective-permute-start.9
  44.4 0.0 collective-permute-done.11.refs_1_
  44.4 3.1 %multiply_sources.6.refs_3_ = f32[1536,512]{1,0:T(8,128)S(1)} custom-call(bf16[1536,2048]{1,0:T(8,128)(2,1)S(1)} %get-tuple-element.16.high_ref, bf16[1536,2048]{1,0:T(8,128)(2,1)S(1)} %get-tuple-element.17.low_ref, f32[2,128,512]{2,1,0:T(8,128)S(1)} %pad_maximum_fusion.1.refs_0_, ...), custom_call_target="tpu_custom_call", output_to_operand_aliasing={{}: (4, {})} | custom-call | flops 2415919104 | tf_op jit(solution)/shard_map/multiply_sources/pallas_call | solution.py:183
  47.4 0.0 collective-permute-done.10.refs_2_
  47.5 0.0 collective-permute-done.9.refs_1_
  47.5 3.1 %multiply_sources.7.refs_1_ = f32[1536,512]{1,0:T(8,128)S(1)} custom-call(bf16[1536,2048]{1,0:T(8,128)(2,1)S(1)} %get-tuple-element.16.high_ref, bf16[1536,2048]{1,0:T(8,128)(2,1)S(1)} %get-tuple-element.17.low_ref, f32[2,128,512]{2,1,0:T(8,128)S(1)} %collective-permute-done.8.refs_0_, ...), custom_call_target="tpu_custom_call", output_to_operand_aliasing={{}: (5, {})} | custom-call | flops 2415919104 | tf_op jit(solution)/shard_map/multiply_sources/pallas_call | solution.py:183
  50.5 0.0 collective-permute-done.7.refs_0_
  50.6 0.1 collective-permute-start.12
  50.7 1.7 %multiply_sources.8.refs_1_ = f32[1536,512]{1,0:T(8,128)S(1)} custom-call(bf16[1536,2048]{1,0:T(8,128)(2,1)S(1)} %get-tuple-element.16.high_ref, bf16[1536,2048]{1,0:T(8,128)(2,1)S(1)} %get-tuple-element.17.low_ref, f32[2,128,512]{2,1,0:T(8,128)S(1)} %collective-permute-done.7.refs_0_, ...), custom_call_target="tpu_custom_call", output_to_operand_aliasing={{}: (3, {})} | custom-call | flops 1207959552 | tf_op jit(solution)/shard_map/multiply_sources/pallas_call | solution.py:183
  52.4 0.1 collective-permute-done.12.refs_0_
  52.5 2.9 %multiply_sources.9 = f32[1,1536,512]{2,1,0:T(8,128)} custom-call(bf16[1536,2048]{1,0:T(8,128)(2,1)S(1)} %get-tuple-element.16.high_ref, bf16[1536,2048]{1,0:T(8,128)(2,1)S(1)} %get-tuple-element.17.low_ref, f32[2,128,512]{2,1,0:T(8,128)S(1)} %collective-permute-done.12.refs_0_, f32[1536,512]{1,0:T(8,128)S(1)} %multiply_sources.8.refs_1_), custom_call_target="tpu_custom_call" | custom-call | flops 1207959552 | tf_op jit(solution)/shard_map/multiply_sources/pallas_call | solution.py:183
  (7 shorter events, 0.3 us)
Async XLA Ops:
  1.1 11.8 %collective-permute-start.3 = (f32[128,512]{1,0:T(8,128)S(1)}, f32[128,512]{1,0:T(8,128)S(1)}, u32[]{:S(2)}, u32[]{:S(2)}) collective-permute-start(f32[128,512]{1,0:T(8,128)S(1)} %get-tuple-element.27), channel_id=1, source_target_pairs={{0,8},{1,17},{2,10},{3,19},{4,12},{5,21},{6,14},{7,23},{8,0},{9,25... | collective-permute-start | bytes 786440 | tf_op jit(solution)/shard_map/ppermute | solution.py:21
  4.2 12.6 %collective-permute-start = (f32[128,512]{1,0:T(8,128)S(1)}, f32[128,512]{1,0:T(8,128)S(1)}, u32[]{:S(2)}, u32[]{:S(2)}) collective-permute-start(f32[128,512]{1,0:T(8,128)S(1)} %get-tuple-element.28), channel_id=1, source_target_pairs={{0,8},{1,17},{2,10},{3,19},{4,12},{5,21},{6,14},{7,23},{8,0},{9,25... | collective-permute-start | bytes 786440 | tf_op jit(solution)/shard_map/ppermute | solution.py:21
  13.0 9.8 %collective-permute-start.4 = (f32[128,512]{1,0:T(8,128)S(1)}, f32[128,512]{1,0:T(8,128)S(1)}, u32[]{:S(2)}, u32[]{:S(2)}) collective-permute-start(f32[128,512]{1,0:T(8,128)S(1)} %multiply_add_fusion), channel_id=1, source_target_pairs={{0,16},{1,9},{2,18},{3,11},{4,20},{5,13},{6,22},{7,15},{8,24},{9,1... | collective-permute-start | bytes 786440 | tf_op jit(solution)/shard_map/ppermute | solution.py:21
  16.8 10.8 %collective-permute-start.1 = (f32[128,512]{1,0:T(8,128)S(1)}, f32[128,512]{1,0:T(8,128)S(1)}, u32[]{:S(2)}, u32[]{:S(2)}) collective-permute-start(f32[128,512]{1,0:T(8,128)S(1)} %multiply_add_fusion.1), channel_id=1, source_target_pairs={{0,16},{1,9},{2,18},{3,11},{4,20},{5,13},{6,22},{7,15},{8,24},{9,1... | collective-permute-start | bytes 786440 | tf_op jit(solution)/shard_map/ppermute | solution.py:21
  22.8 6.4 %collective-permute-start.5 = (f32[1,128,512]{2,1,0:T(8,128)S(1)}, f32[1,128,512]{2,1,0:T(8,128)S(1)}, u32[]{:S(2)}, u32[]{:S(2)}) collective-permute-start(f32[1,128,512]{2,1,0:T(8,128)S(1)} %bitcast.18), channel_id=1, source_target_pairs={{0,2},{1,5},{2,0},{3,7},{4,6},{5,1},{6,4},{7,3},{8,10},{9,13},{10,... | collective-permute-start | bytes 786440 | tf_op jit(solution)/shard_map/ppermute | solution.py:21
  29.3 2.2 %collective-permute-start.6 = (f32[2,128,512]{2,1,0:T(8,128)S(1)}, f32[2,128,512]{2,1,0:T(8,128)S(1)}, u32[]{:S(2)}, u32[]{:S(2)}) collective-permute-start(f32[2,128,512]{2,1,0:T(8,128)S(1)} %pad_maximum_fusion.refs_0_), channel_id=1, source_target_pairs={{0,1},{1,0},{2,3},{3,2},{4,5},{5,4},{6,7},{7,6},{8,9},{9,8},{10,11... | collective-permute-start | bytes 1572872 | tf_op jit(solution)/shard_map/ppermute | solution.py:21
  29.4 6.4 %collective-permute-start.2 = (f32[1,128,512]{2,1,0:T(8,128)S(1)}, f32[1,128,512]{2,1,0:T(8,128)S(1)}, u32[]{:S(2)}, u32[]{:S(2)}) collective-permute-start(f32[1,128,512]{2,1,0:T(8,128)S(1)} %bitcast.16), channel_id=1, source_target_pairs={{0,4},{1,3},{2,6},{3,1},{4,0},{5,7},{6,2},{7,5},{8,12},{9,11},{10,... | collective-permute-start | bytes 786440 | tf_op jit(solution)/shard_map/ppermute | solution.py:21
  30.9 12.8 %collective-permute-start.8 = (f32[2,128,512]{2,1,0:T(8,128)S(1)}, f32[2,128,512]{2,1,0:T(8,128)S(1)}, u32[]{:S(2)}, u32[]{:S(2)}) collective-permute-start(f32[2,128,512]{2,1,0:T(8,128)S(1)} %pad_maximum_fusion.refs_0_), channel_id=1, source_target_pairs={{0,4},{1,3},{2,6},{3,1},{4,0},{5,7},{6,2},{7,5},{8,12},{9,11},{10,... | collective-permute-start | bytes 1572872 | tf_op jit(solution)/shard_map/ppermute | solution.py:21
  35.8 8.5 %collective-permute-start.11 = (f32[2,128,512]{2,1,0:T(8,128)S(1)}, f32[2,128,512]{2,1,0:T(8,128)S(1)}, u32[]{:S(2)}, u32[]{:S(2)}) collective-permute-start(f32[2,128,512]{2,1,0:T(8,128)S(1)} %pad_maximum_fusion.1.refs_0_), channel_id=1, source_target_pairs={{0,1},{1,0},{2,3},{3,2},{4,5},{5,4},{6,7},{7,6},{8,9},{9,8},{10,11... | collective-permute-start | bytes 1572872 | tf_op jit(solution)/shard_map/ppermute | solution.py:21
  35.9 14.6 %collective-permute-start.7 = (f32[2,128,512]{2,1,0:T(8,128)S(1)}, f32[2,128,512]{2,1,0:T(8,128)S(1)}, u32[]{:S(2)}, u32[]{:S(2)}) collective-permute-start(f32[2,128,512]{2,1,0:T(8,128)S(1)} %pad_maximum_fusion.1.refs_0_), channel_id=1, source_target_pairs={{0,2},{1,5},{2,0},{3,7},{4,6},{5,1},{6,4},{7,3},{8,10},{9,13},{10,... | collective-permute-start | bytes 1572872 | tf_op jit(solution)/shard_map/ppermute | solution.py:21
  43.8 3.7 %collective-permute-start.10 = (f32[1,128,512]{2,1,0:T(8,128)S(1)}, f32[1,128,512]{2,1,0:T(8,128)S(1)}, u32[]{:S(2)}, u32[]{:S(2)}) collective-permute-start(f32[1,128,512]{2,1,0:T(8,128)S(1)} %get-tuple-element.25), channel_id=1, source_target_pairs={{0,1},{1,0},{2,3},{3,2},{4,5},{5,4},{6,7},{7,6},{8,9},{9,8},{10,11... | collective-permute-start | bytes 786440 | tf_op jit(solution)/shard_map/ppermute | solution.py:21
  43.9 3.6 %collective-permute-start.9 = (f32[1,128,512]{2,1,0:T(8,128)S(1)}, f32[1,128,512]{2,1,0:T(8,128)S(1)}, u32[]{:S(2)}, u32[]{:S(2)}) collective-permute-start(f32[1,128,512]{2,1,0:T(8,128)S(1)} %get-tuple-element.26), channel_id=1, source_target_pairs={{0,1},{1,0},{2,3},{3,2},{4,5},{5,4},{6,7},{7,6},{8,9},{9,8},{10,11... | collective-permute-start | bytes 786440 | tf_op jit(solution)/shard_map/ppermute | solution.py:21
  50.6 2.0 %collective-permute-start.12 = (f32[2,128,512]{2,1,0:T(8,128)S(1)}, f32[2,128,512]{2,1,0:T(8,128)S(1)}, u32[]{:S(2)}, u32[]{:S(2)}) collective-permute-start(f32[2,128,512]{2,1,0:T(8,128)S(1)} %collective-permute-done.7.refs_0_), channel_id=1, source_target_pairs={{0,1},{1,0},{2,3},{3,2},{4,5},{5,4},{6,7},{7,6},{8,9},{9,8},{10,11... | collective-permute-start | bytes 1572872 | tf_op jit(solution)/shard_map/ppermute | solution.py:21

commit v3 on v2

--- a/solution.py
+++ b/solution.py
@@ -11,8 +11,7 @@
 
 HALF = jnp.bfloat16
 AXES = ("irrep", "row")
-TILES = (2, 4)
-WEIGHT = 6
+TILES = (2, 2)
 
 
 def exchange(value, masks):
@@ -25,33 +24,26 @@
     return [(step + core) % count for core in range(2)]
 
 
-def across(held, step, bits, chunk):
-    return exchange(held, [2 << bit for bit in turns(step + chunk, bits)])
+def across(held, step, bits):
+    return exchange(held, [2 << bit for bit in turns(step, bits)])
 
 
 def swapped(held, parts):
     size = held.shape[0] // parts
     return [exchange(held[at : at + size], [1, 1]) for at in range(0, held.shape[0], size)]
-
-
-def gather_chips(held, steps, bits, chunk, others=None):
-    for step in steps:
-        held = jnp.concatenate([held, after(across(held, step, bits, chunk), others)])
-    return held
 
 
 def numbers(levels, bits):
     me = lax.axis_index("row").astype(jnp.int32)
     octant = lax.axis_index("irrep").astype(jnp.int32)
     core = me & 1
-    half = 1 << (bits - 1)
     table = []
-    for chunk, group, other in itertools.product(range(2), repeat=3):
-        for at in range(group * half, (group + 1) * half):
+    for stage, other in itertools.product(range(bits + 1), range(2)):
+        for at in range(1 << stage >> 1, 1 << stage):
             rel = [other, other]
             for step in range(bits):
                 if at >> step & 1:
-                    for side, bit in enumerate(turns(step + chunk, bits)):
+                    for side, bit in enumerate(turns(step, bits)):
                         rel[side] ^= 2 << bit
             table.append(me ^ jnp.where(core ^ other == 1, rel[1], rel[0]))
     signs = []
@@ -71,7 +63,7 @@
     total = partner + sign * holding
     if step == levels - 1:
         total = total * (1.0 / math.sqrt(lax.axis_size("irrep")))
-    return lax.optimization_barrier(total)
+    return total
 
 
 def partner_of(holding, step, levels):
@@ -88,7 +80,7 @@
     depth = k_ref.shape[1] // owners // chunks
     for chunk in range(chunks):
         for piece in range(owners):
-            start = (table_ref[chunk * owners + piece] * chunks + chunk) * depth
+            start = (table_ref[piece] * chunks + chunk) * depth
             high, low = in_two(k_ref[:, pl.ds(pl.multiple_of(start, depth), depth)])
             at = (chunk * owners + piece) * depth
             high_ref[:, at : at + depth] = high
@@ -118,17 +110,19 @@
 
 def multiply_kernel(start, arrays, accumulate, last, high_ref, low_ref, *refs):
     refs = list(refs)
-    f_refs = [refs.pop(0) for _ in range(arrays)]
+    f_refs = [[refs.pop(0) for _ in range(count)] for count in arrays]
     before = refs.pop(0) if accumulate else None
     out_ref, f_high, f_low = refs[:3]
-    depth = f_refs[0].shape[1]
-    at = 0
-    for ref in f_refs:
-        for piece in range(ref.shape[0]):
-            high, low = in_two(ref[piece])
-            f_high[at : at + depth, :] = high
-            f_low[at : at + depth, :] = low
-            at += depth
+    depth, width = f_refs[0][0].shape[1:]
+    for part, of in enumerate(f_refs):
+        columns = slice(part * width, (part + 1) * width)
+        at = 0
+        for ref in of:
+            for piece in range(ref.shape[0]):
+                high, low = in_two(ref[piece])
+                f_high[at : at + depth, columns] = high
+                f_low[at : at + depth, columns] = low
+                at += depth
     sources = slice(start * depth, start * depth + at)
     tiles = TILES[last]
     tile = high_ref.shape[0] // tiles
@@ -166,11 +160,11 @@
             copy(slice(step * tile, (step + 1) * tile), step).wait()
 
 
-def multiply(k_high, k_low, pieces, start, before, last=False):
-    rows = k_high.shape[0]
-    count, (depth, width) = sum(a.shape[0] for a in pieces), pieces[0].shape[1:]
+def multiply(k_high, k_low, pieces, start, before, last=False, weight=6):
+    rows, (depth, width) = k_high.shape[0], pieces[0][0].shape[1:]
+    count, width = sum(a.shape[0] for a in pieces[0]), width * len(pieces)
     accumulate = before is not None
-    operands = [k_high, k_low, *pieces] + ([before] if accumulate else [])
+    operands = [k_high, k_low, *itertools.chain(*pieces)] + ([before] if accumulate else [])
     operands = [pltpu.with_memory_space_constraint(a, pltpu.VMEM) for a in operands]
     scratch = [pltpu.VMEM((count * depth, width), HALF)] * 2
     alias = {}
@@ -181,14 +175,14 @@
         shape = pltpu.VMEM((rows, width), jnp.float32)
         alias = {len(operands) - 1: 0} if accumulate else {}
     return pl.pallas_call(
-        functools.partial(multiply_kernel, start, len(pieces), accumulate, last),
+        functools.partial(multiply_kernel, start, [len(of) for of in pieces], accumulate, last),
         in_specs=[VMEM] * len(operands),
         out_specs=ANY if last else VMEM,
         out_shape=shape,
         input_output_aliases=alias,
         scratch_shapes=scratch,
         cost_estimate=pl.CostEstimate(
-            flops=int(WEIGHT * rows * count * depth * width), bytes_accessed=0, transcendentals=0
+            flops=int(weight * rows * count * depth * width), bytes_accessed=0, transcendentals=0
         ),
         compiler_params=pltpu.CompilerParams(vmem_limit_bytes=14 * 2**20),
         name="multiply_sources",
@@ -206,23 +200,34 @@
     half = mine.shape[0] // 2
     table, signs = numbers(levels, bits)
     ks = split(table, reduced_kernel[0], 2)
-    parts = [lax.optimization_barrier(mine[at * half : (at + 1) * half]) for at in range(2)]
+    early, late = mine[:half], mine[half:]
+    owners = lax.axis_size("row")
     for step in range(levels):
-        partners = [partner_of(part, step, levels) for part in parts]
-        partners[0] = after(partners[0], tuple(ks) if step == 0 else parts[1])
-        parts = [fold(*pair, signs[step], step, levels) for pair in zip(parts, partners)]
-    last = bits - 1
-    group = lax.axis_size("row") // 2
-    early = gather_chips(parts[0][None], range(last), bits, 0)
-    early = after(early, parts[1])
-    arrived = across(early, last, bits, 0)
-    out = multiply(*ks, [early, exchange(early, [1, 1])], 0, None)
-    late = gather_chips(parts[1][None], range(last), bits, 1, out)
-    out = multiply(*ks, [late, exchange(late, [1, 1])], 2 * group, out)
-    out = multiply(*ks, [arrived, *swapped(arrived, 2)], group, out)
-    arrived = after(across(late, last, bits, 1), out)
-    out = multiply(*ks, [arrived], 3 * group, out)
-    return multiply(*ks, [exchange(arrived, [1, 1])], 3 * group + group // 2, out, True)
+        early, late = [lax.optimization_barrier(part) for part in (early, late)]
+        partners = [partner_of(part, step, levels) for part in (early, late)]
+        partners[0] = after(partners[0], tuple(ks) if step == 0 else late)
+        early = fold(early, partners[0], signs[step], step, levels)
+        late = fold(late, partners[1], signs[step], step, levels)
+    early, late = [lax.optimization_barrier(part[None]) for part in (early, late)]
+    pieces, others = [early], [*swapped(early, 1)]
+    for step in range(bits - 1):
+        pieces.append(across(early, step, bits))
+        others += swapped(pieces[-1], 1)
+        early = jnp.concatenate([early, pieces[-1]])
+    early = after(early, late)
+    first = across(early, bits - 1, bits)
+    pieces = [*itertools.chain(*zip(pieces, others))]
+    out = multiply(*ks, [pieces], 0, None)
+    out = multiply(*ks, [[late, *swapped(late, 1)]], owners, out, weight=0)
+    for step in range(bits - 1):
+        second = after(across(late, step, bits), out)
+        out = multiply(*ks, [[second, *swapped(second, 1)]], owners + (2 << step), out)
+        late = jnp.concatenate([late, second])
+    out = multiply(*ks, [[first, *swapped(first, 2)]], 1 << bits, out)
+    second = after(across(late, bits - 1, bits), out)
+    start = owners + (1 << bits)
+    out = multiply(*ks, [[second]], start, out)
+    return multiply(*ks, [swapped(second, 1)], start + second.shape[0], out, True)
 
 
 def solution(mesh):

time: 55.6 us -> 54.4 us (0.978)
  waiting for transfers between devices: 16.6 us -> 14.7 us
    ppermute x13 -> x15, waiting for transfers between devices: 16.6 us -> 14.7 us  [exchange(): return lax.ppermute(value, AXES, pairs)]
    ppermute x13 -> x15, starting transfers between devices: 15 us -> 15.4 us  [exchange(): return lax.ppermute(value, AXES, pairs)]
    pallas_call x5 -> x6, Pallas kernels: 13.7 us -> 14 us  [multiply(): pl.pallas_call(functools.partial(multiply_kernel, start, [len(of) for of...]
  transfers between devices with their start and end apart: 13 -> 15, of which waited for: 7 -> 7; matrix products, arithmetic and copies ran while one was open for 1% -> 1% of each run, Pallas kernels for 35% -> 37%
where the time goes in v3:
time: 54.4 us; the launch traced here: 54.2 us
  Pallas kernels  22.6 us (42%)
  starting transfers between devices  15.4 us (28%)
  waiting for transfers between devices  14.7 us (27%)
  local copies, waits for them, and re-layouts  1.18 us (2%)
    ppermute x15, starting transfers between devices, exchange(): return lax.ppermute(value, AXES, pairs)  15.4 us
    ppermute x15, waiting for transfers between devices, exchange(): return lax.ppermute(value, AXES, pairs)  14.7 us
    pallas_call x6, Pallas kernels, multiply(): pl.pallas_call(functools.partial(multiply_kernel, start, [len(of) for of...  14 us
    pallas_call x1, Pallas kernels, split(): pl.pallas_call(functools.partial(split_kernel, lax.axis_size('row'), chun...  8.63 us
  transfers between devices with their start and end apart: 15, of which 7 were waited for; matrix products, arithmetic and copies ran while one was open for 1% of the time, Pallas kernels for 37%

profile of v3, /device:TPU:0, one launch (start us, length us, event | category | flops | bytes accessed | tf_op | source)
XLA Modules:
  0.0 54.2 jit_solution(7752385415262512762)
XLA Ops:
  0.0 1.1 %slice_bitcast_fusion = (f32[128,512]{1,0:T(8,128)S(1)}, f32[128,512]{1,0:T(8,128)S(1)}) fusion(f32[1,256,512]{2,1,0:T(8,128)} %param.2), kind=kLoop, calls=%fused_computation.4 | loop fusion | bytes 1048576 | tf_op jit(solution)/shard_map/slice | solution.py:203
  1.1 3.1 %collective-permute-start.4 = (f32[128,512]{1,0:T(8,128)S(1)}, f32[128,512]{1,0:T(8,128)S(1)}, u32[]{:S(2)}, u32[]{:S(2)}) collective-permute-start(f32[128,512]{1,0:T(8,128)S(1)} %get-tuple-element.27), channel_id=1, source_target_pairs={{0,8},{1,17},{2,10},{3,19},{4,12},{5,21},{6,14},{7,23},{8,0},{9,25... | collective-permute-start | bytes 786440 | tf_op jit(solution)/shard_map/ppermute | solution.py:20
  4.2 0.1 collective-permute-start
  4.2 0.1 stack.35.table_ref
  4.3 8.6 %split_reduced_kernel.1 = (bf16[1536,2048]{1,0:T(8,128)(2,1)S(1)}, bf16[1536,2048]{1,0:T(8,128)(2,1)S(1)}) custom-call(s32[8]{0:T(128)S(1)} %stack.35.table_ref, f32[1536,2048]{1,0:T(8,128)} %bitcast.17), custom_call_target="tpu_custom_call" | custom-call | flops 12582912 | bytes 12582912 | tf_op jit(solution)/shard_map/split_reduced_kernel/pallas_call | solution.py:94
  13.0 0.0 collective-permute-done.4
  13.0 3.0 %collective-permute-start.5 = (f32[128,512]{1,0:T(8,128)S(1)}, f32[128,512]{1,0:T(8,128)S(1)}, u32[]{:S(2)}, u32[]{:S(2)}) collective-permute-start(f32[128,512]{1,0:T(8,128)S(1)} %multiply_add_fusion), channel_id=1, source_target_pairs={{0,16},{1,9},{2,18},{3,11},{4,20},{5,13},{6,22},{7,15},{8,24},{9,1... | collective-permute-start | bytes 786440 | tf_op jit(solution)/shard_map/ppermute | solution.py:20
  16.0 0.7 %collective-permute-done = f32[128,512]{1,0:T(8,128)S(1)} collective-permute-done((f32[128,512]{1,0:T(8,128)S(1)}, f32[128,512]{1,0:T(8,128)S(1)}, u32[]{:S(2)}, u32[]{:S(2)}) %collective-permute-start) | collective-permute-done | bytes 262176 | tf_op jit(solution)/shard_map/ppermute | solution.py:20
  16.8 2.6 %collective-permute-start.1 = (f32[128,512]{1,0:T(8,128)S(1)}, f32[128,512]{1,0:T(8,128)S(1)}, u32[]{:S(2)}, u32[]{:S(2)}) collective-permute-start(f32[128,512]{1,0:T(8,128)S(1)} %multiply_add_fusion.1), channel_id=1, source_target_pairs={{0,16},{1,9},{2,18},{3,11},{4,20},{5,13},{6,22},{7,15},{8,24},{9,1... | collective-permute-start | bytes 786440 | tf_op jit(solution)/shard_map/ppermute | solution.py:20
  19.4 3.4 %collective-permute-done.5 = f32[128,512]{1,0:T(8,128)S(1)} collective-permute-done((f32[128,512]{1,0:T(8,128)S(1)}, f32[128,512]{1,0:T(8,128)S(1)}, u32[]{:S(2)}, u32[]{:S(2)}) %collective-permute-start.5) | collective-permute-done | bytes 262176 | tf_op jit(solution)/shard_map/ppermute | solution.py:20
  22.9 1.5 %collective-permute-start.7 = (f32[1,128,512]{2,1,0:T(8,128)S(1)}, f32[1,128,512]{2,1,0:T(8,128)S(1)}, u32[]{:S(2)}, u32[]{:S(2)}) collective-permute-start(f32[1,128,512]{2,1,0:T(8,128)S(1)} %multiply_bitcast_fusion.refs_0_), channel_id=1, source_target_pairs={{0,2},{1,5},{2,0},{3,7},{4,6},{5,1},{6,4},{7,3},{8,10},{9,13},{10,... | collective-permute-start | bytes 786440 | tf_op jit(solution)/shard_map/ppermute | solution.py:20
  24.3 0.0 collective-permute-start.6
  24.3 3.2 %collective-permute-done.1 = f32[128,512]{1,0:T(8,128)S(1)} collective-permute-done((f32[128,512]{1,0:T(8,128)S(1)}, f32[128,512]{1,0:T(8,128)S(1)}, u32[]{:S(2)}, u32[]{:S(2)}) %collective-permute-start.1) | collective-permute-done | bytes 262176 | tf_op jit(solution)/shard_map/ppermute | solution.py:20
  27.6 1.7 %collective-permute-done.7.refs_2_ = f32[1,128,512]{2,1,0:T(8,128)S(1)} collective-permute-done((f32[1,128,512]{2,1,0:T(8,128)S(1)}, f32[1,128,512]{2,1,0:T(8,128)S(1)}, u32[]{:S(2)}, u32[]{:S(2)}) %collective-permute-start.7) | collective-permute-done | bytes 262176 | tf_op jit(solution)/shard_map/ppermute | solution.py:20
  29.3 0.0 collective-permute-start.8
  29.3 1.6 %collective-permute-start.10 = (f32[2,128,512]{2,1,0:T(8,128)S(1)}, f32[2,128,512]{2,1,0:T(8,128)S(1)}, u32[]{:S(2)}, u32[]{:S(2)}) collective-permute-start(f32[2,128,512]{2,1,0:T(8,128)S(1)} %pad_maximum_fusion.1), channel_id=1, source_target_pairs={{0,4},{1,3},{2,6},{3,1},{4,0},{5,7},{6,2},{7,5},{8,12},{9,11},{10,... | collective-permute-start | bytes 1572872 | tf_op jit(solution)/shard_map/ppermute | solution.py:20
  30.9 0.1 collective-permute-start.3
  31.0 1.3 %collective-permute-start.2 = (f32[1,128,512]{2,1,0:T(8,128)S(1)}, f32[1,128,512]{2,1,0:T(8,128)S(1)}, u32[]{:S(2)}, u32[]{:S(2)}) collective-permute-start(f32[1,128,512]{2,1,0:T(8,128)S(1)} %multiply_bitcast_fusion.1.refs_0_), channel_id=1, source_target_pairs={{0,2},{1,5},{2,0},{3,7},{4,6},{5,1},{6,4},{7,3},{8,10},{9,13},{10,... | collective-permute-start | bytes 786440 | tf_op jit(solution)/shard_map/ppermute | solution.py:20
  32.3 0.0 collective-permute-done.6.refs_1_
  32.3 0.0 collective-permute-done.8.refs_3_
  32.3 2.9 %multiply_sources.6.refs_2_ = f32[1536,512]{1,0:T(8,128)S(1)} custom-call(bf16[1536,2048]{1,0:T(8,128)(2,1)S(1)} %get-tuple-element.16.high_ref, bf16[1536,2048]{1,0:T(8,128)(2,1)S(1)} %get-tuple-element.17.low_ref, f32[1,128,512]{2,1,0:T(8,128)S(1)} %multiply_bitcast_fusion.refs_0_, f32[1,128,512]{2,1,0:T(8,128)S(1)} %collective-permute-done.6.refs_1_, ...), custom_call_target="tpu_custom_call" | custom-call | flops 2415919104 | tf_op jit(solution)/shard_map/multiply_sources/pallas_call | solution.py:177
  35.3 0.0 collective-permute-done.3.refs_1_
  35.3 1.7 %multiply_sources.7.refs_2_ = f32[1536,512]{1,0:T(8,128)S(1)} custom-call(bf16[1536,2048]{1,0:T(8,128)(2,1)S(1)} %get-tuple-element.16.high_ref, bf16[1536,2048]{1,0:T(8,128)(2,1)S(1)} %get-tuple-element.17.low_ref, f32[1,128,512]{2,1,0:T(8,128)S(1)} %multiply_bitcast_fusion.1.refs_0_, ...), custom_call_target="tpu_custom_call", output_to_operand_aliasing={{}: (4, {})} | custom-call | tf_op jit(solution)/shard_map/multiply_sources/pallas_call | solution.py:177
  37.0 3.2 %collective-permute-done.2.refs_0_ = f32[1,128,512]{2,1,0:T(8,128)S(1)} collective-permute-done((f32[1,128,512]{2,1,0:T(8,128)S(1)}, f32[1,128,512]{2,1,0:T(8,128)S(1)}, u32[]{:S(2)}, u32[]{:S(2)}) %collective-permute-start.2) | collective-permute-done | bytes 262176 | tf_op jit(solution)/shard_map/ppermute | solution.py:20
  40.3 0.0 collective-permute-start.13
  40.3 1.6 %collective-permute-start.9 = (f32[2,128,512]{2,1,0:T(8,128)S(1)}, f32[2,128,512]{2,1,0:T(8,128)S(1)}, u32[]{:S(2)}, u32[]{:S(2)}) collective-permute-start(f32[2,128,512]{2,1,0:T(8,128)S(1)} %pad_maximum_fusion), channel_id=1, source_target_pairs={{0,4},{1,3},{2,6},{3,1},{4,0},{5,7},{6,2},{7,5},{8,12},{9,11},{10,... | collective-permute-start | bytes 1572872 | tf_op jit(solution)/shard_map/ppermute | solution.py:20
  41.9 0.0 collective-permute-done.10.refs_0_
  41.9 0.1 collective-permute-start.11
  42.0 0.5 collective-permute-start.12
  42.5 0.0 collective-permute-done.13.refs_1_
  42.5 1.7 %multiply_sources.8.refs_3_ = f32[1536,512]{1,0:T(8,128)S(1)} custom-call(bf16[1536,2048]{1,0:T(8,128)(2,1)S(1)} %get-tuple-element.16.high_ref, bf16[1536,2048]{1,0:T(8,128)(2,1)S(1)} %get-tuple-element.17.low_ref, f32[1,128,512]{2,1,0:T(8,128)S(1)} %collective-permute-done.2.refs_0_, ...), custom_call_target="tpu_custom_call", output_to_operand_aliasing={{}: (4, {})} | custom-call | flops 1207959552 | tf_op jit(solution)/shard_map/multiply_sources/pallas_call | solution.py:177
  44.2 0.0 collective-permute-done.11.refs_1_
  44.3 0.0 collective-permute-done.12.refs_2_
  44.3 3.1 %multiply_sources.9.refs_1_ = f32[1536,512]{1,0:T(8,128)S(1)} custom-call(bf16[1536,2048]{1,0:T(8,128)(2,1)S(1)} %get-tuple-element.16.high_ref, bf16[1536,2048]{1,0:T(8,128)(2,1)S(1)} %get-tuple-element.17.low_ref, f32[2,128,512]{2,1,0:T(8,128)S(1)} %collective-permute-done.10.refs_0_, ...), custom_call_target="tpu_custom_call", output_to_operand_aliasing={{}: (5, {})} | custom-call | flops 2415919104 | tf_op jit(solution)/shard_map/multiply_sources/pallas_call | solution.py:177
  47.3 2.2 %collective-permute-done.9.refs_0_ = f32[2,128,512]{2,1,0:T(8,128)S(1)} collective-permute-done((f32[2,128,512]{2,1,0:T(8,128)S(1)}, f32[2,128,512]{2,1,0:T(8,128)S(1)}, u32[]{:S(2)}, u32[]{:S(2)}) %collective-permute-start.9) | collective-permute-done | bytes 524320 | tf_op jit(solution)/shard_map/ppermute | solution.py:20
  49.5 0.0 collective-permute-start.14
  49.5 1.7 %multiply_sources.10.refs_1_ = f32[1536,512]{1,0:T(8,128)S(1)} custom-call(bf16[1536,2048]{1,0:T(8,128)(2,1)S(1)} %get-tuple-element.16.high_ref, bf16[1536,2048]{1,0:T(8,128)(2,1)S(1)} %get-tuple-element.17.low_ref, f32[2,128,512]{2,1,0:T(8,128)S(1)} %collective-permute-done.9.refs_0_, ...), custom_call_target="tpu_custom_call", output_to_operand_aliasing={{}: (3, {})} | custom-call | flops 1207959552 | tf_op jit(solution)/shard_map/multiply_sources/pallas_call | solution.py:177
  51.3 0.2 collective-permute-done.14.refs_0_
  51.5 2.8 %multiply_sources.11 = f32[1,1536,512]{2,1,0:T(8,128)} custom-call(bf16[1536,2048]{1,0:T(8,128)(2,1)S(1)} %get-tuple-element.16.high_ref, bf16[1536,2048]{1,0:T(8,128)(2,1)S(1)} %get-tuple-element.17.low_ref, f32[2,128,512]{2,1,0:T(8,128)S(1)} %collective-permute-done.14.refs_0_, f32[1536,512]{1,0:T(8,128)S(1)} %multiply_sources.10.refs_1_), custom_call_target="tpu_custom_call" | custom-call | flops 1207959552 | tf_op jit(solution)/shard_map/multiply_sources/pallas_call | solution.py:177
  (7 shorter events, 0.3 us)
Async XLA Ops:
  1.1 11.9 %collective-permute-start.4 = (f32[128,512]{1,0:T(8,128)S(1)}, f32[128,512]{1,0:T(8,128)S(1)}, u32[]{:S(2)}, u32[]{:S(2)}) collective-permute-start(f32[128,512]{1,0:T(8,128)S(1)} %get-tuple-element.27), channel_id=1, source_target_pairs={{0,8},{1,17},{2,10},{3,19},{4,12},{5,21},{6,14},{7,23},{8,0},{9,25... | collective-permute-start | bytes 786440 | tf_op jit(solution)/shard_map/ppermute | solution.py:20
  4.2 12.6 %collective-permute-start = (f32[128,512]{1,0:T(8,128)S(1)}, f32[128,512]{1,0:T(8,128)S(1)}, u32[]{:S(2)}, u32[]{:S(2)}) collective-permute-start(f32[128,512]{1,0:T(8,128)S(1)} %get-tuple-element.28), channel_id=1, source_target_pairs={{0,8},{1,17},{2,10},{3,19},{4,12},{5,21},{6,14},{7,23},{8,0},{9,25... | collective-permute-start | bytes 786440 | tf_op jit(solution)/shard_map/ppermute | solution.py:20
  13.0 9.8 %collective-permute-start.5 = (f32[128,512]{1,0:T(8,128)S(1)}, f32[128,512]{1,0:T(8,128)S(1)}, u32[]{:S(2)}, u32[]{:S(2)}) collective-permute-start(f32[128,512]{1,0:T(8,128)S(1)} %multiply_add_fusion), channel_id=1, source_target_pairs={{0,16},{1,9},{2,18},{3,11},{4,20},{5,13},{6,22},{7,15},{8,24},{9,1... | collective-permute-start | bytes 786440 | tf_op jit(solution)/shard_map/ppermute | solution.py:20
  16.8 10.8 %collective-permute-start.1 = (f32[128,512]{1,0:T(8,128)S(1)}, f32[128,512]{1,0:T(8,128)S(1)}, u32[]{:S(2)}, u32[]{:S(2)}) collective-permute-start(f32[128,512]{1,0:T(8,128)S(1)} %multiply_add_fusion.1), channel_id=1, source_target_pairs={{0,16},{1,9},{2,18},{3,11},{4,20},{5,13},{6,22},{7,15},{8,24},{9,1... | collective-permute-start | bytes 786440 | tf_op jit(solution)/shard_map/ppermute | solution.py:20
  22.9 6.4 %collective-permute-start.7 = (f32[1,128,512]{2,1,0:T(8,128)S(1)}, f32[1,128,512]{2,1,0:T(8,128)S(1)}, u32[]{:S(2)}, u32[]{:S(2)}) collective-permute-start(f32[1,128,512]{2,1,0:T(8,128)S(1)} %multiply_bitcast_fusion.refs_0_), channel_id=1, source_target_pairs={{0,2},{1,5},{2,0},{3,7},{4,6},{5,1},{6,4},{7,3},{8,10},{9,13},{10,... | collective-permute-start | bytes 786440 | tf_op jit(solution)/shard_map/ppermute | solution.py:20
  24.3 8.0 %collective-permute-start.6 = (f32[1,128,512]{2,1,0:T(8,128)S(1)}, f32[1,128,512]{2,1,0:T(8,128)S(1)}, u32[]{:S(2)}, u32[]{:S(2)}) collective-permute-start(f32[1,128,512]{2,1,0:T(8,128)S(1)} %multiply_bitcast_fusion.refs_0_), channel_id=1, source_target_pairs={{0,1},{1,0},{2,3},{3,2},{4,5},{5,4},{6,7},{7,6},{8,9},{9,8},{10,11... | collective-permute-start | bytes 786440 | tf_op jit(solution)/shard_map/ppermute | solution.py:20
  29.3 3.0 %collective-permute-start.8 = (f32[1,128,512]{2,1,0:T(8,128)S(1)}, f32[1,128,512]{2,1,0:T(8,128)S(1)}, u32[]{:S(2)}, u32[]{:S(2)}) collective-permute-start(f32[1,128,512]{2,1,0:T(8,128)S(1)} %collective-permute-done.7.refs_2_), channel_id=1, source_target_pairs={{0,1},{1,0},{2,3},{3,2},{4,5},{5,4},{6,7},{7,6},{8,9},{9,8},{10,11... | collective-permute-start | bytes 786440 | tf_op jit(solution)/shard_map/ppermute | solution.py:20
  29.3 12.6 %collective-permute-start.10 = (f32[2,128,512]{2,1,0:T(8,128)S(1)}, f32[2,128,512]{2,1,0:T(8,128)S(1)}, u32[]{:S(2)}, u32[]{:S(2)}) collective-permute-start(f32[2,128,512]{2,1,0:T(8,128)S(1)} %pad_maximum_fusion.1), channel_id=1, source_target_pairs={{0,4},{1,3},{2,6},{3,1},{4,0},{5,7},{6,2},{7,5},{8,12},{9,11},{10,... | collective-permute-start | bytes 1572872 | tf_op jit(solution)/shard_map/ppermute | solution.py:20
  30.9 4.3 %collective-permute-start.3 = (f32[1,128,512]{2,1,0:T(8,128)S(1)}, f32[1,128,512]{2,1,0:T(8,128)S(1)}, u32[]{:S(2)}, u32[]{:S(2)}) collective-permute-start(f32[1,128,512]{2,1,0:T(8,128)S(1)} %multiply_bitcast_fusion.1.refs_0_), channel_id=1, source_target_pairs={{0,1},{1,0},{2,3},{3,2},{4,5},{5,4},{6,7},{7,6},{8,9},{9,8},{10,11... | collective-permute-start | bytes 786440 | tf_op jit(solution)/shard_map/ppermute | solution.py:20
  31.0 9.2 %collective-permute-start.2 = (f32[1,128,512]{2,1,0:T(8,128)S(1)}, f32[1,128,512]{2,1,0:T(8,128)S(1)}, u32[]{:S(2)}, u32[]{:S(2)}) collective-permute-start(f32[1,128,512]{2,1,0:T(8,128)S(1)} %multiply_bitcast_fusion.1.refs_0_), channel_id=1, source_target_pairs={{0,2},{1,5},{2,0},{3,7},{4,6},{5,1},{6,4},{7,3},{8,10},{9,13},{10,... | collective-permute-start | bytes 786440 | tf_op jit(solution)/shard_map/ppermute | solution.py:20
  40.3 2.2 %collective-permute-start.13 = (f32[1,128,512]{2,1,0:T(8,128)S(1)}, f32[1,128,512]{2,1,0:T(8,128)S(1)}, u32[]{:S(2)}, u32[]{:S(2)}) collective-permute-start(f32[1,128,512]{2,1,0:T(8,128)S(1)} %collective-permute-done.2.refs_0_), channel_id=1, source_target_pairs={{0,1},{1,0},{2,3},{3,2},{4,5},{5,4},{6,7},{7,6},{8,9},{9,8},{10,11... | collective-permute-start | bytes 786440 | tf_op jit(solution)/shard_map/ppermute | solution.py:20
  40.3 9.2 %collective-permute-start.9 = (f32[2,128,512]{2,1,0:T(8,128)S(1)}, f32[2,128,512]{2,1,0:T(8,128)S(1)}, u32[]{:S(2)}, u32[]{:S(2)}) collective-permute-start(f32[2,128,512]{2,1,0:T(8,128)S(1)} %pad_maximum_fusion), channel_id=1, source_target_pairs={{0,4},{1,3},{2,6},{3,1},{4,0},{5,7},{6,2},{7,5},{8,12},{9,11},{10,... | collective-permute-start | bytes 1572872 | tf_op jit(solution)/shard_map/ppermute | solution.py:20
  41.9 2.3 %collective-permute-start.11 = (f32[1,128,512]{2,1,0:T(8,128)S(1)}, f32[1,128,512]{2,1,0:T(8,128)S(1)}, u32[]{:S(2)}, u32[]{:S(2)}) collective-permute-start(f32[1,128,512]{2,1,0:T(8,128)S(1)} %get-tuple-element.26), channel_id=1, source_target_pairs={{0,1},{1,0},{2,3},{3,2},{4,5},{5,4},{6,7},{7,6},{8,9},{9,8},{10,11... | collective-permute-start | bytes 786440 | tf_op jit(solution)/shard_map/ppermute | solution.py:20
  42.0 2.2 %collective-permute-start.12 = (f32[1,128,512]{2,1,0:T(8,128)S(1)}, f32[1,128,512]{2,1,0:T(8,128)S(1)}, u32[]{:S(2)}, u32[]{:S(2)}) collective-permute-start(f32[1,128,512]{2,1,0:T(8,128)S(1)} %get-tuple-element.25), channel_id=1, source_target_pairs={{0,1},{1,0},{2,3},{3,2},{4,5},{5,4},{6,7},{7,6},{8,9},{9,8},{10,11... | collective-permute-start | bytes 786440 | tf_op jit(solution)/shard_map/ppermute | solution.py:20
  49.5 1.9 %collective-permute-start.14 = (f32[2,128,512]{2,1,0:T(8,128)S(1)}, f32[2,128,512]{2,1,0:T(8,128)S(1)}, u32[]{:S(2)}, u32[]{:S(2)}) collective-permute-start(f32[2,128,512]{2,1,0:T(8,128)S(1)} %collective-permute-done.9.refs_0_), channel_id=1, source_target_pairs={{0,1},{1,0},{2,3},{3,2},{4,5},{5,4},{6,7},{7,6},{8,9},{9,8},{10,11... | collective-permute-start | bytes 1572872 | tf_op jit(solution)/shard_map/ppermute | solution.py:20

commit v4 on v3

--- a/solution.py
+++ b/solution.py
@@ -211,13 +211,12 @@
     early, late = [lax.optimization_barrier(part[None]) for part in (early, late)]
     pieces, others = [early], [*swapped(early, 1)]
     for step in range(bits - 1):
-        pieces.append(across(early, step, bits))
+        pieces.append(after(across(early, step, bits), late))
         others += swapped(pieces[-1], 1)
         early = jnp.concatenate([early, pieces[-1]])
-    early = after(early, late)
     first = across(early, bits - 1, bits)
     pieces = [*itertools.chain(*zip(pieces, others))]
-    out = multiply(*ks, [pieces], 0, None)
+    out = multiply(*ks, [pieces], 0, None, weight=12)
     out = multiply(*ks, [[late, *swapped(late, 1)]], owners, out, weight=0)
     for step in range(bits - 1):
         second = after(across(late, step, bits), out)

time: 54.4 us -> 53 us (0.974)
  waiting for transfers between devices: 14.7 us -> 12 us
  starting transfers between devices: 15.4 us -> 16.5 us
    ppermute x15, waiting for transfers between devices: 14.7 us -> 12 us  [exchange(): return lax.ppermute(value, AXES, pairs)]
    ppermute x15, starting transfers between devices: 15.4 us -> 16.5 us  [exchange(): return lax.ppermute(value, AXES, pairs)]
  transfers between devices with their start and end apart: 15 -> 15, of which waited for: 7 -> 8; matrix products, arithmetic and copies ran while one was open for 1% -> 1% of each run, Pallas kernels for 37% -> 38%
where the time goes in v4:
time: 53 us; the launch traced here: 52.7 us
  Pallas kernels  22.6 us (43%)
  starting transfers between devices  16.5 us (31%)
  waiting for transfers between devices  12 us (23%)
  local copies, waits for them, and re-layouts  1.18 us (2%)
    ppermute x15, starting transfers between devices, exchange(): return lax.ppermute(value, AXES, pairs)  16.5 us
    pallas_call x6, Pallas kernels, multiply(): pl.pallas_call(functools.partial(multiply_kernel, start, [len(of) for of...  14 us
    ppermute x15, waiting for transfers between devices, exchange(): return lax.ppermute(value, AXES, pairs)  12 us
    pallas_call x1, Pallas kernels, split(): pl.pallas_call(functools.partial(split_kernel, lax.axis_size('row'), chun...  8.63 us
    slice x1, local copies, waits for them, and re-layouts, body(): early, late = (mine[:half], mine[half:])  1.06 us
  transfers between devices with their start and end apart: 15, of which 8 were waited for; matrix products, arithmetic and copies ran while one was open for 1% of the time, Pallas kernels for 38%

profile of v4, /device:TPU:0, one launch (start us, length us, event | category | flops | bytes accessed | tf_op | source)
XLA Modules:
  0.0 52.7 jit_solution(131516880860949926)
XLA Ops:
  0.0 1.1 %slice_bitcast_fusion = (f32[128,512]{1,0:T(8,128)S(1)}, f32[128,512]{1,0:T(8,128)S(1)}) fusion(f32[1,256,512]{2,1,0:T(8,128)} %param.2), kind=kLoop, calls=%fused_computation.4 | loop fusion | bytes 1048576 | tf_op jit(solution)/shard_map/slice | solution.py:203
  1.1 3.1 %collective-permute-start.4 = (f32[128,512]{1,0:T(8,128)S(1)}, f32[128,512]{1,0:T(8,128)S(1)}, u32[]{:S(2)}, u32[]{:S(2)}) collective-permute-start(f32[128,512]{1,0:T(8,128)S(1)} %get-tuple-element.27), channel_id=1, source_target_pairs={{0,8},{1,17},{2,10},{3,19},{4,12},{5,21},{6,14},{7,23},{8,0},{9,25... | collective-permute-start | bytes 786440 | tf_op jit(solution)/shard_map/ppermute | solution.py:20
  4.2 0.1 collective-permute-start
  4.2 0.1 stack.35.table_ref
  4.3 8.6 %split_reduced_kernel.1 = (bf16[1536,2048]{1,0:T(8,128)(2,1)S(1)}, bf16[1536,2048]{1,0:T(8,128)(2,1)S(1)}) custom-call(s32[8]{0:T(128)S(1)} %stack.35.table_ref, f32[1536,2048]{1,0:T(8,128)} %bitcast.17), custom_call_target="tpu_custom_call" | custom-call | flops 12582912 | bytes 12582912 | tf_op jit(solution)/shard_map/split_reduced_kernel/pallas_call | solution.py:94
  13.0 0.0 collective-permute-done.4
  13.0 3.0 %collective-permute-start.5 = (f32[128,512]{1,0:T(8,128)S(1)}, f32[128,512]{1,0:T(8,128)S(1)}, u32[]{:S(2)}, u32[]{:S(2)}) collective-permute-start(f32[128,512]{1,0:T(8,128)S(1)} %multiply_add_fusion), channel_id=1, source_target_pairs={{0,16},{1,9},{2,18},{3,11},{4,20},{5,13},{6,22},{7,15},{8,24},{9,1... | collective-permute-start | bytes 786440 | tf_op jit(solution)/shard_map/ppermute | solution.py:20
  16.0 0.7 %collective-permute-done = f32[128,512]{1,0:T(8,128)S(1)} collective-permute-done((f32[128,512]{1,0:T(8,128)S(1)}, f32[128,512]{1,0:T(8,128)S(1)}, u32[]{:S(2)}, u32[]{:S(2)}) %collective-permute-start) | collective-permute-done | bytes 262176 | tf_op jit(solution)/shard_map/ppermute | solution.py:20
  16.8 2.6 %collective-permute-start.1 = (f32[128,512]{1,0:T(8,128)S(1)}, f32[128,512]{1,0:T(8,128)S(1)}, u32[]{:S(2)}, u32[]{:S(2)}) collective-permute-start(f32[128,512]{1,0:T(8,128)S(1)} %multiply_add_fusion.1), channel_id=1, source_target_pairs={{0,16},{1,9},{2,18},{3,11},{4,20},{5,13},{6,22},{7,15},{8,24},{9,1... | collective-permute-start | bytes 786440 | tf_op jit(solution)/shard_map/ppermute | solution.py:20
  19.4 3.4 %collective-permute-done.5 = f32[128,512]{1,0:T(8,128)S(1)} collective-permute-done((f32[128,512]{1,0:T(8,128)S(1)}, f32[128,512]{1,0:T(8,128)S(1)}, u32[]{:S(2)}, u32[]{:S(2)}) %collective-permute-start.5) | collective-permute-done | bytes 262176 | tf_op jit(solution)/shard_map/ppermute | solution.py:20
  22.9 1.5 %collective-permute-start.7 = (f32[1,128,512]{2,1,0:T(8,128)S(1)}, f32[1,128,512]{2,1,0:T(8,128)S(1)}, u32[]{:S(2)}, u32[]{:S(2)}) collective-permute-start(f32[1,128,512]{2,1,0:T(8,128)S(1)} %multiply_bitcast_fusion.refs_0_), channel_id=1, source_target_pairs={{0,2},{1,5},{2,0},{3,7},{4,6},{5,1},{6,4},{7,3},{8,10},{9,13},{10,... | collective-permute-start | bytes 786440 | tf_op jit(solution)/shard_map/ppermute | solution.py:20
  24.3 0.0 collective-permute-start.6
  24.3 3.2 %collective-permute-done.1 = f32[128,512]{1,0:T(8,128)S(1)} collective-permute-done((f32[128,512]{1,0:T(8,128)S(1)}, f32[128,512]{1,0:T(8,128)S(1)}, u32[]{:S(2)}, u32[]{:S(2)}) %collective-permute-start.1) | collective-permute-done | bytes 262176 | tf_op jit(solution)/shard_map/ppermute | solution.py:20
  27.6 1.7 %collective-permute-done.7.refs_2_ = f32[1,128,512]{2,1,0:T(8,128)S(1)} collective-permute-done((f32[1,128,512]{2,1,0:T(8,128)S(1)}, f32[1,128,512]{2,1,0:T(8,128)S(1)}, u32[]{:S(2)}, u32[]{:S(2)}) %collective-permute-start.7) | collective-permute-done | bytes 262176 | tf_op jit(solution)/shard_map/ppermute | solution.py:20
  29.3 0.0 collective-permute-start.8
  29.3 0.5 collective-permute-start.3
  29.8 1.4 %collective-permute-start.2 = (f32[1,128,512]{2,1,0:T(8,128)S(1)}, f32[1,128,512]{2,1,0:T(8,128)S(1)}, u32[]{:S(2)}, u32[]{:S(2)}) collective-permute-start(f32[1,128,512]{2,1,0:T(8,128)S(1)} %multiply_bitcast_fusion.1.refs_0_), channel_id=1, source_target_pairs={{0,2},{1,5},{2,0},{3,7},{4,6},{5,1},{6,4},{7,3},{8,10},{9,13},{10,... | collective-permute-start | bytes 786440 | tf_op jit(solution)/shard_map/ppermute | solution.py:20
  31.2 1.6 %collective-permute-start.10 = (f32[2,128,512]{2,1,0:T(8,128)S(1)}, f32[2,128,512]{2,1,0:T(8,128)S(1)}, u32[]{:S(2)}, u32[]{:S(2)}) collective-permute-start(f32[2,128,512]{2,1,0:T(8,128)S(1)} %pad_maximum_fusion.1), channel_id=1, source_target_pairs={{0,4},{1,3},{2,6},{3,1},{4,0},{5,7},{6,2},{7,5},{8,12},{9,11},{10,... | collective-permute-start | bytes 1572872 | tf_op jit(solution)/shard_map/ppermute | solution.py:20
  32.8 0.0 collective-permute-done.6.refs_1_
  32.8 0.0 collective-permute-done.8.refs_3_
  32.8 2.9 %multiply_sources.6.refs_2_ = f32[1536,512]{1,0:T(8,128)S(1)} custom-call(bf16[1536,2048]{1,0:T(8,128)(2,1)S(1)} %get-tuple-element.16.high_ref, bf16[1536,2048]{1,0:T(8,128)(2,1)S(1)} %get-tuple-element.17.low_ref, f32[1,128,512]{2,1,0:T(8,128)S(1)} %multiply_bitcast_fusion.refs_0_, f32[1,128,512]{2,1,0:T(8,128)S(1)} %collective-permute-done.6.refs_1_, ...), custom_call_target="tpu_custom_call" | custom-call | flops 4831838208 | tf_op jit(solution)/shard_map/multiply_sources/pallas_call | solution.py:177
  35.8 0.0 collective-permute-done.3.refs_1_
  35.8 1.7 %multiply_sources.7.refs_2_ = f32[1536,512]{1,0:T(8,128)S(1)} custom-call(bf16[1536,2048]{1,0:T(8,128)(2,1)S(1)} %get-tuple-element.16.high_ref, bf16[1536,2048]{1,0:T(8,128)(2,1)S(1)} %get-tuple-element.17.low_ref, f32[1,128,512]{2,1,0:T(8,128)S(1)} %multiply_bitcast_fusion.1.refs_0_, ...), custom_call_target="tpu_custom_call", output_to_operand_aliasing={{}: (4, {})} | custom-call | tf_op jit(solution)/shard_map/multiply_sources/pallas_call | solution.py:177
  37.5 1.2 %collective-permute-done.2.refs_0_ = f32[1,128,512]{2,1,0:T(8,128)S(1)} collective-permute-done((f32[1,128,512]{2,1,0:T(8,128)S(1)}, f32[1,128,512]{2,1,0:T(8,128)S(1)}, u32[]{:S(2)}, u32[]{:S(2)}) %collective-permute-start.2) | collective-permute-done | bytes 262176 | tf_op jit(solution)/shard_map/ppermute | solution.py:20
  38.7 0.0 collective-permute-start.13
  38.7 1.8 %collective-permute-start.9 = (f32[2,128,512]{2,1,0:T(8,128)S(1)}, f32[2,128,512]{2,1,0:T(8,128)S(1)}, u32[]{:S(2)}, u32[]{:S(2)}) collective-permute-start(f32[2,128,512]{2,1,0:T(8,128)S(1)} %pad_maximum_fusion), channel_id=1, source_target_pairs={{0,4},{1,3},{2,6},{3,1},{4,0},{5,7},{6,2},{7,5},{8,12},{9,11},{10,... | collective-permute-start | bytes 1572872 | tf_op jit(solution)/shard_map/ppermute | solution.py:20
  40.6 0.3 collective-permute-done.10.refs_0_
  40.9 0.9 %collective-permute-start.11 = (f32[1,128,512]{2,1,0:T(8,128)S(1)}, f32[1,128,512]{2,1,0:T(8,128)S(1)}, u32[]{:S(2)}, u32[]{:S(2)}) collective-permute-start(f32[1,128,512]{2,1,0:T(8,128)S(1)} %get-tuple-element.26), channel_id=1, source_target_pairs={{0,1},{1,0},{2,3},{3,2},{4,5},{5,4},{6,7},{7,6},{8,9},{9,8},{10,11... | collective-permute-start | bytes 786440 | tf_op jit(solution)/shard_map/ppermute | solution.py:20
  41.7 0.1 collective-permute-start.12
  41.8 0.0 collective-permute-done.13.refs_1_
  41.8 1.7 %multiply_sources.8.refs_3_ = f32[1536,512]{1,0:T(8,128)S(1)} custom-call(bf16[1536,2048]{1,0:T(8,128)(2,1)S(1)} %get-tuple-element.16.high_ref, bf16[1536,2048]{1,0:T(8,128)(2,1)S(1)} %get-tuple-element.17.low_ref, f32[1,128,512]{2,1,0:T(8,128)S(1)} %collective-permute-done.2.refs_0_, ...), custom_call_target="tpu_custom_call", output_to_operand_aliasing={{}: (4, {})} | custom-call | flops 1207959552 | tf_op jit(solution)/shard_map/multiply_sources/pallas_call | solution.py:177
  43.5 0.0 collective-permute-done.11.refs_1_
  43.5 0.0 collective-permute-done.12.refs_2_
  43.6 3.1 %multiply_sources.9.refs_1_ = f32[1536,512]{1,0:T(8,128)S(1)} custom-call(bf16[1536,2048]{1,0:T(8,128)(2,1)S(1)} %get-tuple-element.16.high_ref, bf16[1536,2048]{1,0:T(8,128)(2,1)S(1)} %get-tuple-element.17.low_ref, f32[2,128,512]{2,1,0:T(8,128)S(1)} %collective-permute-done.10.refs_0_, ...), custom_call_target="tpu_custom_call", output_to_operand_aliasing={{}: (5, {})} | custom-call | flops 2415919104 | tf_op jit(solution)/shard_map/multiply_sources/pallas_call | solution.py:177
  46.6 1.4 %collective-permute-done.9.refs_0_ = f32[2,128,512]{2,1,0:T(8,128)S(1)} collective-permute-done((f32[2,128,512]{2,1,0:T(8,128)S(1)}, f32[2,128,512]{2,1,0:T(8,128)S(1)}, u32[]{:S(2)}, u32[]{:S(2)}) %collective-permute-start.9) | collective-permute-done | bytes 524320 | tf_op jit(solution)/shard_map/ppermute | solution.py:20
  48.0 0.0 collective-permute-start.14
  48.0 1.7 %multiply_sources.10.refs_1_ = f32[1536,512]{1,0:T(8,128)S(1)} custom-call(bf16[1536,2048]{1,0:T(8,128)(2,1)S(1)} %get-tuple-element.16.high_ref, bf16[1536,2048]{1,0:T(8,128)(2,1)S(1)} %get-tuple-element.17.low_ref, f32[2,128,512]{2,1,0:T(8,128)S(1)} %collective-permute-done.9.refs_0_, ...), custom_call_target="tpu_custom_call", output_to_operand_aliasing={{}: (3, {})} | custom-call | flops 1207959552 | tf_op jit(solution)/shard_map/multiply_sources/pallas_call | solution.py:177
  49.7 0.2 collective-permute-done.14.refs_0_
  49.9 2.8 %multiply_sources.11 = f32[1,1536,512]{2,1,0:T(8,128)} custom-call(bf16[1536,2048]{1,0:T(8,128)(2,1)S(1)} %get-tuple-element.16.high_ref, bf16[1536,2048]{1,0:T(8,128)(2,1)S(1)} %get-tuple-element.17.low_ref, f32[2,128,512]{2,1,0:T(8,128)S(1)} %collective-permute-done.14.refs_0_, f32[1536,512]{1,0:T(8,128)S(1)} %multiply_sources.10.refs_1_), custom_call_target="tpu_custom_call" | custom-call | flops 1207959552 | tf_op jit(solution)/shard_map/multiply_sources/pallas_call | solution.py:177
  (7 shorter events, 0.3 us)
Async XLA Ops:
  1.1 11.9 %collective-permute-start.4 = (f32[128,512]{1,0:T(8,128)S(1)}, f32[128,512]{1,0:T(8,128)S(1)}, u32[]{:S(2)}, u32[]{:S(2)}) collective-permute-start(f32[128,512]{1,0:T(8,128)S(1)} %get-tuple-element.27), channel_id=1, source_target_pairs={{0,8},{1,17},{2,10},{3,19},{4,12},{5,21},{6,14},{7,23},{8,0},{9,25... | collective-permute-start | bytes 786440 | tf_op jit(solution)/shard_map/ppermute | solution.py:20
  4.2 12.6 %collective-permute-start = (f32[128,512]{1,0:T(8,128)S(1)}, f32[128,512]{1,0:T(8,128)S(1)}, u32[]{:S(2)}, u32[]{:S(2)}) collective-permute-start(f32[128,512]{1,0:T(8,128)S(1)} %get-tuple-element.28), channel_id=1, source_target_pairs={{0,8},{1,17},{2,10},{3,19},{4,12},{5,21},{6,14},{7,23},{8,0},{9,25... | collective-permute-start | bytes 786440 | tf_op jit(solution)/shard_map/ppermute | solution.py:20
  13.0 9.8 %collective-permute-start.5 = (f32[128,512]{1,0:T(8,128)S(1)}, f32[128,512]{1,0:T(8,128)S(1)}, u32[]{:S(2)}, u32[]{:S(2)}) collective-permute-start(f32[128,512]{1,0:T(8,128)S(1)} %multiply_add_fusion), channel_id=1, source_target_pairs={{0,16},{1,9},{2,18},{3,11},{4,20},{5,13},{6,22},{7,15},{8,24},{9,1... | collective-permute-start | bytes 786440 | tf_op jit(solution)/shard_map/ppermute | solution.py:20
  16.8 10.8 %collective-permute-start.1 = (f32[128,512]{1,0:T(8,128)S(1)}, f32[128,512]{1,0:T(8,128)S(1)}, u32[]{:S(2)}, u32[]{:S(2)}) collective-permute-start(f32[128,512]{1,0:T(8,128)S(1)} %multiply_add_fusion.1), channel_id=1, source_target_pairs={{0,16},{1,9},{2,18},{3,11},{4,20},{5,13},{6,22},{7,15},{8,24},{9,1... | collective-permute-start | bytes 786440 | tf_op jit(solution)/shard_map/ppermute | solution.py:20
  22.9 6.4 %collective-permute-start.7 = (f32[1,128,512]{2,1,0:T(8,128)S(1)}, f32[1,128,512]{2,1,0:T(8,128)S(1)}, u32[]{:S(2)}, u32[]{:S(2)}) collective-permute-start(f32[1,128,512]{2,1,0:T(8,128)S(1)} %multiply_bitcast_fusion.refs_0_), channel_id=1, source_target_pairs={{0,2},{1,5},{2,0},{3,7},{4,6},{5,1},{6,4},{7,3},{8,10},{9,13},{10,... | collective-permute-start | bytes 786440 | tf_op jit(solution)/shard_map/ppermute | solution.py:20
  24.3 8.5 %collective-permute-start.6 = (f32[1,128,512]{2,1,0:T(8,128)S(1)}, f32[1,128,512]{2,1,0:T(8,128)S(1)}, u32[]{:S(2)}, u32[]{:S(2)}) collective-permute-start(f32[1,128,512]{2,1,0:T(8,128)S(1)} %multiply_bitcast_fusion.refs_0_), channel_id=1, source_target_pairs={{0,1},{1,0},{2,3},{3,2},{4,5},{5,4},{6,7},{7,6},{8,9},{9,8},{10,11... | collective-permute-start | bytes 786440 | tf_op jit(solution)/shard_map/ppermute | solution.py:20
  29.3 3.5 %collective-permute-start.8 = (f32[1,128,512]{2,1,0:T(8,128)S(1)}, f32[1,128,512]{2,1,0:T(8,128)S(1)}, u32[]{:S(2)}, u32[]{:S(2)}) collective-permute-start(f32[1,128,512]{2,1,0:T(8,128)S(1)} %collective-permute-done.7.refs_2_), channel_id=1, source_target_pairs={{0,1},{1,0},{2,3},{3,2},{4,5},{5,4},{6,7},{7,6},{8,9},{9,8},{10,11... | collective-permute-start | bytes 786440 | tf_op jit(solution)/shard_map/ppermute | solution.py:20
  29.3 6.5 %collective-permute-start.3 = (f32[1,128,512]{2,1,0:T(8,128)S(1)}, f32[1,128,512]{2,1,0:T(8,128)S(1)}, u32[]{:S(2)}, u32[]{:S(2)}) collective-permute-start(f32[1,128,512]{2,1,0:T(8,128)S(1)} %multiply_bitcast_fusion.1.refs_0_), channel_id=1, source_target_pairs={{0,1},{1,0},{2,3},{3,2},{4,5},{5,4},{6,7},{7,6},{8,9},{9,8},{10,11... | collective-permute-start | bytes 786440 | tf_op jit(solution)/shard_map/ppermute | solution.py:20
  29.8 8.9 %collective-permute-start.2 = (f32[1,128,512]{2,1,0:T(8,128)S(1)}, f32[1,128,512]{2,1,0:T(8,128)S(1)}, u32[]{:S(2)}, u32[]{:S(2)}) collective-permute-start(f32[1,128,512]{2,1,0:T(8,128)S(1)} %multiply_bitcast_fusion.1.refs_0_), channel_id=1, source_target_pairs={{0,2},{1,5},{2,0},{3,7},{4,6},{5,1},{6,4},{7,3},{8,10},{9,13},{10,... | collective-permute-start | bytes 786440 | tf_op jit(solution)/shard_map/ppermute | solution.py:20
  31.2 9.6 %collective-permute-start.10 = (f32[2,128,512]{2,1,0:T(8,128)S(1)}, f32[2,128,512]{2,1,0:T(8,128)S(1)}, u32[]{:S(2)}, u32[]{:S(2)}) collective-permute-start(f32[2,128,512]{2,1,0:T(8,128)S(1)} %pad_maximum_fusion.1), channel_id=1, source_target_pairs={{0,4},{1,3},{2,6},{3,1},{4,0},{5,7},{6,2},{7,5},{8,12},{9,11},{10,... | collective-permute-start | bytes 1572872 | tf_op jit(solution)/shard_map/ppermute | solution.py:20
  38.7 3.1 %collective-permute-start.13 = (f32[1,128,512]{2,1,0:T(8,128)S(1)}, f32[1,128,512]{2,1,0:T(8,128)S(1)}, u32[]{:S(2)}, u32[]{:S(2)}) collective-permute-start(f32[1,128,512]{2,1,0:T(8,128)S(1)} %collective-permute-done.2.refs_0_), channel_id=1, source_target_pairs={{0,1},{1,0},{2,3},{3,2},{4,5},{5,4},{6,7},{7,6},{8,9},{9,8},{10,11... | collective-permute-start | bytes 786440 | tf_op jit(solution)/shard_map/ppermute | solution.py:20
  38.7 9.2 %collective-permute-start.9 = (f32[2,128,512]{2,1,0:T(8,128)S(1)}, f32[2,128,512]{2,1,0:T(8,128)S(1)}, u32[]{:S(2)}, u32[]{:S(2)}) collective-permute-start(f32[2,128,512]{2,1,0:T(8,128)S(1)} %pad_maximum_fusion), channel_id=1, source_target_pairs={{0,4},{1,3},{2,6},{3,1},{4,0},{5,7},{6,2},{7,5},{8,12},{9,11},{10,... | collective-permute-start | bytes 1572872 | tf_op jit(solution)/shard_map/ppermute | solution.py:20
  40.9 2.7 %collective-permute-start.11 = (f32[1,128,512]{2,1,0:T(8,128)S(1)}, f32[1,128,512]{2,1,0:T(8,128)S(1)}, u32[]{:S(2)}, u32[]{:S(2)}) collective-permute-start(f32[1,128,512]{2,1,0:T(8,128)S(1)} %get-tuple-element.26), channel_id=1, source_target_pairs={{0,1},{1,0},{2,3},{3,2},{4,5},{5,4},{6,7},{7,6},{8,9},{9,8},{10,11... | collective-permute-start | bytes 786440 | tf_op jit(solution)/shard_map/ppermute | solution.py:20
  41.7 1.8 %collective-permute-start.12 = (f32[1,128,512]{2,1,0:T(8,128)S(1)}, f32[1,128,512]{2,1,0:T(8,128)S(1)}, u32[]{:S(2)}, u32[]{:S(2)}) collective-permute-start(f32[1,128,512]{2,1,0:T(8,128)S(1)} %get-tuple-element.25), channel_id=1, source_target_pairs={{0,1},{1,0},{2,3},{3,2},{4,5},{5,4},{6,7},{7,6},{8,9},{9,8},{10,11... | collective-permute-start | bytes 786440 | tf_op jit(solution)/shard_map/ppermute | solution.py:20
  48.0 1.9 %collective-permute-start.14 = (f32[2,128,512]{2,1,0:T(8,128)S(1)}, f32[2,128,512]{2,1,0:T(8,128)S(1)}, u32[]{:S(2)}, u32[]{:S(2)}) collective-permute-start(f32[2,128,512]{2,1,0:T(8,128)S(1)} %collective-permute-done.9.refs_0_), channel_id=1, source_target_pairs={{0,1},{1,0},{2,3},{3,2},{4,5},{5,4},{6,7},{7,6},{8,9},{9,8},{10,11... | collective-permute-start | bytes 1572872 | tf_op jit(solution)/shard_map/ppermute | solution.py:20

commit v5 on v4

--- a/solution.py
+++ b/solution.py
@@ -11,7 +11,8 @@
 
 HALF = jnp.bfloat16
 AXES = ("irrep", "row")
-TILES = (2, 2)
+TILES = (2, 3)
+COPIES = 4
 
 
 def exchange(value, masks):
@@ -145,19 +146,24 @@
     else:
         result, sems = refs[3:]
 
-        def copy(here, step):
+        size = tile // COPIES
+
+        def copy(number):
+            here = pl.ds(pl.multiple_of(number * size, size), size)
             return pltpu.make_async_copy(
-                result.at[here, :], out_ref.at[0, here, :], sems.at[step]
+                result.at[here, :], out_ref.at[0, here, :], sems.at[number]
             )
 
         @pl.loop(0, tiles)
         def _(step):
             here, total = product(step)
             result[here, :] = total
-            copy(here, step).start()
-
-        for step in range(tiles):
-            copy(slice(step * tile, (step + 1) * tile), step).wait()
+            for part in range(COPIES):
+                number = step * COPIES + part
+                copy(number).start()
+
+        for number in range(tiles * COPIES):
+            copy(number).wait()
 
 
 def multiply(k_high, k_low, pieces, start, before, last=False, weight=6):
@@ -169,7 +175,7 @@
     scratch = [pltpu.VMEM((count * depth, width), HALF)] * 2
     alias = {}
     if last:
-        scratch += [pltpu.VMEM((rows, width), jnp.float32), pltpu.SemaphoreType.DMA((TILES[1],))]
+        scratch += [pltpu.VMEM((rows, width), jnp.float32), pltpu.SemaphoreType.DMA((TILES[1] * COPIES,))]
         shape = jax.ShapeDtypeStruct((1, rows, width), jnp.float32)
     else:
         shape = pltpu.VMEM((rows, width), jnp.float32)

time: 53 us -> 53.1 us (level)
  no operation moved by 1% of the time
where the time goes in v5:
time: 53.1 us; the launch traced here: 52.8 us
  Pallas kernels  22.8 us (43%)
  starting transfers between devices  16.5 us (31%)
  waiting for transfers between devices  12 us (23%)
  local copies, waits for them, and re-layouts  1.18 us (2%)
    ppermute x15, starting transfers between devices, exchange(): return lax.ppermute(value, AXES, pairs)  16.5 us
    pallas_call x6, Pallas kernels, multiply(): pl.pallas_call(functools.partial(multiply_kernel, start, [len(of) for of...  14.1 us
    ppermute x15, waiting for transfers between devices, exchange(): return lax.ppermute(value, AXES, pairs)  12 us
    pallas_call x1, Pallas kernels, split(): pl.pallas_call(functools.partial(split_kernel, lax.axis_size('row'), chun...  8.63 us
    slice x1, local copies, waits for them, and re-layouts, body(): early, late = (mine[:half], mine[half:])  1.06 us
  transfers between devices with their start and end apart: 15, of which 8 were waited for; matrix products, arithmetic and copies ran while one was open for 1% of the time, Pallas kernels for 38%

profile of v5, /device:TPU:0, one launch (start us, length us, event | category | flops | bytes accessed | tf_op | source)
XLA Modules:
  0.0 52.8 jit_solution(5789571894448510141)
XLA Ops:
  0.0 1.1 %slice_bitcast_fusion = (f32[128,512]{1,0:T(8,128)S(1)}, f32[128,512]{1,0:T(8,128)S(1)}) fusion(f32[1,256,512]{2,1,0:T(8,128)} %param.2), kind=kLoop, calls=%fused_computation.4 | loop fusion | bytes 1048576 | tf_op jit(solution)/shard_map/slice | solution.py:209
  1.1 3.1 %collective-permute-start.4 = (f32[128,512]{1,0:T(8,128)S(1)}, f32[128,512]{1,0:T(8,128)S(1)}, u32[]{:S(2)}, u32[]{:S(2)}) collective-permute-start(f32[128,512]{1,0:T(8,128)S(1)} %get-tuple-element.27), channel_id=1, source_target_pairs={{0,8},{1,17},{2,10},{3,19},{4,12},{5,21},{6,14},{7,23},{8,0},{9,25... | collective-permute-start | bytes 786440 | tf_op jit(solution)/shard_map/ppermute | solution.py:21
  4.2 0.1 collective-permute-start
  4.2 0.1 stack.35.table_ref
  4.3 8.6 %split_reduced_kernel.1 = (bf16[1536,2048]{1,0:T(8,128)(2,1)S(1)}, bf16[1536,2048]{1,0:T(8,128)(2,1)S(1)}) custom-call(s32[8]{0:T(128)S(1)} %stack.35.table_ref, f32[1536,2048]{1,0:T(8,128)} %bitcast.17), custom_call_target="tpu_custom_call" | custom-call | flops 12582912 | bytes 12582912 | tf_op jit(solution)/shard_map/split_reduced_kernel/pallas_call | solution.py:95
  13.0 0.0 collective-permute-done.4
  13.0 3.0 %collective-permute-start.5 = (f32[128,512]{1,0:T(8,128)S(1)}, f32[128,512]{1,0:T(8,128)S(1)}, u32[]{:S(2)}, u32[]{:S(2)}) collective-permute-start(f32[128,512]{1,0:T(8,128)S(1)} %multiply_add_fusion), channel_id=1, source_target_pairs={{0,16},{1,9},{2,18},{3,11},{4,20},{5,13},{6,22},{7,15},{8,24},{9,1... | collective-permute-start | bytes 786440 | tf_op jit(solution)/shard_map/ppermute | solution.py:21
  16.0 0.7 %collective-permute-done = f32[128,512]{1,0:T(8,128)S(1)} collective-permute-done((f32[128,512]{1,0:T(8,128)S(1)}, f32[128,512]{1,0:T(8,128)S(1)}, u32[]{:S(2)}, u32[]{:S(2)}) %collective-permute-start) | collective-permute-done | bytes 262176 | tf_op jit(solution)/shard_map/ppermute | solution.py:21
  16.8 2.6 %collective-permute-start.1 = (f32[128,512]{1,0:T(8,128)S(1)}, f32[128,512]{1,0:T(8,128)S(1)}, u32[]{:S(2)}, u32[]{:S(2)}) collective-permute-start(f32[128,512]{1,0:T(8,128)S(1)} %multiply_add_fusion.1), channel_id=1, source_target_pairs={{0,16},{1,9},{2,18},{3,11},{4,20},{5,13},{6,22},{7,15},{8,24},{9,1... | collective-permute-start | bytes 786440 | tf_op jit(solution)/shard_map/ppermute | solution.py:21
  19.4 3.4 %collective-permute-done.5 = f32[128,512]{1,0:T(8,128)S(1)} collective-permute-done((f32[128,512]{1,0:T(8,128)S(1)}, f32[128,512]{1,0:T(8,128)S(1)}, u32[]{:S(2)}, u32[]{:S(2)}) %collective-permute-start.5) | collective-permute-done | bytes 262176 | tf_op jit(solution)/shard_map/ppermute | solution.py:21
  22.9 1.5 %collective-permute-start.7 = (f32[1,128,512]{2,1,0:T(8,128)S(1)}, f32[1,128,512]{2,1,0:T(8,128)S(1)}, u32[]{:S(2)}, u32[]{:S(2)}) collective-permute-start(f32[1,128,512]{2,1,0:T(8,128)S(1)} %multiply_bitcast_fusion.refs_0_), channel_id=1, source_target_pairs={{0,2},{1,5},{2,0},{3,7},{4,6},{5,1},{6,4},{7,3},{8,10},{9,13},{10,... | collective-permute-start | bytes 786440 | tf_op jit(solution)/shard_map/ppermute | solution.py:21
  24.3 0.0 collective-permute-start.6
  24.3 3.2 %collective-permute-done.1 = f32[128,512]{1,0:T(8,128)S(1)} collective-permute-done((f32[128,512]{1,0:T(8,128)S(1)}, f32[128,512]{1,0:T(8,128)S(1)}, u32[]{:S(2)}, u32[]{:S(2)}) %collective-permute-start.1) | collective-permute-done | bytes 262176 | tf_op jit(solution)/shard_map/ppermute | solution.py:21
  27.6 1.7 %collective-permute-done.7.refs_2_ = f32[1,128,512]{2,1,0:T(8,128)S(1)} collective-permute-done((f32[1,128,512]{2,1,0:T(8,128)S(1)}, f32[1,128,512]{2,1,0:T(8,128)S(1)}, u32[]{:S(2)}, u32[]{:S(2)}) %collective-permute-start.7) | collective-permute-done | bytes 262176 | tf_op jit(solution)/shard_map/ppermute | solution.py:21
  29.3 0.0 collective-permute-start.8
  29.3 0.5 collective-permute-start.3
  29.8 1.4 %collective-permute-start.2 = (f32[1,128,512]{2,1,0:T(8,128)S(1)}, f32[1,128,512]{2,1,0:T(8,128)S(1)}, u32[]{:S(2)}, u32[]{:S(2)}) collective-permute-start(f32[1,128,512]{2,1,0:T(8,128)S(1)} %multiply_bitcast_fusion.1.refs_0_), channel_id=1, source_target_pairs={{0,2},{1,5},{2,0},{3,7},{4,6},{5,1},{6,4},{7,3},{8,10},{9,13},{10,... | collective-permute-start | bytes 786440 | tf_op jit(solution)/shard_map/ppermute | solution.py:21
  31.2 1.6 %collective-permute-start.10 = (f32[2,128,512]{2,1,0:T(8,128)S(1)}, f32[2,128,512]{2,1,0:T(8,128)S(1)}, u32[]{:S(2)}, u32[]{:S(2)}) collective-permute-start(f32[2,128,512]{2,1,0:T(8,128)S(1)} %pad_maximum_fusion.1), channel_id=1, source_target_pairs={{0,4},{1,3},{2,6},{3,1},{4,0},{5,7},{6,2},{7,5},{8,12},{9,11},{10,... | collective-permute-start | bytes 1572872 | tf_op jit(solution)/shard_map/ppermute | solution.py:21
  32.8 0.0 collective-permute-done.6.refs_1_
  32.8 0.0 collective-permute-done.8.refs_3_
  32.8 2.9 %multiply_sources.6.refs_2_ = f32[1536,512]{1,0:T(8,128)S(1)} custom-call(bf16[1536,2048]{1,0:T(8,128)(2,1)S(1)} %get-tuple-element.16.high_ref, bf16[1536,2048]{1,0:T(8,128)(2,1)S(1)} %get-tuple-element.17.low_ref, f32[1,128,512]{2,1,0:T(8,128)S(1)} %multiply_bitcast_fusion.refs_0_, f32[1,128,512]{2,1,0:T(8,128)S(1)} %collective-permute-done.6.refs_1_, ...), custom_call_target="tpu_custom_call" | custom-call | flops 4831838208 | tf_op jit(solution)/shard_map/multiply_sources/pallas_call | solution.py:183
  35.8 0.0 collective-permute-done.3.refs_1_
  35.8 1.7 %multiply_sources.7.refs_2_ = f32[1536,512]{1,0:T(8,128)S(1)} custom-call(bf16[1536,2048]{1,0:T(8,128)(2,1)S(1)} %get-tuple-element.16.high_ref, bf16[1536,2048]{1,0:T(8,128)(2,1)S(1)} %get-tuple-element.17.low_ref, f32[1,128,512]{2,1,0:T(8,128)S(1)} %multiply_bitcast_fusion.1.refs_0_, ...), custom_call_target="tpu_custom_call", output_to_operand_aliasing={{}: (4, {})} | custom-call | tf_op jit(solution)/shard_map/multiply_sources/pallas_call | solution.py:183
  37.5 1.2 %collective-permute-done.2.refs_0_ = f32[1,128,512]{2,1,0:T(8,128)S(1)} collective-permute-done((f32[1,128,512]{2,1,0:T(8,128)S(1)}, f32[1,128,512]{2,1,0:T(8,128)S(1)}, u32[]{:S(2)}, u32[]{:S(2)}) %collective-permute-start.2) | collective-permute-done | bytes 262176 | tf_op jit(solution)/shard_map/ppermute | solution.py:21
  38.7 0.0 collective-permute-start.13
  38.7 1.8 %collective-permute-start.9 = (f32[2,128,512]{2,1,0:T(8,128)S(1)}, f32[2,128,512]{2,1,0:T(8,128)S(1)}, u32[]{:S(2)}, u32[]{:S(2)}) collective-permute-start(f32[2,128,512]{2,1,0:T(8,128)S(1)} %pad_maximum_fusion), channel_id=1, source_target_pairs={{0,4},{1,3},{2,6},{3,1},{4,0},{5,7},{6,2},{7,5},{8,12},{9,11},{10,... | collective-permute-start | bytes 1572872 | tf_op jit(solution)/shard_map/ppermute | solution.py:21
  40.6 0.3 collective-permute-done.10.refs_0_
  40.9 0.9 %collective-permute-start.11 = (f32[1,128,512]{2,1,0:T(8,128)S(1)}, f32[1,128,512]{2,1,0:T(8,128)S(1)}, u32[]{:S(2)}, u32[]{:S(2)}) collective-permute-start(f32[1,128,512]{2,1,0:T(8,128)S(1)} %get-tuple-element.26), channel_id=1, source_target_pairs={{0,1},{1,0},{2,3},{3,2},{4,5},{5,4},{6,7},{7,6},{8,9},{9,8},{10,11... | collective-permute-start | bytes 786440 | tf_op jit(solution)/shard_map/ppermute | solution.py:21
  41.7 0.1 collective-permute-start.12
  41.8 0.0 collective-permute-done.13.refs_1_
  41.8 1.7 %multiply_sources.8.refs_3_ = f32[1536,512]{1,0:T(8,128)S(1)} custom-call(bf16[1536,2048]{1,0:T(8,128)(2,1)S(1)} %get-tuple-element.16.high_ref, bf16[1536,2048]{1,0:T(8,128)(2,1)S(1)} %get-tuple-element.17.low_ref, f32[1,128,512]{2,1,0:T(8,128)S(1)} %collective-permute-done.2.refs_0_, ...), custom_call_target="tpu_custom_call", output_to_operand_aliasing={{}: (4, {})} | custom-call | flops 1207959552 | tf_op jit(solution)/shard_map/multiply_sources/pallas_call | solution.py:183
  43.5 0.0 collective-permute-done.11.refs_1_
  43.5 0.0 collective-permute-done.12.refs_2_
  43.6 3.1 %multiply_sources.9.refs_1_ = f32[1536,512]{1,0:T(8,128)S(1)} custom-call(bf16[1536,2048]{1,0:T(8,128)(2,1)S(1)} %get-tuple-element.16.high_ref, bf16[1536,2048]{1,0:T(8,128)(2,1)S(1)} %get-tuple-element.17.low_ref, f32[2,128,512]{2,1,0:T(8,128)S(1)} %collective-permute-done.10.refs_0_, ...), custom_call_target="tpu_custom_call", output_to_operand_aliasing={{}: (5, {})} | custom-call | flops 2415919104 | tf_op jit(solution)/shard_map/multiply_sources/pallas_call | solution.py:183
  46.6 1.4 %collective-permute-done.9.refs_0_ = f32[2,128,512]{2,1,0:T(8,128)S(1)} collective-permute-done((f32[2,128,512]{2,1,0:T(8,128)S(1)}, f32[2,128,512]{2,1,0:T(8,128)S(1)}, u32[]{:S(2)}, u32[]{:S(2)}) %collective-permute-start.9) | collective-permute-done | bytes 524320 | tf_op jit(solution)/shard_map/ppermute | solution.py:21
  48.0 0.0 collective-permute-start.14
  48.0 1.7 %multiply_sources.10.refs_1_ = f32[1536,512]{1,0:T(8,128)S(1)} custom-call(bf16[1536,2048]{1,0:T(8,128)(2,1)S(1)} %get-tuple-element.16.high_ref, bf16[1536,2048]{1,0:T(8,128)(2,1)S(1)} %get-tuple-element.17.low_ref, f32[2,128,512]{2,1,0:T(8,128)S(1)} %collective-permute-done.9.refs_0_, ...), custom_call_target="tpu_custom_call", output_to_operand_aliasing={{}: (3, {})} | custom-call | flops 1207959552 | tf_op jit(solution)/shard_map/multiply_sources/pallas_call | solution.py:183
  49.7 0.2 collective-permute-done.14.refs_0_
  49.9 2.9 %multiply_sources.11 = f32[1,1536,512]{2,1,0:T(8,128)} custom-call(bf16[1536,2048]{1,0:T(8,128)(2,1)S(1)} %get-tuple-element.16.high_ref, bf16[1536,2048]{1,0:T(8,128)(2,1)S(1)} %get-tuple-element.17.low_ref, f32[2,128,512]{2,1,0:T(8,128)S(1)} %collective-permute-done.14.refs_0_, f32[1536,512]{1,0:T(8,128)S(1)} %multiply_sources.10.refs_1_), custom_call_target="tpu_custom_call" | custom-call | flops 1207959552 | tf_op jit(solution)/shard_map/multiply_sources/pallas_call | solution.py:183
  (7 shorter events, 0.3 us)
Async XLA Ops:
  1.1 11.9 %collective-permute-start.4 = (f32[128,512]{1,0:T(8,128)S(1)}, f32[128,512]{1,0:T(8,128)S(1)}, u32[]{:S(2)}, u32[]{:S(2)}) collective-permute-start(f32[128,512]{1,0:T(8,128)S(1)} %get-tuple-element.27), channel_id=1, source_target_pairs={{0,8},{1,17},{2,10},{3,19},{4,12},{5,21},{6,14},{7,23},{8,0},{9,25... | collective-permute-start | bytes 786440 | tf_op jit(solution)/shard_map/ppermute | solution.py:21
  4.2 12.6 %collective-permute-start = (f32[128,512]{1,0:T(8,128)S(1)}, f32[128,512]{1,0:T(8,128)S(1)}, u32[]{:S(2)}, u32[]{:S(2)}) collective-permute-start(f32[128,512]{1,0:T(8,128)S(1)} %get-tuple-element.28), channel_id=1, source_target_pairs={{0,8},{1,17},{2,10},{3,19},{4,12},{5,21},{6,14},{7,23},{8,0},{9,25... | collective-permute-start | bytes 786440 | tf_op jit(solution)/shard_map/ppermute | solution.py:21
  13.0 9.8 %collective-permute-start.5 = (f32[128,512]{1,0:T(8,128)S(1)}, f32[128,512]{1,0:T(8,128)S(1)}, u32[]{:S(2)}, u32[]{:S(2)}) collective-permute-start(f32[128,512]{1,0:T(8,128)S(1)} %multiply_add_fusion), channel_id=1, source_target_pairs={{0,16},{1,9},{2,18},{3,11},{4,20},{5,13},{6,22},{7,15},{8,24},{9,1... | collective-permute-start | bytes 786440 | tf_op jit(solution)/shard_map/ppermute | solution.py:21
  16.8 10.8 %collective-permute-start.1 = (f32[128,512]{1,0:T(8,128)S(1)}, f32[128,512]{1,0:T(8,128)S(1)}, u32[]{:S(2)}, u32[]{:S(2)}) collective-permute-start(f32[128,512]{1,0:T(8,128)S(1)} %multiply_add_fusion.1), channel_id=1, source_target_pairs={{0,16},{1,9},{2,18},{3,11},{4,20},{5,13},{6,22},{7,15},{8,24},{9,1... | collective-permute-start | bytes 786440 | tf_op jit(solution)/shard_map/ppermute | solution.py:21
  22.9 6.4 %collective-permute-start.7 = (f32[1,128,512]{2,1,0:T(8,128)S(1)}, f32[1,128,512]{2,1,0:T(8,128)S(1)}, u32[]{:S(2)}, u32[]{:S(2)}) collective-permute-start(f32[1,128,512]{2,1,0:T(8,128)S(1)} %multiply_bitcast_fusion.refs_0_), channel_id=1, source_target_pairs={{0,2},{1,5},{2,0},{3,7},{4,6},{5,1},{6,4},{7,3},{8,10},{9,13},{10,... | collective-permute-start | bytes 786440 | tf_op jit(solution)/shard_map/ppermute | solution.py:21
  24.3 8.5 %collective-permute-start.6 = (f32[1,128,512]{2,1,0:T(8,128)S(1)}, f32[1,128,512]{2,1,0:T(8,128)S(1)}, u32[]{:S(2)}, u32[]{:S(2)}) collective-permute-start(f32[1,128,512]{2,1,0:T(8,128)S(1)} %multiply_bitcast_fusion.refs_0_), channel_id=1, source_target_pairs={{0,1},{1,0},{2,3},{3,2},{4,5},{5,4},{6,7},{7,6},{8,9},{9,8},{10,11... | collective-permute-start | bytes 786440 | tf_op jit(solution)/shard_map/ppermute | solution.py:21
  29.3 3.5 %collective-permute-start.8 = (f32[1,128,512]{2,1,0:T(8,128)S(1)}, f32[1,128,512]{2,1,0:T(8,128)S(1)}, u32[]{:S(2)}, u32[]{:S(2)}) collective-permute-start(f32[1,128,512]{2,1,0:T(8,128)S(1)} %collective-permute-done.7.refs_2_), channel_id=1, source_target_pairs={{0,1},{1,0},{2,3},{3,2},{4,5},{5,4},{6,7},{7,6},{8,9},{9,8},{10,11... | collective-permute-start | bytes 786440 | tf_op jit(solution)/shard_map/ppermute | solution.py:21
  29.3 6.5 %collective-permute-start.3 = (f32[1,128,512]{2,1,0:T(8,128)S(1)}, f32[1,128,512]{2,1,0:T(8,128)S(1)}, u32[]{:S(2)}, u32[]{:S(2)}) collective-permute-start(f32[1,128,512]{2,1,0:T(8,128)S(1)} %multiply_bitcast_fusion.1.refs_0_), channel_id=1, source_target_pairs={{0,1},{1,0},{2,3},{3,2},{4,5},{5,4},{6,7},{7,6},{8,9},{9,8},{10,11... | collective-permute-start | bytes 786440 | tf_op jit(solution)/shard_map/ppermute | solution.py:21
  29.8 8.9 %collective-permute-start.2 = (f32[1,128,512]{2,1,0:T(8,128)S(1)}, f32[1,128,512]{2,1,0:T(8,128)S(1)}, u32[]{:S(2)}, u32[]{:S(2)}) collective-permute-start(f32[1,128,512]{2,1,0:T(8,128)S(1)} %multiply_bitcast_fusion.1.refs_0_), channel_id=1, source_target_pairs={{0,2},{1,5},{2,0},{3,7},{4,6},{5,1},{6,4},{7,3},{8,10},{9,13},{10,... | collective-permute-start | bytes 786440 | tf_op jit(solution)/shard_map/ppermute | solution.py:21
  31.2 9.6 %collective-permute-start.10 = (f32[2,128,512]{2,1,0:T(8,128)S(1)}, f32[2,128,512]{2,1,0:T(8,128)S(1)}, u32[]{:S(2)}, u32[]{:S(2)}) collective-permute-start(f32[2,128,512]{2,1,0:T(8,128)S(1)} %pad_maximum_fusion.1), channel_id=1, source_target_pairs={{0,4},{1,3},{2,6},{3,1},{4,0},{5,7},{6,2},{7,5},{8,12},{9,11},{10,... | collective-permute-start | bytes 1572872 | tf_op jit(solution)/shard_map/ppermute | solution.py:21
  38.7 3.1 %collective-permute-start.13 = (f32[1,128,512]{2,1,0:T(8,128)S(1)}, f32[1,128,512]{2,1,0:T(8,128)S(1)}, u32[]{:S(2)}, u32[]{:S(2)}) collective-permute-start(f32[1,128,512]{2,1,0:T(8,128)S(1)} %collective-permute-done.2.refs_0_), channel_id=1, source_target_pairs={{0,1},{1,0},{2,3},{3,2},{4,5},{5,4},{6,7},{7,6},{8,9},{9,8},{10,11... | collective-permute-start | bytes 786440 | tf_op jit(solution)/shard_map/ppermute | solution.py:21
  38.7 9.2 %collective-permute-start.9 = (f32[2,128,512]{2,1,0:T(8,128)S(1)}, f32[2,128,512]{2,1,0:T(8,128)S(1)}, u32[]{:S(2)}, u32[]{:S(2)}) collective-permute-start(f32[2,128,512]{2,1,0:T(8,128)S(1)} %pad_maximum_fusion), channel_id=1, source_target_pairs={{0,4},{1,3},{2,6},{3,1},{4,0},{5,7},{6,2},{7,5},{8,12},{9,11},{10,... | collective-permute-start | bytes 1572872 | tf_op jit(solution)/shard_map/ppermute | solution.py:21
  40.9 2.7 %collective-permute-start.11 = (f32[1,128,512]{2,1,0:T(8,128)S(1)}, f32[1,128,512]{2,1,0:T(8,128)S(1)}, u32[]{:S(2)}, u32[]{:S(2)}) collective-permute-start(f32[1,128,512]{2,1,0:T(8,128)S(1)} %get-tuple-element.26), channel_id=1, source_target_pairs={{0,1},{1,0},{2,3},{3,2},{4,5},{5,4},{6,7},{7,6},{8,9},{9,8},{10,11... | collective-permute-start | bytes 786440 | tf_op jit(solution)/shard_map/ppermute | solution.py:21
  41.7 1.8 %collective-permute-start.12 = (f32[1,128,512]{2,1,0:T(8,128)S(1)}, f32[1,128,512]{2,1,0:T(8,128)S(1)}, u32[]{:S(2)}, u32[]{:S(2)}) collective-permute-start(f32[1,128,512]{2,1,0:T(8,128)S(1)} %get-tuple-element.25), channel_id=1, source_target_pairs={{0,1},{1,0},{2,3},{3,2},{4,5},{5,4},{6,7},{7,6},{8,9},{9,8},{10,11... | collective-permute-start | bytes 786440 | tf_op jit(solution)/shard_map/ppermute | solution.py:21
  48.0 1.9 %collective-permute-start.14 = (f32[2,128,512]{2,1,0:T(8,128)S(1)}, f32[2,128,512]{2,1,0:T(8,128)S(1)}, u32[]{:S(2)}, u32[]{:S(2)}) collective-permute-start(f32[2,128,512]{2,1,0:T(8,128)S(1)} %collective-permute-done.9.refs_0_), channel_id=1, source_target_pairs={{0,1},{1,0},{2,3},{3,2},{4,5},{5,4},{6,7},{7,6},{8,9},{9,8},{10,11... | collective-permute-start | bytes 1572872 | tf_op jit(solution)/shard_map/ppermute | solution.py:21

commit v6 on v5

--- a/solution.py
+++ b/solution.py
@@ -25,8 +25,8 @@
     return [(step + core) % count for core in range(2)]
 
 
-def across(held, step, bits):
-    return exchange(held, [2 << bit for bit in turns(step, bits)])
+def across(held, step, bits, chunk):
+    return exchange(held, [2 << bit for bit in turns(step + chunk, bits)])
 
 
 def swapped(held, parts):
@@ -39,12 +39,12 @@
     octant = lax.axis_index("irrep").astype(jnp.int32)
     core = me & 1
     table = []
-    for stage, other in itertools.product(range(bits + 1), range(2)):
+    for chunk, stage, other in itertools.product(range(2), range(bits + 1), range(2)):
         for at in range(1 << stage >> 1, 1 << stage):
             rel = [other, other]
             for step in range(bits):
                 if at >> step & 1:
-                    for side, bit in enumerate(turns(step, bits)):
+                    for side, bit in enumerate(turns(step + chunk, bits)):
                         rel[side] ^= 2 << bit
             table.append(me ^ jnp.where(core ^ other == 1, rel[1], rel[0]))
     signs = []
@@ -81,7 +81,7 @@
     depth = k_ref.shape[1] // owners // chunks
     for chunk in range(chunks):
         for piece in range(owners):
-            start = (table_ref[piece] * chunks + chunk) * depth
+            start = (table_ref[chunk * owners + piece] * chunks + chunk) * depth
             high, low = in_two(k_ref[:, pl.ds(pl.multiple_of(start, depth), depth)])
             at = (chunk * owners + piece) * depth
             high_ref[:, at : at + depth] = high
@@ -217,19 +217,20 @@
     early, late = [lax.optimization_barrier(part[None]) for part in (early, late)]
     pieces, others = [early], [*swapped(early, 1)]
     for step in range(bits - 1):
-        pieces.append(after(across(early, step, bits), late))
+        pieces.append(after(across(early, step, bits, 0), late))
         others += swapped(pieces[-1], 1)
         early = jnp.concatenate([early, pieces[-1]])
-    first = across(early, bits - 1, bits)
+    first = across(early, bits - 1, bits, 0)
     pieces = [*itertools.chain(*zip(pieces, others))]
     out = multiply(*ks, [pieces], 0, None, weight=12)
     out = multiply(*ks, [[late, *swapped(late, 1)]], owners, out, weight=0)
     for step in range(bits - 1):
-        second = after(across(late, step, bits), out)
+        second = after(across(late, step, bits, 1), out)
         out = multiply(*ks, [[second, *swapped(second, 1)]], owners + (2 << step), out)
         late = jnp.concatenate([late, second])
+    first = after(first, out)
     out = multiply(*ks, [[first, *swapped(first, 2)]], 1 << bits, out)
-    second = after(across(late, bits - 1, bits), out)
+    second = after(across(late, bits - 1, bits, 1), out)
     start = owners + (1 << bits)
     out = multiply(*ks, [[second]], start, out)
     return multiply(*ks, [swapped(second, 1)], start + second.shape[0], out, True)

time: 53.1 us -> 53.7 us (1.011)
  waiting for transfers between devices: 12 us -> 13.9 us
  starting transfers between devices: 16.5 us -> 15.5 us
    ppermute x15, waiting for transfers between devices: 12 us -> 13.9 us  [exchange(): return lax.ppermute(value, AXES, pairs)]
    ppermute x15, starting transfers between devices: 16.5 us -> 15.5 us  [exchange(): return lax.ppermute(value, AXES, pairs)]
  transfers between devices with their start and end apart: 15 -> 15, of which waited for: 8 -> 7; matrix products, arithmetic and copies ran while one was open for 1% -> 1% of each run, Pallas kernels for 38% -> 37%
where the time goes in v6:
time: 53.7 us; the launch traced here: 53.5 us
  Pallas kernels  22.7 us (42%)
  starting transfers between devices  15.5 us (29%)
  waiting for transfers between devices  13.9 us (26%)
  local copies, waits for them, and re-layouts  1.19 us (2%)
    ppermute x15, starting transfers between devices, exchange(): return lax.ppermute(value, AXES, pairs)  15.5 us
    pallas_call x6, Pallas kernels, multiply(): pl.pallas_call(functools.partial(multiply_kernel, start, [len(of) for of...  14.1 us
    ppermute x15, waiting for transfers between devices, exchange(): return lax.ppermute(value, AXES, pairs)  13.9 us
    pallas_call x1, Pallas kernels, split(): pl.pallas_call(functools.partial(split_kernel, lax.axis_size('row'), chun...  8.56 us
  transfers between devices with their start and end apart: 15, of which 7 were waited for; matrix products, arithmetic and copies ran while one was open for 1% of the time, Pallas kernels for 37%

profile of v6, /device:TPU:0, one launch (start us, length us, event | category | flops | bytes accessed | tf_op | source)
XLA Modules:
  0.0 53.5 jit_solution(16743569594919020558)
XLA Ops:
  0.0 1.1 %slice_bitcast_fusion = (f32[128,512]{1,0:T(8,128)S(1)}, f32[128,512]{1,0:T(8,128)S(1)}) fusion(f32[1,256,512]{2,1,0:T(8,128)} %param.2), kind=kLoop, calls=%fused_computation.4 | loop fusion | bytes 1048576 | tf_op jit(solution)/shard_map/slice | solution.py:209
  1.1 3.1 %collective-permute-start.4 = (f32[128,512]{1,0:T(8,128)S(1)}, f32[128,512]{1,0:T(8,128)S(1)}, u32[]{:S(2)}, u32[]{:S(2)}) collective-permute-start(f32[128,512]{1,0:T(8,128)S(1)} %get-tuple-element.29), channel_id=1, source_target_pairs={{0,8},{1,17},{2,10},{3,19},{4,12},{5,21},{6,14},{7,23},{8,0},{9,25... | collective-permute-start | bytes 786440 | tf_op jit(solution)/shard_map/ppermute | solution.py:21
  4.2 0.1 collective-permute-start
  4.2 0.1 stack.43.table_ref
  4.3 8.6 %split_reduced_kernel.1 = (bf16[1536,2048]{1,0:T(8,128)(2,1)S(1)}, bf16[1536,2048]{1,0:T(8,128)(2,1)S(1)}) custom-call(s32[16]{0:T(128)S(1)} %stack.43.table_ref, f32[1536,2048]{1,0:T(8,128)} %bitcast.17), custom_call_target="tpu_custom_call" | custom-call | flops 12582912 | bytes 12582912 | tf_op jit(solution)/shard_map/split_reduced_kernel/pallas_call | solution.py:95
  12.9 0.0 collective-permute-done.4
  13.0 3.0 %collective-permute-start.5 = (f32[128,512]{1,0:T(8,128)S(1)}, f32[128,512]{1,0:T(8,128)S(1)}, u32[]{:S(2)}, u32[]{:S(2)}) collective-permute-start(f32[128,512]{1,0:T(8,128)S(1)} %multiply_add_fusion), channel_id=1, source_target_pairs={{0,16},{1,9},{2,18},{3,11},{4,20},{5,13},{6,22},{7,15},{8,24},{9,1... | collective-permute-start | bytes 786440 | tf_op jit(solution)/shard_map/ppermute | solution.py:21
  16.0 0.8 %collective-permute-done = f32[128,512]{1,0:T(8,128)S(1)} collective-permute-done((f32[128,512]{1,0:T(8,128)S(1)}, f32[128,512]{1,0:T(8,128)S(1)}, u32[]{:S(2)}, u32[]{:S(2)}) %collective-permute-start) | collective-permute-done | bytes 262176 | tf_op jit(solution)/shard_map/ppermute | solution.py:21
  16.8 2.6 %collective-permute-start.1 = (f32[128,512]{1,0:T(8,128)S(1)}, f32[128,512]{1,0:T(8,128)S(1)}, u32[]{:S(2)}, u32[]{:S(2)}) collective-permute-start(f32[128,512]{1,0:T(8,128)S(1)} %multiply_add_fusion.1), channel_id=1, source_target_pairs={{0,16},{1,9},{2,18},{3,11},{4,20},{5,13},{6,22},{7,15},{8,24},{9,1... | collective-permute-start | bytes 786440 | tf_op jit(solution)/shard_map/ppermute | solution.py:21
  19.4 3.3 %collective-permute-done.5 = f32[128,512]{1,0:T(8,128)S(1)} collective-permute-done((f32[128,512]{1,0:T(8,128)S(1)}, f32[128,512]{1,0:T(8,128)S(1)}, u32[]{:S(2)}, u32[]{:S(2)}) %collective-permute-start.5) | collective-permute-done | bytes 262176 | tf_op jit(solution)/shard_map/ppermute | solution.py:21
  22.8 1.6 %collective-permute-start.7 = (f32[1,128,512]{2,1,0:T(8,128)S(1)}, f32[1,128,512]{2,1,0:T(8,128)S(1)}, u32[]{:S(2)}, u32[]{:S(2)}) collective-permute-start(f32[1,128,512]{2,1,0:T(8,128)S(1)} %multiply_bitcast_fusion.refs_0_), channel_id=1, source_target_pairs={{0,2},{1,5},{2,0},{3,7},{4,6},{5,1},{6,4},{7,3},{8,10},{9,13},{10,... | collective-permute-start | bytes 786440 | tf_op jit(solution)/shard_map/ppermute | solution.py:21
  24.4 0.0 collective-permute-start.6
  24.4 3.2 %collective-permute-done.1 = f32[128,512]{1,0:T(8,128)S(1)} collective-permute-done((f32[128,512]{1,0:T(8,128)S(1)}, f32[128,512]{1,0:T(8,128)S(1)}, u32[]{:S(2)}, u32[]{:S(2)}) %collective-permute-start.1) | collective-permute-done | bytes 262176 | tf_op jit(solution)/shard_map/ppermute | solution.py:21
  27.6 1.6 %collective-permute-done.7.refs_2_ = f32[1,128,512]{2,1,0:T(8,128)S(1)} collective-permute-done((f32[1,128,512]{2,1,0:T(8,128)S(1)}, f32[1,128,512]{2,1,0:T(8,128)S(1)}, u32[]{:S(2)}, u32[]{:S(2)}) %collective-permute-start.7) | collective-permute-done | bytes 262176 | tf_op jit(solution)/shard_map/ppermute | solution.py:21
  29.2 0.0 collective-permute-start.8
  29.2 0.5 collective-permute-start.3
  29.7 1.5 %collective-permute-start.2 = (f32[1,128,512]{2,1,0:T(8,128)S(1)}, f32[1,128,512]{2,1,0:T(8,128)S(1)}, u32[]{:S(2)}, u32[]{:S(2)}) collective-permute-start(f32[1,128,512]{2,1,0:T(8,128)S(1)} %multiply_bitcast_fusion.1.refs_0_), channel_id=1, source_target_pairs={{0,4},{1,3},{2,6},{3,1},{4,0},{5,7},{6,2},{7,5},{8,12},{9,11},{10,... | collective-permute-start | bytes 786440 | tf_op jit(solution)/shard_map/ppermute | solution.py:21
  31.3 0.6 %collective-permute-start.10 = (f32[2,128,512]{2,1,0:T(8,128)S(1)}, f32[2,128,512]{2,1,0:T(8,128)S(1)}, u32[]{:S(2)}, u32[]{:S(2)}) collective-permute-start(f32[2,128,512]{2,1,0:T(8,128)S(1)} %pad_maximum_fusion.1), channel_id=1, source_target_pairs={{0,4},{1,3},{2,6},{3,1},{4,0},{5,7},{6,2},{7,5},{8,12},{9,11},{10,... | collective-permute-start | bytes 1572872 | tf_op jit(solution)/shard_map/ppermute | solution.py:21
  31.9 0.0 collective-permute-done.6.refs_1_
  31.9 0.0 collective-permute-done.8.refs_3_
  31.9 2.9 %multiply_sources.6.refs_2_ = f32[1536,512]{1,0:T(8,128)S(1)} custom-call(bf16[1536,2048]{1,0:T(8,128)(2,1)S(1)} %get-tuple-element.17.high_ref, bf16[1536,2048]{1,0:T(8,128)(2,1)S(1)} %get-tuple-element.18.low_ref, f32[1,128,512]{2,1,0:T(8,128)S(1)} %multiply_bitcast_fusion.refs_0_, f32[1,128,512]{2,1,0:T(8,128)S(1)} %collective-permute-done.6.refs_1_, ...), custom_call_target="tpu_custom_call" | custom-call | flops 4831838208 | tf_op jit(solution)/shard_map/multiply_sources/pallas_call | solution.py:183
  34.8 0.0 collective-permute-done.3.refs_1_
  34.8 1.7 %multiply_sources.7.refs_2_ = f32[1536,512]{1,0:T(8,128)S(1)} custom-call(bf16[1536,2048]{1,0:T(8,128)(2,1)S(1)} %get-tuple-element.17.high_ref, bf16[1536,2048]{1,0:T(8,128)(2,1)S(1)} %get-tuple-element.18.low_ref, f32[1,128,512]{2,1,0:T(8,128)S(1)} %multiply_bitcast_fusion.1.refs_0_, ...), custom_call_target="tpu_custom_call", output_to_operand_aliasing={{}: (4, {})} | custom-call | tf_op jit(solution)/shard_map/multiply_sources/pallas_call | solution.py:183
  36.6 0.0 collective-permute-done.2.refs_0_
  36.6 0.1 collective-permute-start.11
  36.7 1.6 %collective-permute-start.9 = (f32[2,128,512]{2,1,0:T(8,128)S(1)}, f32[2,128,512]{2,1,0:T(8,128)S(1)}, u32[]{:S(2)}, u32[]{:S(2)}) collective-permute-start(f32[2,128,512]{2,1,0:T(8,128)S(1)} %pad_maximum_fusion), channel_id=1, source_target_pairs={{0,2},{1,5},{2,0},{3,7},{4,6},{5,1},{6,4},{7,3},{8,10},{9,13},{10,... | collective-permute-start | bytes 1572872 | tf_op jit(solution)/shard_map/ppermute | solution.py:21
  38.3 0.0 collective-permute-done.11.refs_1_
  38.3 1.7 %multiply_sources.8.refs_3_ = f32[1536,512]{1,0:T(8,128)S(1)} custom-call(bf16[1536,2048]{1,0:T(8,128)(2,1)S(1)} %get-tuple-element.17.high_ref, bf16[1536,2048]{1,0:T(8,128)(2,1)S(1)} %get-tuple-element.18.low_ref, f32[1,128,512]{2,1,0:T(8,128)S(1)} %collective-permute-done.2.refs_0_, ...), custom_call_target="tpu_custom_call", output_to_operand_aliasing={{}: (4, {})} | custom-call | flops 1207959552 | tf_op jit(solution)/shard_map/multiply_sources/pallas_call | solution.py:183
  40.0 3.5 %collective-permute-done.10.refs_0_ = f32[2,128,512]{2,1,0:T(8,128)S(1)} collective-permute-done((f32[2,128,512]{2,1,0:T(8,128)S(1)}, f32[2,128,512]{2,1,0:T(8,128)S(1)}, u32[]{:S(2)}, u32[]{:S(2)}) %collective-permute-start.10) | collective-permute-done | bytes 524320 | tf_op jit(solution)/shard_map/ppermute | solution.py:21
  43.6 0.1 collective-permute-start.13
  43.7 0.5 collective-permute-start.12
  44.2 1.0 %collective-permute-done.13.refs_2_ = f32[1,128,512]{2,1,0:T(8,128)S(1)} collective-permute-done((f32[1,128,512]{2,1,0:T(8,128)S(1)}, f32[1,128,512]{2,1,0:T(8,128)S(1)}, u32[]{:S(2)}, u32[]{:S(2)}) %collective-permute-start.13) | collective-permute-done | bytes 262176 | tf_op jit(solution)/shard_map/ppermute | solution.py:21
  45.2 0.4 collective-permute-done.12.refs_1_
  45.6 3.1 %multiply_sources.9.refs_1_ = f32[1536,512]{1,0:T(8,128)S(1)} custom-call(bf16[1536,2048]{1,0:T(8,128)(2,1)S(1)} %get-tuple-element.17.high_ref, bf16[1536,2048]{1,0:T(8,128)(2,1)S(1)} %get-tuple-element.18.low_ref, f32[2,128,512]{2,1,0:T(8,128)S(1)} %collective-permute-done.10.refs_0_, ...), custom_call_target="tpu_custom_call", output_to_operand_aliasing={{}: (5, {})} | custom-call | flops 2415919104 | tf_op jit(solution)/shard_map/multiply_sources/pallas_call | solution.py:183
  48.6 0.0 collective-permute-done.9.refs_0_
  48.6 0.2 collective-permute-start.14
  48.8 1.7 %multiply_sources.10.refs_1_ = f32[1536,512]{1,0:T(8,128)S(1)} custom-call(bf16[1536,2048]{1,0:T(8,128)(2,1)S(1)} %get-tuple-element.17.high_ref, bf16[1536,2048]{1,0:T(8,128)(2,1)S(1)} %get-tuple-element.18.low_ref, f32[2,128,512]{2,1,0:T(8,128)S(1)} %collective-permute-done.9.refs_0_, ...), custom_call_target="tpu_custom_call", output_to_operand_aliasing={{}: (3, {})} | custom-call | flops 1207959552 | tf_op jit(solution)/shard_map/multiply_sources/pallas_call | solution.py:183
  50.6 0.0 collective-permute-done.14.refs_0_
  50.6 2.9 %multiply_sources.11 = f32[1,1536,512]{2,1,0:T(8,128)} custom-call(bf16[1536,2048]{1,0:T(8,128)(2,1)S(1)} %get-tuple-element.17.high_ref, bf16[1536,2048]{1,0:T(8,128)(2,1)S(1)} %get-tuple-element.18.low_ref, f32[2,128,512]{2,1,0:T(8,128)S(1)} %collective-permute-done.14.refs_0_, f32[1536,512]{1,0:T(8,128)S(1)} %multiply_sources.10.refs_1_), custom_call_target="tpu_custom_call" | custom-call | flops 1207959552 | tf_op jit(solution)/shard_map/multiply_sources/pallas_call | solution.py:183
  (7 shorter events, 0.3 us)
Async XLA Ops:
  1.1 11.8 %collective-permute-start.4 = (f32[128,512]{1,0:T(8,128)S(1)}, f32[128,512]{1,0:T(8,128)S(1)}, u32[]{:S(2)}, u32[]{:S(2)}) collective-permute-start(f32[128,512]{1,0:T(8,128)S(1)} %get-tuple-element.29), channel_id=1, source_target_pairs={{0,8},{1,17},{2,10},{3,19},{4,12},{5,21},{6,14},{7,23},{8,0},{9,25... | collective-permute-start | bytes 786440 | tf_op jit(solution)/shard_map/ppermute | solution.py:21
  4.2 12.6 %collective-permute-start = (f32[128,512]{1,0:T(8,128)S(1)}, f32[128,512]{1,0:T(8,128)S(1)}, u32[]{:S(2)}, u32[]{:S(2)}) collective-permute-start(f32[128,512]{1,0:T(8,128)S(1)} %get-tuple-element.30), channel_id=1, source_target_pairs={{0,8},{1,17},{2,10},{3,19},{4,12},{5,21},{6,14},{7,23},{8,0},{9,25... | collective-permute-start | bytes 786440 | tf_op jit(solution)/shard_map/ppermute | solution.py:21
  13.0 9.8 %collective-permute-start.5 = (f32[128,512]{1,0:T(8,128)S(1)}, f32[128,512]{1,0:T(8,128)S(1)}, u32[]{:S(2)}, u32[]{:S(2)}) collective-permute-start(f32[128,512]{1,0:T(8,128)S(1)} %multiply_add_fusion), channel_id=1, source_target_pairs={{0,16},{1,9},{2,18},{3,11},{4,20},{5,13},{6,22},{7,15},{8,24},{9,1... | collective-permute-start | bytes 786440 | tf_op jit(solution)/shard_map/ppermute | solution.py:21
  16.8 10.8 %collective-permute-start.1 = (f32[128,512]{1,0:T(8,128)S(1)}, f32[128,512]{1,0:T(8,128)S(1)}, u32[]{:S(2)}, u32[]{:S(2)}) collective-permute-start(f32[128,512]{1,0:T(8,128)S(1)} %multiply_add_fusion.1), channel_id=1, source_target_pairs={{0,16},{1,9},{2,18},{3,11},{4,20},{5,13},{6,22},{7,15},{8,24},{9,1... | collective-permute-start | bytes 786440 | tf_op jit(solution)/shard_map/ppermute | solution.py:21
  22.8 6.4 %collective-permute-start.7 = (f32[1,128,512]{2,1,0:T(8,128)S(1)}, f32[1,128,512]{2,1,0:T(8,128)S(1)}, u32[]{:S(2)}, u32[]{:S(2)}) collective-permute-start(f32[1,128,512]{2,1,0:T(8,128)S(1)} %multiply_bitcast_fusion.refs_0_), channel_id=1, source_target_pairs={{0,2},{1,5},{2,0},{3,7},{4,6},{5,1},{6,4},{7,3},{8,10},{9,13},{10,... | collective-permute-start | bytes 786440 | tf_op jit(solution)/shard_map/ppermute | solution.py:21
  24.4 7.5 %collective-permute-start.6 = (f32[1,128,512]{2,1,0:T(8,128)S(1)}, f32[1,128,512]{2,1,0:T(8,128)S(1)}, u32[]{:S(2)}, u32[]{:S(2)}) collective-permute-start(f32[1,128,512]{2,1,0:T(8,128)S(1)} %multiply_bitcast_fusion.refs_0_), channel_id=1, source_target_pairs={{0,1},{1,0},{2,3},{3,2},{4,5},{5,4},{6,7},{7,6},{8,9},{9,8},{10,11... | collective-permute-start | bytes 786440 | tf_op jit(solution)/shard_map/ppermute | solution.py:21
  29.2 2.6 %collective-permute-start.8 = (f32[1,128,512]{2,1,0:T(8,128)S(1)}, f32[1,128,512]{2,1,0:T(8,128)S(1)}, u32[]{:S(2)}, u32[]{:S(2)}) collective-permute-start(f32[1,128,512]{2,1,0:T(8,128)S(1)} %collective-permute-done.7.refs_2_), channel_id=1, source_target_pairs={{0,1},{1,0},{2,3},{3,2},{4,5},{5,4},{6,7},{7,6},{8,9},{9,8},{10,11... | collective-permute-start | bytes 786440 | tf_op jit(solution)/shard_map/ppermute | solution.py:21
  29.2 5.6 %collective-permute-start.3 = (f32[1,128,512]{2,1,0:T(8,128)S(1)}, f32[1,128,512]{2,1,0:T(8,128)S(1)}, u32[]{:S(2)}, u32[]{:S(2)}) collective-permute-start(f32[1,128,512]{2,1,0:T(8,128)S(1)} %multiply_bitcast_fusion.1.refs_0_), channel_id=1, source_target_pairs={{0,1},{1,0},{2,3},{3,2},{4,5},{5,4},{6,7},{7,6},{8,9},{9,8},{10,11... | collective-permute-start | bytes 786440 | tf_op jit(solution)/shard_map/ppermute | solution.py:21
  29.7 6.8 %collective-permute-start.2 = (f32[1,128,512]{2,1,0:T(8,128)S(1)}, f32[1,128,512]{2,1,0:T(8,128)S(1)}, u32[]{:S(2)}, u32[]{:S(2)}) collective-permute-start(f32[1,128,512]{2,1,0:T(8,128)S(1)} %multiply_bitcast_fusion.1.refs_0_), channel_id=1, source_target_pairs={{0,4},{1,3},{2,6},{3,1},{4,0},{5,7},{6,2},{7,5},{8,12},{9,11},{10,... | collective-permute-start | bytes 786440 | tf_op jit(solution)/shard_map/ppermute | solution.py:21
  31.3 12.2 %collective-permute-start.10 = (f32[2,128,512]{2,1,0:T(8,128)S(1)}, f32[2,128,512]{2,1,0:T(8,128)S(1)}, u32[]{:S(2)}, u32[]{:S(2)}) collective-permute-start(f32[2,128,512]{2,1,0:T(8,128)S(1)} %pad_maximum_fusion.1), channel_id=1, source_target_pairs={{0,4},{1,3},{2,6},{3,1},{4,0},{5,7},{6,2},{7,5},{8,12},{9,11},{10,... | collective-permute-start | bytes 1572872 | tf_op jit(solution)/shard_map/ppermute | solution.py:21
  36.6 1.7 %collective-permute-start.11 = (f32[1,128,512]{2,1,0:T(8,128)S(1)}, f32[1,128,512]{2,1,0:T(8,128)S(1)}, u32[]{:S(2)}, u32[]{:S(2)}) collective-permute-start(f32[1,128,512]{2,1,0:T(8,128)S(1)} %collective-permute-done.2.refs_0_), channel_id=1, source_target_pairs={{0,1},{1,0},{2,3},{3,2},{4,5},{5,4},{6,7},{7,6},{8,9},{9,8},{10,11... | collective-permute-start | bytes 786440 | tf_op jit(solution)/shard_map/ppermute | solution.py:21
  36.7 11.9 %collective-permute-start.9 = (f32[2,128,512]{2,1,0:T(8,128)S(1)}, f32[2,128,512]{2,1,0:T(8,128)S(1)}, u32[]{:S(2)}, u32[]{:S(2)}) collective-permute-start(f32[2,128,512]{2,1,0:T(8,128)S(1)} %pad_maximum_fusion), channel_id=1, source_target_pairs={{0,2},{1,5},{2,0},{3,7},{4,6},{5,1},{6,4},{7,3},{8,10},{9,13},{10,... | collective-permute-start | bytes 1572872 | tf_op jit(solution)/shard_map/ppermute | solution.py:21
  43.6 1.6 %collective-permute-start.13 = (f32[1,128,512]{2,1,0:T(8,128)S(1)}, f32[1,128,512]{2,1,0:T(8,128)S(1)}, u32[]{:S(2)}, u32[]{:S(2)}) collective-permute-start(f32[1,128,512]{2,1,0:T(8,128)S(1)} %get-tuple-element.27), channel_id=1, source_target_pairs={{0,1},{1,0},{2,3},{3,2},{4,5},{5,4},{6,7},{7,6},{8,9},{9,8},{10,11... | collective-permute-start | bytes 786440 | tf_op jit(solution)/shard_map/ppermute | solution.py:21
  43.7 1.9 %collective-permute-start.12 = (f32[1,128,512]{2,1,0:T(8,128)S(1)}, f32[1,128,512]{2,1,0:T(8,128)S(1)}, u32[]{:S(2)}, u32[]{:S(2)}) collective-permute-start(f32[1,128,512]{2,1,0:T(8,128)S(1)} %get-tuple-element.28), channel_id=1, source_target_pairs={{0,1},{1,0},{2,3},{3,2},{4,5},{5,4},{6,7},{7,6},{8,9},{9,8},{10,11... | collective-permute-start | bytes 786440 | tf_op jit(solution)/shard_map/ppermute | solution.py:21
  48.6 2.0 %collective-permute-start.14 = (f32[2,128,512]{2,1,0:T(8,128)S(1)}, f32[2,128,512]{2,1,0:T(8,128)S(1)}, u32[]{:S(2)}, u32[]{:S(2)}) collective-permute-start(f32[2,128,512]{2,1,0:T(8,128)S(1)} %collective-permute-done.9.refs_0_), channel_id=1, source_target_pairs={{0,1},{1,0},{2,3},{3,2},{4,5},{5,4},{6,7},{7,6},{8,9},{9,8},{10,11... | collective-permute-start | bytes 1572872 | tf_op jit(solution)/shard_map/ppermute | solution.py:21

commit v7 on v1

--- a/solution.py
+++ b/solution.py
@@ -10,7 +10,7 @@
 
 HALF = jnp.bfloat16
 AXES = ("irrep", "row")
-TILES = 2
+TILES = (1, 2)
 WEIGHT = 6
 
 
@@ -130,7 +130,8 @@
             f_low[at : at + depth, :] = low
             at += depth
     sources = slice(start * depth, start * depth + at)
-    tile = high_ref.shape[0] // TILES
+    tiles = TILES[last]
+    tile = high_ref.shape[0] // tiles
 
     def product(step):
         here = pl.ds(pl.multiple_of(step * tile, tile), tile)
@@ -142,7 +143,7 @@
 
     if not last:
 
-        @pl.loop(0, TILES)
+        @pl.loop(0, tiles)
         def _(step):
             here, total = product(step)
             out_ref[here, :] = total
@@ -155,13 +156,13 @@
                 result.at[here, :], out_ref.at[0, here, :], sems.at[step]
             )
 
-        @pl.loop(0, TILES)
+        @pl.loop(0, tiles)
         def _(step):
             here, total = product(step)
             result[here, :] = total
             copy(here, step).start()
 
-        for step in range(TILES):
+        for step in range(tiles):
             copy(slice(step * tile, (step + 1) * tile), step).wait()
 
 
@@ -174,7 +175,7 @@
     scratch = [pltpu.VMEM((count * depth, width), HALF)] * 2
     alias = {}
     if last:
-        scratch += [pltpu.VMEM((rows, width), jnp.float32), pltpu.SemaphoreType.DMA((TILES,))]
+        scratch += [pltpu.VMEM((rows, width), jnp.float32), pltpu.SemaphoreType.DMA((TILES[1],))]
         shape = jax.ShapeDtypeStruct((1, rows, width), jnp.float32)
     else:
         shape = pltpu.VMEM((rows, width), jnp.float32)

time: 53.2 us -> 52.9 us (level)
  Pallas kernels: 21.7 us -> 20.5 us
  waiting for transfers between devices: 13.8 us -> 15 us
    ppermute x13, waiting for transfers between devices: 13.8 us -> 15 us  [exchange(): return lax.ppermute(value, AXES, pairs)]
    pallas_call x5, Pallas kernels: 13.6 us -> 12.5 us  [multiply(): pl.pallas_call(functools.partial(multiply_kernel, start, len(pieces), acc...]
  transfers between devices with their start and end apart: 13 -> 13, of which waited for: 5 -> 7; matrix products, arithmetic and copies ran while one was open for 1% -> 1% of each run, Pallas kernels for 36% -> 34%
where the time goes in v7:
time: 52.9 us; the launch traced here: 52.7 us
  Pallas kernels  20.5 us (39%)
  starting transfers between devices  15.6 us (29%)
  waiting for transfers between devices  15 us (28%)
  local copies, waits for them, and re-layouts  1.18 us (2%)
    ppermute x13, starting transfers between devices, exchange(): return lax.ppermute(value, AXES, pairs)  15.6 us
    ppermute x13, waiting for transfers between devices, exchange(): return lax.ppermute(value, AXES, pairs)  15 us
    pallas_call x5, Pallas kernels, multiply(): pl.pallas_call(functools.partial(multiply_kernel, start, len(pieces), acc...  12.5 us
    pallas_call x1, Pallas kernels, split(): pl.pallas_call(functools.partial(split_kernel, lax.axis_size('row'), chun...  8.05 us
    slice x1, local copies, waits for them, and re-layouts, body(): mine[at * half:(at + 1) * half]  1.06 us
  transfers between devices with their start and end apart: 13, of which 7 were waited for; matrix products, arithmetic and copies ran while one was open for 1% of the time, Pallas kernels for 34%

profile of v7, /device:TPU:0, one launch (start us, length us, event | category | flops | bytes accessed | tf_op | source)
XLA Modules:
  0.0 52.7 jit_solution(16361757814592719590)
XLA Ops:
  0.0 1.1 %slice_bitcast_fusion = (f32[128,512]{1,0:T(8,128)S(1)}, f32[128,512]{1,0:T(8,128)S(1)}) fusion(f32[1,256,512]{2,1,0:T(8,128)} %param.2), kind=kLoop, calls=%fused_computation.4 | loop fusion | bytes 1048576 | tf_op jit(solution)/shard_map/slice | solution.py:209
  1.1 3.1 %collective-permute-start.3 = (f32[128,512]{1,0:T(8,128)S(1)}, f32[128,512]{1,0:T(8,128)S(1)}, u32[]{:S(2)}, u32[]{:S(2)}) collective-permute-start(f32[128,512]{1,0:T(8,128)S(1)} %get-tuple-element.27), channel_id=1, source_target_pairs={{0,8},{1,17},{2,10},{3,19},{4,12},{5,21},{6,14},{7,23},{8,0},{9,25... | collective-permute-start | bytes 786440 | tf_op jit(solution)/shard_map/ppermute | solution.py:20
  4.2 0.1 collective-permute-start
  4.2 0.1 stack.35.table_ref
  4.3 8.0 %split_reduced_kernel.1 = (bf16[1536,2048]{1,0:T(8,128)(2,1)S(1)}, bf16[1536,2048]{1,0:T(8,128)(2,1)S(1)}) custom-call(s32[8]{0:T(128)S(1)} %stack.35.table_ref, f32[1536,2048]{1,0:T(8,128)} %bitcast.15), custom_call_target="tpu_custom_call" | custom-call | flops 12582912 | bytes 12582912 | tf_op jit(solution)/shard_map/split_reduced_kernel/pallas_call | solution.py:102
  12.4 0.0 collective-permute-done.3
  12.4 3.0 %collective-permute-start.4 = (f32[128,512]{1,0:T(8,128)S(1)}, f32[128,512]{1,0:T(8,128)S(1)}, u32[]{:S(2)}, u32[]{:S(2)}) collective-permute-start(f32[128,512]{1,0:T(8,128)S(1)} %multiply_add_fusion), channel_id=1, source_target_pairs={{0,16},{1,9},{2,18},{3,11},{4,20},{5,13},{6,22},{7,15},{8,24},{9,1... | collective-permute-start | bytes 786440 | tf_op jit(solution)/shard_map/ppermute | solution.py:20
  15.5 3.5 %collective-permute-done = f32[128,512]{1,0:T(8,128)S(1)} collective-permute-done((f32[128,512]{1,0:T(8,128)S(1)}, f32[128,512]{1,0:T(8,128)S(1)}, u32[]{:S(2)}, u32[]{:S(2)}) %collective-permute-start) | collective-permute-done | bytes 262176 | tf_op jit(solution)/shard_map/ppermute | solution.py:20
  19.0 1.1 %collective-permute-start.1 = (f32[128,512]{1,0:T(8,128)S(1)}, f32[128,512]{1,0:T(8,128)S(1)}, u32[]{:S(2)}, u32[]{:S(2)}) collective-permute-start(f32[128,512]{1,0:T(8,128)S(1)} %multiply_add_fusion.1), channel_id=1, source_target_pairs={{0,16},{1,9},{2,18},{3,11},{4,20},{5,13},{6,22},{7,15},{8,24},{9,1... | collective-permute-start | bytes 786440 | tf_op jit(solution)/shard_map/ppermute | solution.py:20
  20.1 2.1 %collective-permute-done.4 = f32[128,512]{1,0:T(8,128)S(1)} collective-permute-done((f32[128,512]{1,0:T(8,128)S(1)}, f32[128,512]{1,0:T(8,128)S(1)}, u32[]{:S(2)}, u32[]{:S(2)}) %collective-permute-start.4) | collective-permute-done | bytes 262176 | tf_op jit(solution)/shard_map/ppermute | solution.py:20
  22.3 1.4 %collective-permute-start.5 = (f32[1,128,512]{2,1,0:T(8,128)S(1)}, f32[1,128,512]{2,1,0:T(8,128)S(1)}, u32[]{:S(2)}, u32[]{:S(2)}) collective-permute-start(f32[1,128,512]{2,1,0:T(8,128)S(1)} %bitcast.18), channel_id=1, source_target_pairs={{0,2},{1,5},{2,0},{3,7},{4,6},{5,1},{6,4},{7,3},{8,10},{9,13},{10,... | collective-permute-start | bytes 786440 | tf_op jit(solution)/shard_map/ppermute | solution.py:20
  23.7 5.9 %collective-permute-done.1 = f32[128,512]{1,0:T(8,128)S(1)} collective-permute-done((f32[128,512]{1,0:T(8,128)S(1)}, f32[128,512]{1,0:T(8,128)S(1)}, u32[]{:S(2)}, u32[]{:S(2)}) %collective-permute-start.1) | collective-permute-done | bytes 262176 | tf_op jit(solution)/shard_map/ppermute | solution.py:20
  29.6 0.0 collective-permute-done.5
  29.7 0.1 collective-permute-start.6
  29.7 2.0 %collective-permute-start.2 = (f32[1,128,512]{2,1,0:T(8,128)S(1)}, f32[1,128,512]{2,1,0:T(8,128)S(1)}, u32[]{:S(2)}, u32[]{:S(2)}) collective-permute-start(f32[1,128,512]{2,1,0:T(8,128)S(1)} %bitcast.16), channel_id=1, source_target_pairs={{0,2},{1,5},{2,0},{3,7},{4,6},{5,1},{6,4},{7,3},{8,10},{9,13},{10,... | collective-permute-start | bytes 786440 | tf_op jit(solution)/shard_map/ppermute | solution.py:20
  31.7 1.5 %collective-permute-start.8 = (f32[2,128,512]{2,1,0:T(8,128)S(1)}, f32[2,128,512]{2,1,0:T(8,128)S(1)}, u32[]{:S(2)}, u32[]{:S(2)}) collective-permute-start(f32[2,128,512]{2,1,0:T(8,128)S(1)} %pad_maximum_fusion.refs_0_), channel_id=1, source_target_pairs={{0,4},{1,3},{2,6},{3,1},{4,0},{5,7},{6,2},{7,5},{8,12},{9,11},{10,... | collective-permute-start | bytes 1572872 | tf_op jit(solution)/shard_map/ppermute | solution.py:20
  33.2 0.0 collective-permute-done.6.refs_1_
  33.2 2.6 %multiply_sources.5.refs_2_ = f32[1536,512]{1,0:T(8,128)S(1)} custom-call(bf16[1536,2048]{1,0:T(8,128)(2,1)S(1)} %get-tuple-element.16.high_ref, bf16[1536,2048]{1,0:T(8,128)(2,1)S(1)} %get-tuple-element.17.low_ref, f32[2,128,512]{2,1,0:T(8,128)S(1)} %pad_maximum_fusion.refs_0_, f32[2,128,512]{2,1,0:T(8,128)S(1)} %collective-permute-done.6.refs_1_), custom_call_target="tpu_custom_call" | custom-call | flops 2415919104 | tf_op jit(solution)/shard_map/multiply_sources/pallas_call | solution.py:183
  35.9 2.2 %collective-permute-done.2 = f32[1,128,512]{2,1,0:T(8,128)S(1)} collective-permute-done((f32[1,128,512]{2,1,0:T(8,128)S(1)}, f32[1,128,512]{2,1,0:T(8,128)S(1)}, u32[]{:S(2)}, u32[]{:S(2)}) %collective-permute-start.2) | collective-permute-done | bytes 262176 | tf_op jit(solution)/shard_map/ppermute | solution.py:20
  38.1 0.1 collective-permute-start.11
  38.1 2.7 %collective-permute-start.7 = (f32[2,128,512]{2,1,0:T(8,128)S(1)}, f32[2,128,512]{2,1,0:T(8,128)S(1)}, u32[]{:S(2)}, u32[]{:S(2)}) collective-permute-start(f32[2,128,512]{2,1,0:T(8,128)S(1)} %pad_maximum_fusion.1.refs_0_), channel_id=1, source_target_pairs={{0,4},{1,3},{2,6},{3,1},{4,0},{5,7},{6,2},{7,5},{8,12},{9,11},{10,... | collective-permute-start | bytes 1572872 | tf_op jit(solution)/shard_map/ppermute | solution.py:20
  40.9 0.4 collective-permute-done.8.refs_0_
  41.3 0.4 collective-permute-start.10
  41.7 0.2 collective-permute-start.9
  41.9 0.0 collective-permute-done.11.refs_1_
  41.9 2.7 %multiply_sources.6.refs_3_ = f32[1536,512]{1,0:T(8,128)S(1)} custom-call(bf16[1536,2048]{1,0:T(8,128)(2,1)S(1)} %get-tuple-element.16.high_ref, bf16[1536,2048]{1,0:T(8,128)(2,1)S(1)} %get-tuple-element.17.low_ref, f32[2,128,512]{2,1,0:T(8,128)S(1)} %pad_maximum_fusion.1.refs_0_, ...), custom_call_target="tpu_custom_call", output_to_operand_aliasing={{}: (4, {})} | custom-call | flops 2415919104 | tf_op jit(solution)/shard_map/multiply_sources/pallas_call | solution.py:183
  44.6 0.0 collective-permute-done.10.refs_2_
  44.6 0.0 collective-permute-done.9.refs_1_
  44.6 2.6 %multiply_sources.7.refs_1_ = f32[1536,512]{1,0:T(8,128)S(1)} custom-call(bf16[1536,2048]{1,0:T(8,128)(2,1)S(1)} %get-tuple-element.16.high_ref, bf16[1536,2048]{1,0:T(8,128)(2,1)S(1)} %get-tuple-element.17.low_ref, f32[2,128,512]{2,1,0:T(8,128)S(1)} %collective-permute-done.8.refs_0_, ...), custom_call_target="tpu_custom_call", output_to_operand_aliasing={{}: (5, {})} | custom-call | flops 2415919104 | tf_op jit(solution)/shard_map/multiply_sources/pallas_call | solution.py:183
  47.3 0.8 %collective-permute-done.7.refs_0_ = f32[2,128,512]{2,1,0:T(8,128)S(1)} collective-permute-done((f32[2,128,512]{2,1,0:T(8,128)S(1)}, f32[2,128,512]{2,1,0:T(8,128)S(1)}, u32[]{:S(2)}, u32[]{:S(2)}) %collective-permute-start.7) | collective-permute-done | bytes 524320 | tf_op jit(solution)/shard_map/ppermute | solution.py:20
  48.0 0.0 collective-permute-start.12
  48.0 1.8 %multiply_sources.8.refs_1_ = f32[1536,512]{1,0:T(8,128)S(1)} custom-call(bf16[1536,2048]{1,0:T(8,128)(2,1)S(1)} %get-tuple-element.16.high_ref, bf16[1536,2048]{1,0:T(8,128)(2,1)S(1)} %get-tuple-element.17.low_ref, f32[2,128,512]{2,1,0:T(8,128)S(1)} %collective-permute-done.7.refs_0_, ...), custom_call_target="tpu_custom_call", output_to_operand_aliasing={{}: (3, {})} | custom-call | flops 1207959552 | tf_op jit(solution)/shard_map/multiply_sources/pallas_call | solution.py:183
  49.8 0.1 collective-permute-done.12.refs_0_
  49.9 2.8 %multiply_sources.9 = f32[1,1536,512]{2,1,0:T(8,128)} custom-call(bf16[1536,2048]{1,0:T(8,128)(2,1)S(1)} %get-tuple-element.16.high_ref, bf16[1536,2048]{1,0:T(8,128)(2,1)S(1)} %get-tuple-element.17.low_ref, f32[2,128,512]{2,1,0:T(8,128)S(1)} %collective-permute-done.12.refs_0_, f32[1536,512]{1,0:T(8,128)S(1)} %multiply_sources.8.refs_1_), custom_call_target="tpu_custom_call" | custom-call | flops 1207959552 | tf_op jit(solution)/shard_map/multiply_sources/pallas_call | solution.py:183
  (7 shorter events, 0.3 us)
Async XLA Ops:
  1.1 11.3 %collective-permute-start.3 = (f32[128,512]{1,0:T(8,128)S(1)}, f32[128,512]{1,0:T(8,128)S(1)}, u32[]{:S(2)}, u32[]{:S(2)}) collective-permute-start(f32[128,512]{1,0:T(8,128)S(1)} %get-tuple-element.27), channel_id=1, source_target_pairs={{0,8},{1,17},{2,10},{3,19},{4,12},{5,21},{6,14},{7,23},{8,0},{9,25... | collective-permute-start | bytes 786440 | tf_op jit(solution)/shard_map/ppermute | solution.py:20
  4.2 14.8 %collective-permute-start = (f32[128,512]{1,0:T(8,128)S(1)}, f32[128,512]{1,0:T(8,128)S(1)}, u32[]{:S(2)}, u32[]{:S(2)}) collective-permute-start(f32[128,512]{1,0:T(8,128)S(1)} %get-tuple-element.28), channel_id=1, source_target_pairs={{0,8},{1,17},{2,10},{3,19},{4,12},{5,21},{6,14},{7,23},{8,0},{9,25... | collective-permute-start | bytes 786440 | tf_op jit(solution)/shard_map/ppermute | solution.py:20
  12.4 9.8 %collective-permute-start.4 = (f32[128,512]{1,0:T(8,128)S(1)}, f32[128,512]{1,0:T(8,128)S(1)}, u32[]{:S(2)}, u32[]{:S(2)}) collective-permute-start(f32[128,512]{1,0:T(8,128)S(1)} %multiply_add_fusion), channel_id=1, source_target_pairs={{0,16},{1,9},{2,18},{3,11},{4,20},{5,13},{6,22},{7,15},{8,24},{9,1... | collective-permute-start | bytes 786440 | tf_op jit(solution)/shard_map/ppermute | solution.py:20
  19.0 10.5 %collective-permute-start.1 = (f32[128,512]{1,0:T(8,128)S(1)}, f32[128,512]{1,0:T(8,128)S(1)}, u32[]{:S(2)}, u32[]{:S(2)}) collective-permute-start(f32[128,512]{1,0:T(8,128)S(1)} %multiply_add_fusion.1), channel_id=1, source_target_pairs={{0,16},{1,9},{2,18},{3,11},{4,20},{5,13},{6,22},{7,15},{8,24},{9,1... | collective-permute-start | bytes 786440 | tf_op jit(solution)/shard_map/ppermute | solution.py:20
  22.3 7.3 %collective-permute-start.5 = (f32[1,128,512]{2,1,0:T(8,128)S(1)}, f32[1,128,512]{2,1,0:T(8,128)S(1)}, u32[]{:S(2)}, u32[]{:S(2)}) collective-permute-start(f32[1,128,512]{2,1,0:T(8,128)S(1)} %bitcast.18), channel_id=1, source_target_pairs={{0,2},{1,5},{2,0},{3,7},{4,6},{5,1},{6,4},{7,3},{8,10},{9,13},{10,... | collective-permute-start | bytes 786440 | tf_op jit(solution)/shard_map/ppermute | solution.py:20
  29.7 3.6 %collective-permute-start.6 = (f32[2,128,512]{2,1,0:T(8,128)S(1)}, f32[2,128,512]{2,1,0:T(8,128)S(1)}, u32[]{:S(2)}, u32[]{:S(2)}) collective-permute-start(f32[2,128,512]{2,1,0:T(8,128)S(1)} %pad_maximum_fusion.refs_0_), channel_id=1, source_target_pairs={{0,1},{1,0},{2,3},{3,2},{4,5},{5,4},{6,7},{7,6},{8,9},{9,8},{10,11... | collective-permute-start | bytes 1572872 | tf_op jit(solution)/shard_map/ppermute | solution.py:20
  29.7 8.3 %collective-permute-start.2 = (f32[1,128,512]{2,1,0:T(8,128)S(1)}, f32[1,128,512]{2,1,0:T(8,128)S(1)}, u32[]{:S(2)}, u32[]{:S(2)}) collective-permute-start(f32[1,128,512]{2,1,0:T(8,128)S(1)} %bitcast.16), channel_id=1, source_target_pairs={{0,2},{1,5},{2,0},{3,7},{4,6},{5,1},{6,4},{7,3},{8,10},{9,13},{10,... | collective-permute-start | bytes 786440 | tf_op jit(solution)/shard_map/ppermute | solution.py:20
  31.7 9.6 %collective-permute-start.8 = (f32[2,128,512]{2,1,0:T(8,128)S(1)}, f32[2,128,512]{2,1,0:T(8,128)S(1)}, u32[]{:S(2)}, u32[]{:S(2)}) collective-permute-start(f32[2,128,512]{2,1,0:T(8,128)S(1)} %pad_maximum_fusion.refs_0_), channel_id=1, source_target_pairs={{0,4},{1,3},{2,6},{3,1},{4,0},{5,7},{6,2},{7,5},{8,12},{9,11},{10,... | collective-permute-start | bytes 1572872 | tf_op jit(solution)/shard_map/ppermute | solution.py:20
  38.1 3.8 %collective-permute-start.11 = (f32[2,128,512]{2,1,0:T(8,128)S(1)}, f32[2,128,512]{2,1,0:T(8,128)S(1)}, u32[]{:S(2)}, u32[]{:S(2)}) collective-permute-start(f32[2,128,512]{2,1,0:T(8,128)S(1)} %pad_maximum_fusion.1.refs_0_), channel_id=1, source_target_pairs={{0,1},{1,0},{2,3},{3,2},{4,5},{5,4},{6,7},{7,6},{8,9},{9,8},{10,11... | collective-permute-start | bytes 1572872 | tf_op jit(solution)/shard_map/ppermute | solution.py:20
  38.1 9.9 %collective-permute-start.7 = (f32[2,128,512]{2,1,0:T(8,128)S(1)}, f32[2,128,512]{2,1,0:T(8,128)S(1)}, u32[]{:S(2)}, u32[]{:S(2)}) collective-permute-start(f32[2,128,512]{2,1,0:T(8,128)S(1)} %pad_maximum_fusion.1.refs_0_), channel_id=1, source_target_pairs={{0,4},{1,3},{2,6},{3,1},{4,0},{5,7},{6,2},{7,5},{8,12},{9,11},{10,... | collective-permute-start | bytes 1572872 | tf_op jit(solution)/shard_map/ppermute | solution.py:20
  41.3 3.3 %collective-permute-start.10 = (f32[1,128,512]{2,1,0:T(8,128)S(1)}, f32[1,128,512]{2,1,0:T(8,128)S(1)}, u32[]{:S(2)}, u32[]{:S(2)}) collective-permute-start(f32[1,128,512]{2,1,0:T(8,128)S(1)} %get-tuple-element.25), channel_id=1, source_target_pairs={{0,1},{1,0},{2,3},{3,2},{4,5},{5,4},{6,7},{7,6},{8,9},{9,8},{10,11... | collective-permute-start | bytes 786440 | tf_op jit(solution)/shard_map/ppermute | solution.py:20
  41.7 2.9 %collective-permute-start.9 = (f32[1,128,512]{2,1,0:T(8,128)S(1)}, f32[1,128,512]{2,1,0:T(8,128)S(1)}, u32[]{:S(2)}, u32[]{:S(2)}) collective-permute-start(f32[1,128,512]{2,1,0:T(8,128)S(1)} %get-tuple-element.26), channel_id=1, source_target_pairs={{0,1},{1,0},{2,3},{3,2},{4,5},{5,4},{6,7},{7,6},{8,9},{9,8},{10,11... | collective-permute-start | bytes 786440 | tf_op jit(solution)/shard_map/ppermute | solution.py:20
  48.0 1.9 %collective-permute-start.12 = (f32[2,128,512]{2,1,0:T(8,128)S(1)}, f32[2,128,512]{2,1,0:T(8,128)S(1)}, u32[]{:S(2)}, u32[]{:S(2)}) collective-permute-start(f32[2,128,512]{2,1,0:T(8,128)S(1)} %collective-permute-done.7.refs_0_), channel_id=1, source_target_pairs={{0,1},{1,0},{2,3},{3,2},{4,5},{5,4},{6,7},{7,6},{8,9},{9,8},{10,11... | collective-permute-start | bytes 1572872 | tf_op jit(solution)/shard_map/ppermute | solution.py:20

commit v8 on v7

--- a/solution.py
+++ b/solution.py
@@ -97,7 +97,7 @@
 
 def split(table, k, chunks):
     rows, sources = k.shape
-    tile = rows // 6
+    tile = rows // 8
     block = pl.BlockSpec((tile, sources), lambda m, table: (m, 0))
     return pl.pallas_call(
         functools.partial(split_kernel, lax.axis_size("row"), chunks),

time: 52.9 us -> 52.8 us (level)
  waiting for transfers between devices: 15 us -> 13.4 us
  Pallas kernels: 20.5 us -> 21.1 us
  starting transfers between devices: 15.6 us -> 16.2 us
    ppermute x13, waiting for transfers between devices: 15 us -> 13.4 us  [exchange(): return lax.ppermute(value, AXES, pairs)]
    pallas_call x1, Pallas kernels: 8.05 us -> 8.63 us  [split(): pl.pallas_call(functools.partial(split_kernel, lax.axis_size('row'), chun...]
    ppermute x13, starting transfers between devices: 15.6 us -> 16.2 us  [exchange(): return lax.ppermute(value, AXES, pairs)]
  transfers between devices with their start and end apart: 13 -> 13, of which waited for: 7 -> 8; matrix products, arithmetic and copies ran while one was open for 1% -> 1% of each run, Pallas kernels for 34% -> 35%
where the time goes in v8:
time: 52.8 us; the launch traced here: 52.2 us
  Pallas kernels  21.1 us (40%)
  starting transfers between devices  16.2 us (31%)
  waiting for transfers between devices  13.4 us (25%)
  local copies, waits for them, and re-layouts  1.18 us (2%)
    ppermute x13, starting transfers between devices, exchange(): return lax.ppermute(value, AXES, pairs)  16.2 us
    ppermute x13, waiting for transfers between devices, exchange(): return lax.ppermute(value, AXES, pairs)  13.4 us
    pallas_call x5, Pallas kernels, multiply(): pl.pallas_call(functools.partial(multiply_kernel, start, len(pieces), acc...  12.5 us
    pallas_call x1, Pallas kernels, split(): pl.pallas_call(functools.partial(split_kernel, lax.axis_size('row'), chun...  8.63 us
    slice x1, local copies, waits for them, and re-layouts, body(): mine[at * half:(at + 1) * half]  1.06 us
  transfers between devices with their start and end apart: 13, of which 8 were waited for; matrix products, arithmetic and copies ran while one was open for 1% of the time, Pallas kernels for 35%

profile of v8, /device:TPU:0, one launch (start us, length us, event | category | flops | bytes accessed | tf_op | source)
XLA Modules:
  0.0 52.2 jit_solution(4322013860859484060)
XLA Ops:
  0.0 1.1 %slice_bitcast_fusion = (f32[128,512]{1,0:T(8,128)S(1)}, f32[128,512]{1,0:T(8,128)S(1)}) fusion(f32[1,256,512]{2,1,0:T(8,128)} %param.2), kind=kLoop, calls=%fused_computation.4 | loop fusion | bytes 1048576 | tf_op jit(solution)/shard_map/slice | solution.py:209
  1.1 3.1 %collective-permute-start.3 = (f32[128,512]{1,0:T(8,128)S(1)}, f32[128,512]{1,0:T(8,128)S(1)}, u32[]{:S(2)}, u32[]{:S(2)}) collective-permute-start(f32[128,512]{1,0:T(8,128)S(1)} %get-tuple-element.27), channel_id=1, source_target_pairs={{0,8},{1,17},{2,10},{3,19},{4,12},{5,21},{6,14},{7,23},{8,0},{9,25... | collective-permute-start | bytes 786440 | tf_op jit(solution)/shard_map/ppermute | solution.py:20
  4.2 0.1 collective-permute-start
  4.2 0.1 stack.35.table_ref
  4.3 8.6 %split_reduced_kernel.1 = (bf16[1536,2048]{1,0:T(8,128)(2,1)S(1)}, bf16[1536,2048]{1,0:T(8,128)(2,1)S(1)}) custom-call(s32[8]{0:T(128)S(1)} %stack.35.table_ref, f32[1536,2048]{1,0:T(8,128)} %bitcast.15), custom_call_target="tpu_custom_call" | custom-call | flops 12582912 | bytes 12582912 | tf_op jit(solution)/shard_map/split_reduced_kernel/pallas_call | solution.py:102
  13.0 0.0 collective-permute-done.3
  13.0 3.0 %collective-permute-start.4 = (f32[128,512]{1,0:T(8,128)S(1)}, f32[128,512]{1,0:T(8,128)S(1)}, u32[]{:S(2)}, u32[]{:S(2)}) collective-permute-start(f32[128,512]{1,0:T(8,128)S(1)} %multiply_add_fusion), channel_id=1, source_target_pairs={{0,16},{1,9},{2,18},{3,11},{4,20},{5,13},{6,22},{7,15},{8,24},{9,1... | collective-permute-start | bytes 786440 | tf_op jit(solution)/shard_map/ppermute | solution.py:20
  16.0 0.7 %collective-permute-done = f32[128,512]{1,0:T(8,128)S(1)} collective-permute-done((f32[128,512]{1,0:T(8,128)S(1)}, f32[128,512]{1,0:T(8,128)S(1)}, u32[]{:S(2)}, u32[]{:S(2)}) %collective-permute-start) | collective-permute-done | bytes 262176 | tf_op jit(solution)/shard_map/ppermute | solution.py:20
  16.8 2.6 %collective-permute-start.1 = (f32[128,512]{1,0:T(8,128)S(1)}, f32[128,512]{1,0:T(8,128)S(1)}, u32[]{:S(2)}, u32[]{:S(2)}) collective-permute-start(f32[128,512]{1,0:T(8,128)S(1)} %multiply_add_fusion.1), channel_id=1, source_target_pairs={{0,16},{1,9},{2,18},{3,11},{4,20},{5,13},{6,22},{7,15},{8,24},{9,1... | collective-permute-start | bytes 786440 | tf_op jit(solution)/shard_map/ppermute | solution.py:20
  19.4 3.4 %collective-permute-done.4 = f32[128,512]{1,0:T(8,128)S(1)} collective-permute-done((f32[128,512]{1,0:T(8,128)S(1)}, f32[128,512]{1,0:T(8,128)S(1)}, u32[]{:S(2)}, u32[]{:S(2)}) %collective-permute-start.4) | collective-permute-done | bytes 262176 | tf_op jit(solution)/shard_map/ppermute | solution.py:20
  22.9 1.4 %collective-permute-start.5 = (f32[1,128,512]{2,1,0:T(8,128)S(1)}, f32[1,128,512]{2,1,0:T(8,128)S(1)}, u32[]{:S(2)}, u32[]{:S(2)}) collective-permute-start(f32[1,128,512]{2,1,0:T(8,128)S(1)} %bitcast.18), channel_id=1, source_target_pairs={{0,2},{1,5},{2,0},{3,7},{4,6},{5,1},{6,4},{7,3},{8,10},{9,13},{10,... | collective-permute-start | bytes 786440 | tf_op jit(solution)/shard_map/ppermute | solution.py:20
  24.3 3.3 %collective-permute-done.1 = f32[128,512]{1,0:T(8,128)S(1)} collective-permute-done((f32[128,512]{1,0:T(8,128)S(1)}, f32[128,512]{1,0:T(8,128)S(1)}, u32[]{:S(2)}, u32[]{:S(2)}) %collective-permute-start.1) | collective-permute-done | bytes 262176 | tf_op jit(solution)/shard_map/ppermute | solution.py:20
  27.6 1.7 %collective-permute-done.5 = f32[1,128,512]{2,1,0:T(8,128)S(1)} collective-permute-done((f32[1,128,512]{2,1,0:T(8,128)S(1)}, f32[1,128,512]{2,1,0:T(8,128)S(1)}, u32[]{:S(2)}, u32[]{:S(2)}) %collective-permute-start.5) | collective-permute-done | bytes 262176 | tf_op jit(solution)/shard_map/ppermute | solution.py:20
  29.3 0.1 collective-permute-start.6
  29.4 1.4 %collective-permute-start.2 = (f32[1,128,512]{2,1,0:T(8,128)S(1)}, f32[1,128,512]{2,1,0:T(8,128)S(1)}, u32[]{:S(2)}, u32[]{:S(2)}) collective-permute-start(f32[1,128,512]{2,1,0:T(8,128)S(1)} %bitcast.16), channel_id=1, source_target_pairs={{0,2},{1,5},{2,0},{3,7},{4,6},{5,1},{6,4},{7,3},{8,10},{9,13},{10,... | collective-permute-start | bytes 786440 | tf_op jit(solution)/shard_map/ppermute | solution.py:20
  30.9 1.5 %collective-permute-start.8 = (f32[2,128,512]{2,1,0:T(8,128)S(1)}, f32[2,128,512]{2,1,0:T(8,128)S(1)}, u32[]{:S(2)}, u32[]{:S(2)}) collective-permute-start(f32[2,128,512]{2,1,0:T(8,128)S(1)} %pad_maximum_fusion.refs_0_), channel_id=1, source_target_pairs={{0,4},{1,3},{2,6},{3,1},{4,0},{5,7},{6,2},{7,5},{8,12},{9,11},{10,... | collective-permute-start | bytes 1572872 | tf_op jit(solution)/shard_map/ppermute | solution.py:20
  32.4 0.0 collective-permute-done.6.refs_1_
  32.4 2.6 %multiply_sources.5.refs_2_ = f32[1536,512]{1,0:T(8,128)S(1)} custom-call(bf16[1536,2048]{1,0:T(8,128)(2,1)S(1)} %get-tuple-element.16.high_ref, bf16[1536,2048]{1,0:T(8,128)(2,1)S(1)} %get-tuple-element.17.low_ref, f32[2,128,512]{2,1,0:T(8,128)S(1)} %pad_maximum_fusion.refs_0_, f32[2,128,512]{2,1,0:T(8,128)S(1)} %collective-permute-done.6.refs_1_), custom_call_target="tpu_custom_call" | custom-call | flops 2415919104 | tf_op jit(solution)/shard_map/multiply_sources/pallas_call | solution.py:183
  35.0 3.0 %collective-permute-done.2 = f32[1,128,512]{2,1,0:T(8,128)S(1)} collective-permute-done((f32[1,128,512]{2,1,0:T(8,128)S(1)}, f32[1,128,512]{2,1,0:T(8,128)S(1)}, u32[]{:S(2)}, u32[]{:S(2)}) %collective-permute-start.2) | collective-permute-done | bytes 262176 | tf_op jit(solution)/shard_map/ppermute | solution.py:20
  38.0 0.1 collective-permute-start.11
  38.1 2.2 %collective-permute-start.7 = (f32[2,128,512]{2,1,0:T(8,128)S(1)}, f32[2,128,512]{2,1,0:T(8,128)S(1)}, u32[]{:S(2)}, u32[]{:S(2)}) collective-permute-start(f32[2,128,512]{2,1,0:T(8,128)S(1)} %pad_maximum_fusion.1.refs_0_), channel_id=1, source_target_pairs={{0,4},{1,3},{2,6},{3,1},{4,0},{5,7},{6,2},{7,5},{8,12},{9,11},{10,... | collective-permute-start | bytes 1572872 | tf_op jit(solution)/shard_map/ppermute | solution.py:20
  40.4 0.6 %collective-permute-done.8.refs_0_ = f32[2,128,512]{2,1,0:T(8,128)S(1)} collective-permute-done((f32[2,128,512]{2,1,0:T(8,128)S(1)}, f32[2,128,512]{2,1,0:T(8,128)S(1)}, u32[]{:S(2)}, u32[]{:S(2)}) %collective-permute-start.8) | collective-permute-done | bytes 524320 | tf_op jit(solution)/shard_map/ppermute | solution.py:20
  41.0 0.4 collective-permute-start.10
  41.4 0.2 collective-permute-start.9
  41.5 0.0 collective-permute-done.11.refs_1_
  41.6 2.7 %multiply_sources.6.refs_3_ = f32[1536,512]{1,0:T(8,128)S(1)} custom-call(bf16[1536,2048]{1,0:T(8,128)(2,1)S(1)} %get-tuple-element.16.high_ref, bf16[1536,2048]{1,0:T(8,128)(2,1)S(1)} %get-tuple-element.17.low_ref, f32[2,128,512]{2,1,0:T(8,128)S(1)} %pad_maximum_fusion.1.refs_0_, ...), custom_call_target="tpu_custom_call", output_to_operand_aliasing={{}: (4, {})} | custom-call | flops 2415919104 | tf_op jit(solution)/shard_map/multiply_sources/pallas_call | solution.py:183
  44.2 0.0 collective-permute-done.10.refs_2_
  44.2 0.0 collective-permute-done.9.refs_1_
  44.2 2.6 %multiply_sources.7.refs_1_ = f32[1536,512]{1,0:T(8,128)S(1)} custom-call(bf16[1536,2048]{1,0:T(8,128)(2,1)S(1)} %get-tuple-element.16.high_ref, bf16[1536,2048]{1,0:T(8,128)(2,1)S(1)} %get-tuple-element.17.low_ref, f32[2,128,512]{2,1,0:T(8,128)S(1)} %collective-permute-done.8.refs_0_, ...), custom_call_target="tpu_custom_call", output_to_operand_aliasing={{}: (5, {})} | custom-call | flops 2415919104 | tf_op jit(solution)/shard_map/multiply_sources/pallas_call | solution.py:183
  46.9 0.6 %collective-permute-done.7.refs_0_ = f32[2,128,512]{2,1,0:T(8,128)S(1)} collective-permute-done((f32[2,128,512]{2,1,0:T(8,128)S(1)}, f32[2,128,512]{2,1,0:T(8,128)S(1)}, u32[]{:S(2)}, u32[]{:S(2)}) %collective-permute-start.7) | collective-permute-done | bytes 524320 | tf_op jit(solution)/shard_map/ppermute | solution.py:20
  47.5 0.0 collective-permute-start.12
  47.5 1.8 %multiply_sources.8.refs_1_ = f32[1536,512]{1,0:T(8,128)S(1)} custom-call(bf16[1536,2048]{1,0:T(8,128)(2,1)S(1)} %get-tuple-element.16.high_ref, bf16[1536,2048]{1,0:T(8,128)(2,1)S(1)} %get-tuple-element.17.low_ref, f32[2,128,512]{2,1,0:T(8,128)S(1)} %collective-permute-done.7.refs_0_, ...), custom_call_target="tpu_custom_call", output_to_operand_aliasing={{}: (3, {})} | custom-call | flops 1207959552 | tf_op jit(solution)/shard_map/multiply_sources/pallas_call | solution.py:183
  49.3 0.1 collective-permute-done.12.refs_0_
  49.4 2.8 %multiply_sources.9 = f32[1,1536,512]{2,1,0:T(8,128)} custom-call(bf16[1536,2048]{1,0:T(8,128)(2,1)S(1)} %get-tuple-element.16.high_ref, bf16[1536,2048]{1,0:T(8,128)(2,1)S(1)} %get-tuple-element.17.low_ref, f32[2,128,512]{2,1,0:T(8,128)S(1)} %collective-permute-done.12.refs_0_, f32[1536,512]{1,0:T(8,128)S(1)} %multiply_sources.8.refs_1_), custom_call_target="tpu_custom_call" | custom-call | flops 1207959552 | tf_op jit(solution)/shard_map/multiply_sources/pallas_call | solution.py:183
  (7 shorter events, 0.3 us)
Async XLA Ops:
  1.1 11.9 %collective-permute-start.3 = (f32[128,512]{1,0:T(8,128)S(1)}, f32[128,512]{1,0:T(8,128)S(1)}, u32[]{:S(2)}, u32[]{:S(2)}) collective-permute-start(f32[128,512]{1,0:T(8,128)S(1)} %get-tuple-element.27), channel_id=1, source_target_pairs={{0,8},{1,17},{2,10},{3,19},{4,12},{5,21},{6,14},{7,23},{8,0},{9,25... | collective-permute-start | bytes 786440 | tf_op jit(solution)/shard_map/ppermute | solution.py:20
  4.2 12.6 %collective-permute-start = (f32[128,512]{1,0:T(8,128)S(1)}, f32[128,512]{1,0:T(8,128)S(1)}, u32[]{:S(2)}, u32[]{:S(2)}) collective-permute-start(f32[128,512]{1,0:T(8,128)S(1)} %get-tuple-element.28), channel_id=1, source_target_pairs={{0,8},{1,17},{2,10},{3,19},{4,12},{5,21},{6,14},{7,23},{8,0},{9,25... | collective-permute-start | bytes 786440 | tf_op jit(solution)/shard_map/ppermute | solution.py:20
  13.0 9.8 %collective-permute-start.4 = (f32[128,512]{1,0:T(8,128)S(1)}, f32[128,512]{1,0:T(8,128)S(1)}, u32[]{:S(2)}, u32[]{:S(2)}) collective-permute-start(f32[128,512]{1,0:T(8,128)S(1)} %multiply_add_fusion), channel_id=1, source_target_pairs={{0,16},{1,9},{2,18},{3,11},{4,20},{5,13},{6,22},{7,15},{8,24},{9,1... | collective-permute-start | bytes 786440 | tf_op jit(solution)/shard_map/ppermute | solution.py:20
  16.8 10.8 %collective-permute-start.1 = (f32[128,512]{1,0:T(8,128)S(1)}, f32[128,512]{1,0:T(8,128)S(1)}, u32[]{:S(2)}, u32[]{:S(2)}) collective-permute-start(f32[128,512]{1,0:T(8,128)S(1)} %multiply_add_fusion.1), channel_id=1, source_target_pairs={{0,16},{1,9},{2,18},{3,11},{4,20},{5,13},{6,22},{7,15},{8,24},{9,1... | collective-permute-start | bytes 786440 | tf_op jit(solution)/shard_map/ppermute | solution.py:20
  22.9 6.4 %collective-permute-start.5 = (f32[1,128,512]{2,1,0:T(8,128)S(1)}, f32[1,128,512]{2,1,0:T(8,128)S(1)}, u32[]{:S(2)}, u32[]{:S(2)}) collective-permute-start(f32[1,128,512]{2,1,0:T(8,128)S(1)} %bitcast.18), channel_id=1, source_target_pairs={{0,2},{1,5},{2,0},{3,7},{4,6},{5,1},{6,4},{7,3},{8,10},{9,13},{10,... | collective-permute-start | bytes 786440 | tf_op jit(solution)/shard_map/ppermute | solution.py:20
  29.3 3.0 %collective-permute-start.6 = (f32[2,128,512]{2,1,0:T(8,128)S(1)}, f32[2,128,512]{2,1,0:T(8,128)S(1)}, u32[]{:S(2)}, u32[]{:S(2)}) collective-permute-start(f32[2,128,512]{2,1,0:T(8,128)S(1)} %pad_maximum_fusion.refs_0_), channel_id=1, source_target_pairs={{0,1},{1,0},{2,3},{3,2},{4,5},{5,4},{6,7},{7,6},{8,9},{9,8},{10,11... | collective-permute-start | bytes 1572872 | tf_op jit(solution)/shard_map/ppermute | solution.py:20
  29.4 8.6 %collective-permute-start.2 = (f32[1,128,512]{2,1,0:T(8,128)S(1)}, f32[1,128,512]{2,1,0:T(8,128)S(1)}, u32[]{:S(2)}, u32[]{:S(2)}) collective-permute-start(f32[1,128,512]{2,1,0:T(8,128)S(1)} %bitcast.16), channel_id=1, source_target_pairs={{0,2},{1,5},{2,0},{3,7},{4,6},{5,1},{6,4},{7,3},{8,10},{9,13},{10,... | collective-permute-start | bytes 786440 | tf_op jit(solution)/shard_map/ppermute | solution.py:20
  30.9 10.1 %collective-permute-start.8 = (f32[2,128,512]{2,1,0:T(8,128)S(1)}, f32[2,128,512]{2,1,0:T(8,128)S(1)}, u32[]{:S(2)}, u32[]{:S(2)}) collective-permute-start(f32[2,128,512]{2,1,0:T(8,128)S(1)} %pad_maximum_fusion.refs_0_), channel_id=1, source_target_pairs={{0,4},{1,3},{2,6},{3,1},{4,0},{5,7},{6,2},{7,5},{8,12},{9,11},{10,... | collective-permute-start | bytes 1572872 | tf_op jit(solution)/shard_map/ppermute | solution.py:20
  38.0 3.5 %collective-permute-start.11 = (f32[2,128,512]{2,1,0:T(8,128)S(1)}, f32[2,128,512]{2,1,0:T(8,128)S(1)}, u32[]{:S(2)}, u32[]{:S(2)}) collective-permute-start(f32[2,128,512]{2,1,0:T(8,128)S(1)} %pad_maximum_fusion.1.refs_0_), channel_id=1, source_target_pairs={{0,1},{1,0},{2,3},{3,2},{4,5},{5,4},{6,7},{7,6},{8,9},{9,8},{10,11... | collective-permute-start | bytes 1572872 | tf_op jit(solution)/shard_map/ppermute | solution.py:20
  38.1 9.4 %collective-permute-start.7 = (f32[2,128,512]{2,1,0:T(8,128)S(1)}, f32[2,128,512]{2,1,0:T(8,128)S(1)}, u32[]{:S(2)}, u32[]{:S(2)}) collective-permute-start(f32[2,128,512]{2,1,0:T(8,128)S(1)} %pad_maximum_fusion.1.refs_0_), channel_id=1, source_target_pairs={{0,4},{1,3},{2,6},{3,1},{4,0},{5,7},{6,2},{7,5},{8,12},{9,11},{10,... | collective-permute-start | bytes 1572872 | tf_op jit(solution)/shard_map/ppermute | solution.py:20
  41.0 3.3 %collective-permute-start.10 = (f32[1,128,512]{2,1,0:T(8,128)S(1)}, f32[1,128,512]{2,1,0:T(8,128)S(1)}, u32[]{:S(2)}, u32[]{:S(2)}) collective-permute-start(f32[1,128,512]{2,1,0:T(8,128)S(1)} %get-tuple-element.25), channel_id=1, source_target_pairs={{0,1},{1,0},{2,3},{3,2},{4,5},{5,4},{6,7},{7,6},{8,9},{9,8},{10,11... | collective-permute-start | bytes 786440 | tf_op jit(solution)/shard_map/ppermute | solution.py:20
  41.4 2.8 %collective-permute-start.9 = (f32[1,128,512]{2,1,0:T(8,128)S(1)}, f32[1,128,512]{2,1,0:T(8,128)S(1)}, u32[]{:S(2)}, u32[]{:S(2)}) collective-permute-start(f32[1,128,512]{2,1,0:T(8,128)S(1)} %get-tuple-element.26), channel_id=1, source_target_pairs={{0,1},{1,0},{2,3},{3,2},{4,5},{5,4},{6,7},{7,6},{8,9},{9,8},{10,11... | collective-permute-start | bytes 786440 | tf_op jit(solution)/shard_map/ppermute | solution.py:20
  47.5 1.9 %collective-permute-start.12 = (f32[2,128,512]{2,1,0:T(8,128)S(1)}, f32[2,128,512]{2,1,0:T(8,128)S(1)}, u32[]{:S(2)}, u32[]{:S(2)}) collective-permute-start(f32[2,128,512]{2,1,0:T(8,128)S(1)} %collective-permute-done.7.refs_0_), channel_id=1, source_target_pairs={{0,1},{1,0},{2,3},{3,2},{4,5},{5,4},{6,7},{7,6},{8,9},{9,8},{10,11... | collective-permute-start | bytes 1572872 | tf_op jit(solution)/shard_map/ppermute | solution.py:20
